TPU v7x, 32 devices: a whole 2x2x4 slice. The times are simulated.
32 devices in a mesh: grp: 2 (over y), seq: 4 (over z), img: 4 (over x, core).
Axes of the slice: x: 2, y: 2, z: 4, core: 2. Of those that a mesh axis runs over, the one named last changes fastest.
Arguments:
- queries: bfloat16 [16, 1024, 4096], P(('grp', 'img'), 'seq'), parts along dimension 0, may hold values from -43 to 43
- keys: bfloat16 [16, 1024, 4096], P(('grp', 'img'), 'seq'), parts along dimension 0, may hold values from -4 to 4
- values: bfloat16 [16, 1024, 4096], P(('grp', 'img'), 'seq'), parts along dimension 0, may hold values from -6 to 6
- residual: bfloat16 [16, 1024, 6144], P(('grp', 'img'), 'seq'), parts along dimension 0, may hold values from -6 to 6
- out_weight: bfloat16 [4096, 6144], P('img', 'seq'), may hold values from -0.09375 to 0.09375
Outputs:
- mixed: bfloat16 [16, 1024, 6144], P(('grp', 'img'), 'seq'), parts along dimension 0
There are 2 independent parts, one for each index of `grp`. A program takes and returns all parts, laid end to end along the dimension named above; an argument that names none is the same for every part. Nothing has to cross between parts.
All inputs are finite; a program needn't handle non-finite values.
Results may differ from a plain program's by a relative error of at most 0.0034.
Values may be sent and summed in bfloat16 or wider, within the bound.
No kernel may reach another device: no remote copies, remote signals or barrier semaphores. Data moves between devices by JAX's collectives and lax.ppermute only.
A program may use at most 256 MiB of HBM per device.

v0:
```python
import jax
import jax.numpy as jnp
from jax import lax
from jax.sharding import PartitionSpec as P

HEAD_DIM = 128


def attend(triple):
    query_rows, key_rows, value_rows = triple
    images_here, patches_all, row_width = query_rows.shape
    heads_here = row_width // HEAD_DIM
    query_heads = query_rows.reshape(images_here, patches_all, heads_here, HEAD_DIM)
    key_heads = key_rows.reshape(images_here, patches_all, heads_here, HEAD_DIM)
    value_heads = value_rows.reshape(images_here, patches_all, heads_here, HEAD_DIM)
    scores = jnp.einsum(
        "nqhd,nkhd->nhqk", query_heads, key_heads, preferred_element_type=jnp.float32
    )
    scores = scores * (1.0 / HEAD_DIM**0.5)
    weights = jax.nn.softmax(scores, axis=-1).astype(jnp.bfloat16)
    attended = jnp.einsum(
        "nhqk,nkhd->nqhd", weights, value_heads, preferred_element_type=jnp.float32
    )
    attended = attended.astype(jnp.bfloat16).reshape(images_here, patches_all, row_width)
    return lax.all_to_all(attended, "seq", split_axis=1, concat_axis=2, tiled=True)


def local(queries, keys, values, residual, out_weight):
    attended = attend(
        (
            lax.all_to_all(queries, "seq", split_axis=2, concat_axis=1, tiled=True),
            lax.all_to_all(keys, "seq", split_axis=2, concat_axis=1, tiled=True),
            lax.all_to_all(values, "seq", split_axis=2, concat_axis=1, tiled=True),
        )
    )
    head_block = lax.all_to_all(attended, "img", split_axis=2, concat_axis=0, tiled=True)
    partial_value = jnp.einsum(
        "ipc,cd->ipd",
        head_block,
        lax.all_gather(out_weight, "seq", axis=1, tiled=True),
        preferred_element_type=jnp.float32,
    )
    summed = lax.psum_scatter(
        partial_value.astype(jnp.bfloat16), "img", scatter_dimension=0, tiled=True
    ).astype(jnp.float32)
    return (residual.astype(jnp.float32) + summed).astype(jnp.bfloat16)


def solution(mesh):
    in_specs = (
        P(("grp", "img"), "seq", None),
        P(("grp", "img"), "seq", None),
        P(("grp", "img"), "seq", None),
        P(("grp", "img"), "seq", None),
        P("img", "seq"),
    )
    out_specs = P(("grp", "img"), "seq", None)
    return jax.shard_map(local, mesh=mesh, in_specs=in_specs, out_specs=out_specs, check_vma=False)
```

profile of v0, /device:TPU:0, one launch (start us, length us, event | category | flops | bytes accessed | tf_op | source)
XLA Modules:
  0.0 912.4 jit_solution(8390820176620775947)
XLA Ops:
  6.5 11.1 %copy.24 = bf16[2,256,4096]{1,0,2:T(2,128)(2,1)} copy(bf16[2,256,4096]{2,1,0:T(8,128)(2,1)} %param.5) | data formatting | bytes 8388608 | tf_op args[0]
  17.6 6.3 all-to-all-start
  24.0 11.1 %copy.26 = bf16[2,256,4096]{1,0,2:T(2,128)(2,1)} copy(bf16[2,256,4096]{2,1,0:T(8,128)(2,1)} %param.6) | data formatting | bytes 8388608 | tf_op args[1]
  35.1 82.3 %all-to-all-done = bf16[2,256,4096]{1,0,2:T(2,128)(2,1)} async-done(((bf16[2,256,4096]{1,0,2:T(2,128)(2,1)}), bf16[2,256,4096]{1,0,2:T(2,128)(2,1)}, u32[]{:S(2)}, u32[]{:S(2)}) %all-to-all-start) | async-done | bytes 4194336 | tf_op jit(solution)/shard_map/all_to_all | solution.py:31
  122.3 11.1 %copy.30 = bf16[2,256,4096]{1,0,2:T(2,128)(2,1)} copy(bf16[2,256,4096]{2,1,0:T(8,128)(2,1)} %param.7) | data formatting | bytes 8388608 | tf_op args[2]
  133.4 81.5 %all-to-all-done.1 = bf16[2,256,4096]{1,0,2:T(2,128)(2,1)} async-done(((bf16[2,256,4096]{1,0,2:T(2,128)(2,1)}), bf16[2,256,4096]{1,0,2:T(2,128)(2,1)}, u32[]{:S(2)}, u32[]{:S(2)}) %all-to-all-start.1) | async-done | bytes 4194336 | tf_op jit(solution)/shard_map/all_to_all | solution.py:32
  220.5 11.2 %copy.25 = bf16[2,256,4,1024]{3,1,2,0:T(8,128)(2,1)} copy(bf16[2,256,4,1024]{1,0,3,2:T(2,128)(2,1)} %bitcast) | data formatting | bytes 8388608 | tf_op jit(solution)/shard_map/all_to_all | solution.py:31
  231.7 6.0 copy.40
  237.7 11.3 %copy.27 = bf16[2,256,4,1024]{3,1,2,0:T(8,128)(2,1)} copy(bf16[2,256,4,1024]{1,0,3,2:T(2,128)(2,1)} %bitcast.2) | data formatting | bytes 8388608 | tf_op jit(solution)/shard_map/all_to_all | solution.py:32
  249.0 5.3 copy.41
  254.2 170.8 %all-to-all-done.2 = bf16[2,256,4096]{1,0,2:T(2,128)(2,1)} async-done(((bf16[2,256,4096]{1,0,2:T(2,128)(2,1)}), bf16[2,256,4096]{1,0,2:T(2,128)(2,1)}, u32[]{:S(2)}, u32[]{:S(2)}) %all-to-all-start.2) | async-done | bytes 4194336 | tf_op jit(solution)/shard_map/all_to_all | solution.py:33
  425.0 7.4 copy.65
  432.5 7.7 reshape.19
  440.2 34.4 %fusion.22 = (f32[2,8,1024]{2,1,0:T(8,128)S(1)}, f32[2,8,1024,1024]{2,3,1,0:T(8,128)}) fusion(bf16[2,1024,8,128]{3,2,1,0:T(8,128)(2,1)} %bitcast.43, bf16[2,1024,8,128]{3,2,1,0:T(8,128)(2,1)} %bitcast.42), kind=kOutput, calls=%fused_computation.19 | convolution fusion | flops 4345299968 | bytes 75563008 | tf_op jit(solution)/shard_map/sub | solution.py:20
  474.6 25.2 %fusion.20 = bf16[2,8,1024,128]{2,3,1,0:T(8,128)(2,1)} fusion(bf16[2,1024,8,128]{1,3,2,0:T(8,128)(2,1)} %reshape.19, f32[2,8,1024,1024]{2,3,1,0:T(8,128)} %get-tuple-element.6, f32[2,8,1024]{2,1,0:T(8,128)S(1)} %get-tuple-element.5), kind=kOutput, calls=%fused_computation.17 | convolution fusion | flops 4330618880 | bytes 75563008 | tf_op jit(solution)/shard_map/nhqk,nkhd->nqhd/dot_general | solution.py:21
  499.8 11.3 %copy.33 = bf16[2,1024,1024]{2,0,1:T(2,128)(2,1)} copy(bf16[2,1024,1024]{1,2,0:T(8,128)(2,1)} %bitcast.45) | data formatting | bytes 8388608 | tf_op jit(solution)/shard_map/reshape | solution.py:24
  511.1 94.3 %all_to_all.81 = bf16[2,1024,1024]{2,0,1:T(2,128)(2,1)S(1)} all-to-all(bf16[2,1024,1024]{2,0,1:T(2,128)(2,1)} %copy.33), channel_id=1, replica_groups=mesh['grp'=2,'seq'=4,'img'=4] {'seq'}, dimensions={1} | all-to-all | bytes 8388608 | tf_op jit(solution)/shard_map/all_to_all | solution.py:25
  608.8 6.3 copy.35
  615.0 8.4 copy.36
  623.4 50.9 %all_to_all.82 = bf16[2,256,4096]{1,0,2:T(2,128)(2,1)S(1)} all-to-all(bf16[2,256,4096]{1,0,2:T(2,128)(2,1)S(1)} %copy.36), channel_id=1, replica_groups=mesh['grp'=2,'seq'=4,'img'=4] {'img'}, dimensions={2} | all-to-all | bytes 8388608 | tf_op jit(solution)/shard_map/all_to_all | solution.py:36
  676.9 6.3 copy.38
  683.2 33.6 %convolution_convert_fusion = bf16[8,256,6144]{2,1,0:T(8,128)(2,1)} fusion(bf16[8,256,1024]{2,1,0:T(8,128)(2,1)} %bitcast.44, bf16[1024,6144]{1,0:T(8,128)(2,1)} %all-gather.2.cloned.1.call-done), kind=kOutput, calls=%fused_computation.8 | convolution fusion | flops 25782386688 | bytes 41943040 | tf_op jit(solution)/shard_map/ipc,cd->ipd/dot_general | solution.py:37
  716.8 178.8 %reduce-scatter.2.cloned.1.call-done = bf16[2,256,6144]{2,1,0:T(8,128)(2,1)} async-done(((bf16[8,256,6144]{2,1,0:T(8,128)(2,1)}), bf16[2,256,6144]{2,1,0:T(8,128)(2,1)}) %reduce-scatter.2.cloned.1.call-update) | async-done | bytes 6291472 | tf_op jit(solution)/shard_map/reduce_scatter | solution.py:43
  895.6 10.0 %add_convert_fusion = bf16[2,256,6144]{2,1,0:T(8,128)(2,1)} fusion(bf16[2,256,6144]{2,1,0:T(8,128)(2,1)} %reduce-scatter.2.cloned.1.call-done, bf16[2,256,6144]{2,1,0:T(8,128)(2,1)} %param.8), kind=kLoop, calls=%fused_computation.10 | loop fusion | flops 12582912 | bytes 18874368 | tf_op jit(solution)/shard_map/convert_element_type | solution.py:46
  (9 shorter events, 16.3 us)
Async XLA Ops:
  17.6 99.7 %all-to-all-start = ((bf16[2,256,4096]{1,0,2:T(2,128)(2,1)}), bf16[2,256,4096]{1,0,2:T(2,128)(2,1)}, u32[]{:S(2)}, u32[]{:S(2)}) async-start(bf16[2,256,4096]{1,0,2:T(2,128)(2,1)} %copy.24), calls=%async_computation | async-start | bytes 8388608 | tf_op jit(solution)/shard_map/all_to_all | solution.py:31
  117.4 97.5 %all-to-all-start.1 = ((bf16[2,256,4096]{1,0,2:T(2,128)(2,1)}), bf16[2,256,4096]{1,0,2:T(2,128)(2,1)}, u32[]{:S(2)}, u32[]{:S(2)}) async-start(bf16[2,256,4096]{1,0,2:T(2,128)(2,1)} %copy.26), calls=%async_computation.1 | async-start | bytes 8388608 | tf_op jit(solution)/shard_map/all_to_all | solution.py:32
  214.9 210.2 %all-to-all-start.2 = ((bf16[2,256,4096]{1,0,2:T(2,128)(2,1)}), bf16[2,256,4096]{1,0,2:T(2,128)(2,1)}, u32[]{:S(2)}, u32[]{:S(2)}) async-start(bf16[2,256,4096]{1,0,2:T(2,128)(2,1)} %copy.30), calls=%async_computation.2 | async-start | bytes 8388608 | tf_op jit(solution)/shard_map/all_to_all | solution.py:33
  219.7 463.5 %all-gather.2.cloned.1.call-start = ((), (), s32[]{:S(2)}) async-start(), calls=%async_computation.6 | async-start | bytes 15728640 | tf_op jit(solution)/shard_map/all_gather | solution.py:40
  220.5 675.1 %reduce-scatter.2.cloned.1.call-start = ((), (), s32[]{:S(2)}) async-start(), calls=%async_computation.7 | async-start | bytes 31457280 | tf_op jit(solution)/shard_map/reduce_scatter | solution.py:43
Sparse Core Ops, SparseCore 0:
  222.1 292.9 all-gather.1
  717.0 178.6 reduce-scatter.1
where the time goes:
time: 915 us; the launch traced here: 912 us
  waiting for transfers between devices  514 us (56%)
  blocking collectives  145 us (16%)
  local copies, waits for them, and re-layouts  120 us (13%)
  matrix products  93.2 us (10%)
  starting transfers between devices  16.1 us (2%)
  between operations  13.4 us (1%)
  other arithmetic  9.96 us (1%)
    reduce_scatter x1, waiting for transfers between devices, local(): lax.psum_scatter(partial_value.astype(jnp.bfloat16), 'img', scatter_dimen...  179 us
    all_to_all x1, waiting for transfers between devices, local(): lax.all_to_all(values, 'seq', split_axis=2, concat_axis=1, tiled=True)  171 us
    all_to_all x1, blocking collectives, attend(): lax.all_to_all(attended, 'seq', split_axis=1, concat_axis=2, tiled=True)  94.3 us
    all_to_all x1, waiting for transfers between devices, local(): lax.all_to_all(queries, 'seq', split_axis=2, concat_axis=1, tiled=True)  82.3 us
    all_to_all x1, waiting for transfers between devices, local(): lax.all_to_all(keys, 'seq', split_axis=2, concat_axis=1, tiled=True)  81.5 us
    all_to_all x1, blocking collectives, local(): lax.all_to_all(attended, 'img', split_axis=2, concat_axis=0, tiled=True)  50.9 us
    unnamed x5, local copies, waits for them, and re-layouts  44.6 us
    sub x1, matrix products, attend(): weights = jax.nn.softmax(scores, axis=-1).astype(jnp.bfloat16)  34.4 us
  transfers between devices with their start and end apart: 5, of which 4 were waited for; matrix products, arithmetic and copies ran while one was open for 19% of the time, Pallas kernels for 0%

commit v1 on v0

v1 whole, which is shorter than its diff:
```python
import jax
import jax.numpy as jnp
from jax import lax
from jax.experimental import pallas as pl
from jax.experimental.pallas import tpu as pltpu
from jax.sharding import PartitionSpec as P

HEAD_DIM = 128
CHUNKS = 4
BF16 = jnp.bfloat16
F32 = jnp.float32


def attend(triple):
    query_rows, key_rows, value_rows = triple
    images_here, patches_all, row_width = query_rows.shape
    heads_here = row_width // HEAD_DIM
    query_heads = query_rows.reshape(images_here, patches_all, heads_here, HEAD_DIM)
    key_heads = key_rows.reshape(images_here, patches_all, heads_here, HEAD_DIM)
    value_heads = value_rows.reshape(images_here, patches_all, heads_here, HEAD_DIM)
    scores = jnp.einsum(
        "nqhd,nkhd->nhqk", query_heads, key_heads, preferred_element_type=F32
    )
    scores = scores * (1.0 / HEAD_DIM**0.5)
    weights = jax.nn.softmax(scores, axis=-1).astype(BF16)
    attended = jnp.einsum(
        "nhqk,nkhd->nqhd", weights, value_heads, preferred_element_type=F32
    )
    attended = attended.astype(BF16).reshape(images_here, patches_all, row_width)
    return lax.all_to_all(attended, "seq", split_axis=1, concat_axis=2, tiled=True)


def local_any(queries, keys, values, residual, out_weight):
    attended = attend(
        (
            lax.all_to_all(queries, "seq", split_axis=2, concat_axis=1, tiled=True),
            lax.all_to_all(keys, "seq", split_axis=2, concat_axis=1, tiled=True),
            lax.all_to_all(values, "seq", split_axis=2, concat_axis=1, tiled=True),
        )
    )
    head_block = lax.all_to_all(attended, "img", split_axis=2, concat_axis=0, tiled=True)
    partial_value = jnp.einsum(
        "ipc,cd->ipd",
        head_block,
        lax.all_gather(out_weight, "seq", axis=1, tiled=True),
        preferred_element_type=F32,
    )
    summed = lax.psum_scatter(
        partial_value.astype(BF16), "img", scatter_dimension=0, tiled=True
    ).astype(F32)
    return (residual.astype(F32) + summed).astype(BF16)


def pack(z, queries, keys, values, chunk, width, after):
    images, rows, columns = queries.shape
    n = 4
    span = columns // n

    def body(z_ref, q, k, v, *rest):
        outs, sems = rest[-n:-1], rest[-1]
        copies = []
        for s in range(1, n):
            start = lax.rem(z_ref[0] + s, n) * span + chunk * width
            cols = pl.ds(pl.multiple_of(start, HEAD_DIM), width)
            for t, src in enumerate((q, k, v)):
                copies.append(
                    pltpu.make_async_copy(
                        src.at[:, :, cols], outs[s - 1].at[t], sems.at[s - 1, t]
                    )
                )
        for copy in copies:
            copy.start()
        for copy in copies:
            copy.wait()

    anywhere = pl.BlockSpec(memory_space=pl.ANY)
    return pl.pallas_call(
        body,
        out_shape=[jax.ShapeDtypeStruct((3, images, rows, width), BF16)] * (n - 1),
        grid_spec=pltpu.PrefetchScalarGridSpec(
            num_scalar_prefetch=1,
            grid=(),
            in_specs=[anywhere] * (3 + len(after)),
            out_specs=[anywhere] * (n - 1),
            scratch_shapes=[pltpu.SemaphoreType.DMA((n - 1, 3))],
        ),
        cost_estimate=pl.CostEstimate(
            flops=0, bytes_accessed=18 * images * rows * width * 2, transcendentals=0
        ),
        name=f"pack{chunk}",
    )(z, queries, keys, values, *after)


def attention(z, queries, keys, values, received, chunk, width):
    images, rows, columns = queries.shape
    n = 4
    heads = width // HEAD_DIM
    at_first = chunk * heads
    per_device = columns // n // HEAD_DIM
    factor = 1.4426950408889634 / HEAD_DIM**0.5

    def body(z_ref, q0, k0, v0, r1, r2, r3, o0, o1, o2, o3, k_all, v_all):
        k_all[0:rows] = k0[0]
        v_all[0:rows, 0:HEAD_DIM] = v0[0]
        for s, r in enumerate((r1, r2, r3), 1):
            k_all[s * rows : (s + 1) * rows] = r[1, 0]
            v_all[s * rows : (s + 1) * rows, 0:HEAD_DIM] = r[2, 0]
        v_all[:, HEAD_DIM:] = jnp.ones((n * rows, HEAD_DIM), BF16)
        for q, out in (
            (q0[0], o0),
            (r1[0, 0], o1),
            (r2[0, 0], o2),
            (r3[0, 0], o3),
        ):
            scores = lax.dot_general(
                q, k_all[...], (((1,), (1,)), ((), ())), preferred_element_type=F32
            )
            most = jnp.max(scores, axis=-1, keepdims=True)
            weights = jnp.exp2((scores - most) * factor).astype(BF16)
            sums = jnp.dot(weights, v_all[...], preferred_element_type=F32)
            out[0] = (sums[:, :HEAD_DIM] / sums[:, HEAD_DIM:]).astype(BF16)

    own = pl.BlockSpec(
        (1, rows, HEAD_DIM), lambda i, h, z_ref: (i, 0, z_ref[0] * per_device + at_first + h)
    )
    other = pl.BlockSpec((3, 1, rows, HEAD_DIM), lambda i, h, z_ref: (0, i, 0, h))
    result = pl.BlockSpec((1, rows, HEAD_DIM), lambda i, h, z_ref: (i, 0, h))
    work = images * heads * (n * rows) ** 2
    return pl.pallas_call(
        body,
        out_shape=[jax.ShapeDtypeStruct((images, rows, width), BF16)] * n,
        grid_spec=pltpu.PrefetchScalarGridSpec(
            num_scalar_prefetch=1,
            grid=(images, heads),
            in_specs=[own] * 3 + [other] * 3,
            out_specs=[result] * n,
            scratch_shapes=[
                pltpu.VMEM((n * rows, HEAD_DIM), BF16),
                pltpu.VMEM((n * rows, 2 * HEAD_DIM), BF16),
            ],
        ),
        compiler_params=pltpu.CompilerParams(vmem_limit_bytes=32 * 2**20),
        cost_estimate=pl.CostEstimate(
            flops=4 * work * HEAD_DIM,
            bytes_accessed=4 * n * images * rows * width * 2,
            transcendentals=work,
        ),
        name=f"attention{chunk}",
    )(z, queries, keys, values, *received)


def project(z, attended, pieces, total, chunks, width, out_type):
    images, rows, model = total.shape
    n = 4
    tile = 512
    tiles = model // n // tile
    pieces = [p.reshape(n, CHUNKS, width, model // n) for p in pieces]
    many = len(chunks)

    def body(z_ref, *refs):
        o_refs = refs[: many * n]
        w_refs = refs[many * n : many * n + many * n]
        total_ref, out_ref = refs[-2:]
        at = pl.program_id(0)
        for m in range(n):

            @pl.when(at // tiles == m)
            def _():
                value = total_ref[...].astype(F32).reshape(images * rows, tile)
                for i in range(many):
                    for s in range(n):
                        heads_of = lax.rem(z_ref[0] + (n - s), n)
                        value += jnp.dot(
                            o_refs[i * n + s][...].reshape(images * rows, width),
                            w_refs[i * n + m][heads_of, 0],
                            preferred_element_type=F32,
                        )
                out_ref[...] = value.astype(out_type).reshape(images, rows, tile)

    def column(at, z_ref):
        return (0, 0, jnp.bitwise_xor(z_ref[0], at // tiles) * tiles + at % tiles)

    def weight_spec(chunk, m):
        return pl.BlockSpec(
            (n, 1, width, tile),
            lambda at, z_ref: (0, chunk, 0, jnp.clip(at - m * tiles, 0, tiles - 1)),
        )

    whole = pl.BlockSpec((images, rows, width), lambda at, z_ref: (0, 0, 0))
    block = pl.BlockSpec((images, rows, tile), column)
    return pl.pallas_call(
        body,
        out_shape=jax.ShapeDtypeStruct((images, rows, model), out_type),
        grid_spec=pltpu.PrefetchScalarGridSpec(
            num_scalar_prefetch=1,
            grid=(n * tiles,),
            in_specs=[whole] * (n * many)
            + [weight_spec(chunk, m) for chunk in chunks for m in range(n)]
            + [block],
            out_specs=block,
        ),
        compiler_params=pltpu.CompilerParams(vmem_limit_bytes=56 * 2**20),
        cost_estimate=pl.CostEstimate(
            flops=2 * many * n * images * rows * width * model,
            bytes_accessed=many * n * width * model * 2 + images * rows * model * 8,
            transcendentals=0,
        ),
        name="project" + "".join(str(c) for c in chunks),
    )(
        z,
        *[o for chunk in attended for o in chunk],
        *[p for _ in chunks for p in pieces],
        total,
    )


def local_line(queries, keys, values, residual, out_weight):
    n = 4
    images, rows, columns = queries.shape
    width = columns // n // CHUNKS
    index = lax.axis_index("seq")
    z = index.astype(jnp.int32).reshape(1)
    onward = [[(i, (i + s) % n) for i in range(n)] for s in range(n)]
    back = [[(i, (i - s) % n) for i in range(n)] for s in range(n)]

    half = out_weight.shape[0] // lax.axis_size("grp")
    mine = lax.dynamic_slice_in_dim(out_weight, lax.axis_index("grp") * half, half, 0)
    far = lax.ppermute(mine, "seq", [(i, i ^ 2) for i in range(n)])
    near = lax.ppermute(jnp.stack([mine, far]), "seq", [(i, i ^ 1) for i in range(n)])

    def whole(piece):
        return lax.all_gather(piece, ("img", "grp"), axis=0, tiled=True)

    pieces = [whole(mine), whole(near[0]), whole(far), whole(near[1])]

    received = {}
    for c in range(CHUNKS):
        after = [received[c - 1][0]] if c else []
        packs = pack(z, queries, keys, values, c, width, after)
        received[c] = [lax.ppermute(packs[s - 1], "seq", onward[s]) for s in (1, 2, 3)]

    attended = []
    for c in range(CHUNKS):
        outs = attention(z, queries, keys, values, received[c], c, width)
        attended.append(
            [outs[0]] + [lax.ppermute(outs[s], "seq", back[s]) for s in (1, 2, 3)]
        )
    attended = [[a[0], a[3], a[2], a[1]] for a in attended]

    total = residual
    for group in ([0, 1], [2], [3]):
        last = group[-1] == CHUNKS - 1
        total = project(
            z, [attended[c] for c in group], pieces, total, group, width, BF16 if last else F32
        )
    return total


def solution(mesh):
    in_specs = (
        P(("grp", "img"), "seq", None),
        P(("grp", "img"), "seq", None),
        P(("grp", "img"), "seq", None),
        P(("grp", "img"), "seq", None),
        P("img", "seq"),
    )
    out_specs = P(("grp", "img"), "seq", None)
    local = local_line if mesh.shape["seq"] == 4 else local_any
    return jax.shard_map(local, mesh=mesh, in_specs=in_specs, out_specs=out_specs, check_vma=False)
```

time: 915 us -> 757 us (0.83)
  Pallas kernels: 0 us -> 387 us
  waiting for transfers between devices: 514 us -> 195 us
  blocking collectives: 145 us -> 0 us
  starting transfers between devices: 16.1 us -> 133 us
  local copies, waits for them, and re-layouts: 120 us -> 25.7 us
  matrix products: 93.2 us -> 0 us
    pallas_call x0 -> x11, Pallas kernels: none -> 387 us  [the longest x4 291 us: pack(): pl.pallas_call(body, out_shape=[jax.ShapeDtypeStruct((3, images, rows, wi...]
    all_to_all x3 -> x0, waiting for transfers between devices: 335 us -> none  [the longest x1 171 us: local(): lax.all_to_all(values, 'seq', split_axis=2, concat_axis=1, tiled=True)]
    ppermute x0 -> x26, waiting for transfers between devices: none -> 195 us  [the longest x1 68.6 us: local_line(): lax.ppermute(jnp.stack([mine, far]), 'seq', [(i, i ^ 1) for i in range(n)])]
    reduce_scatter x1 -> x0, waiting for transfers between devices: 179 us -> none  [local(): lax.psum_scatter(partial_value.astype(jnp.bfloat16), 'img', scatter_dimen...]
    all_to_all x2 -> x0, blocking collectives: 145 us -> none  [the longest x1 94.3 us: attend(): lax.all_to_all(attended, 'seq', split_axis=1, concat_axis=2, tiled=True)]
    ppermute x0 -> x26, starting transfers between devices: none -> 132 us  [the longest x12 87.6 us: local_line(): lax.ppermute(packs[s - 1], 'seq', onward[s])]
    dot_general x2 -> x0, matrix products: 58.8 us -> none  [the longest x1 33.6 us: local(): jnp.einsum('ipc,cd->ipd', head_block, lax.all_gather(out_weight, 'seq', a...]
    all_to_all x8 -> x0, local copies, waits for them, and re-layouts: 56.8 us -> none  [the longest x3 18 us: attend(): lax.all_to_all(attended, 'seq', split_axis=1, concat_axis=2, tiled=True)]
  transfers between devices with their start and end apart: 5 -> 30, of which waited for: 4 -> 5; matrix products, arithmetic and copies ran while one was open for 19% -> 0% of each run, Pallas kernels for 0% -> 49%
where the time goes in v1:
time: 757 us; the launch traced here: 755 us
  Pallas kernels  387 us (51%)
  waiting for transfers between devices  195 us (26%)
  starting transfers between devices  133 us (18%)
  local copies, waits for them, and re-layouts  25.7 us (3%)
  between operations  13.4 us (2%)
    pallas_call x4, Pallas kernels, pack(): pl.pallas_call(body, out_shape=[jax.ShapeDtypeStruct((3, images, rows, wi...  291 us
    ppermute x12, starting transfers between devices, local_line(): lax.ppermute(packs[s - 1], 'seq', onward[s])  87.6 us
    ppermute x1, waiting for transfers between devices, local_line(): lax.ppermute(jnp.stack([mine, far]), 'seq', [(i, i ^ 1) for i in range(n)])  68.6 us
    ppermute x1, waiting for transfers between devices, local_line(): far = lax.ppermute(mine, 'seq', [(i, i ^ 2) for i in range(n)])  68.4 us
    pallas_call x3, Pallas kernels, project(): pl.pallas_call(body, out_shape=jax.ShapeDtypeStruct((images, rows, model)...  62.3 us
    ppermute x12, waiting for transfers between devices, local_line(): lax.ppermute(packs[s - 1], 'seq', onward[s])  57.6 us
    ppermute x12, starting transfers between devices, local_line(): lax.ppermute(outs[s], 'seq', back[s])  40.1 us
    pallas_call x4, Pallas kernels, attention(): pl.pallas_call(body, out_shape=[jax.ShapeDtypeStruct((images, rows, width...  33.8 us
  transfers between devices with their start and end apart: 30, of which 5 were waited for; matrix products, arithmetic and copies ran while one was open for 0% of the time, Pallas kernels for 49%

profile of v1, /device:TPU:0, one launch (start us, length us, event | category | flops | bytes accessed | tf_op | source)
XLA Modules:
  0.0 755.5 jit_solution(14606133545052067828)
XLA Ops:
  9.7 4.1 collective-permute-start.9
  13.8 68.4 %collective-permute-done.9 = bf16[512,1536]{1,0:T(8,128)(2,1)} collective-permute-done((bf16[512,1536]{1,0:T(8,128)(2,1)}, bf16[512,1536]{1,0:T(8,128)(2,1)}, u32[]{:S(2)}, u32[]{:S(2)}) %collective-permute-start.9) | collective-permute-done | bytes 1572896 | tf_op jit(solution)/shard_map/ppermute | solution.py:228
  84.9 68.6 %collective-permute-done.10 = bf16[2,512,1536]{2,1,0:T(8,128)(2,1)S(1)} collective-permute-done((bf16[2,512,1536]{2,1,0:T(8,128)(2,1)S(1)}, bf16[2,512,1536]{2,1,0:T(8,128)(2,1)S(1)}, u32[]{:S(2)}, u32[]{:S(2)}) %collective-permute-start.10) | collective-permute-done | bytes 3145760 | tf_op jit(solution)/shard_map/ppermute | solution.py:229
  155.9 72.7 %pack0.1 = (bf16[3,2,256,256]{3,2,1,0:T(8,128)(2,1)}, bf16[3,2,256,256]{3,2,1,0:T(8,128)(2,1)}, bf16[3,2,256,256]{3,2,1,0:T(8,128)(2,1)}) custom-call(s32[1]{0:T(128)} %bitcast.z_ref, bf16[2,256,4096]{2,1,0:T(8,128)(2,1)} %q0.7, bf16[2,256,4096]{2,1,0:T(8,128)(2,1)} %k0.7, bf16[2,256,4096]{2,1,0:T(8,128)(2,1)} %v0.7), custom_call_target="tpu_custom_call" | custom-call | bytes 4718592 | tf_op jit(solution)/shard_map/pack0/pallas_call | solution.py:77
  230.1 20.1 %collective-permute-done.rest_0_.r1 = bf16[3,2,256,256]{3,2,1,0:T(8,128)(2,1)S(1)} collective-permute-done((bf16[3,2,256,256]{3,2,1,0:T(8,128)(2,1)}, bf16[3,2,256,256]{3,2,1,0:T(8,128)(2,1)S(1)}, u32[]{:S(2)}, u32[]{:S(2)}) %collective-permute-start) | collective-permute-done | bytes 786464 | tf_op jit(solution)/shard_map/ppermute | solution.py:240
  251.2 72.6 %pack1.1 = (bf16[3,2,256,256]{3,2,1,0:T(8,128)(2,1)}, bf16[3,2,256,256]{3,2,1,0:T(8,128)(2,1)}, bf16[3,2,256,256]{3,2,1,0:T(8,128)(2,1)}) custom-call(s32[1]{0:T(128)} %bitcast.z_ref, bf16[2,256,4096]{2,1,0:T(8,128)(2,1)} %q0.7, bf16[2,256,4096]{2,1,0:T(8,128)(2,1)} %k0.7, bf16[2,256,4096]{2,1,0:T(8,128)(2,1)} %v0.7, bf16[3,2,256,256]{3,2,1,0:T(8,128)(2,1)} %copy-done.12), custom_call_target="tpu_custom_call" | custom-call | bytes 4718592 | tf_op jit(solution)/shard_map/pack1/pallas_call | solution.py:77
  327.7 18.8 %collective-permute-done.1.rest_0_.r1 = bf16[3,2,256,256]{3,2,1,0:T(8,128)(2,1)S(1)} collective-permute-done((bf16[3,2,256,256]{3,2,1,0:T(8,128)(2,1)}, bf16[3,2,256,256]{3,2,1,0:T(8,128)(2,1)S(1)}, u32[]{:S(2)}, u32[]{:S(2)}) %collective-permute-start.1) | collective-permute-done | bytes 786464 | tf_op jit(solution)/shard_map/ppermute | solution.py:240
  347.3 72.6 %pack2.1 = (bf16[3,2,256,256]{3,2,1,0:T(8,128)(2,1)}, bf16[3,2,256,256]{3,2,1,0:T(8,128)(2,1)}, bf16[3,2,256,256]{3,2,1,0:T(8,128)(2,1)}) custom-call(s32[1]{0:T(128)} %bitcast.z_ref, bf16[2,256,4096]{2,1,0:T(8,128)(2,1)} %q0.7, bf16[2,256,4096]{2,1,0:T(8,128)(2,1)} %k0.7, bf16[2,256,4096]{2,1,0:T(8,128)(2,1)} %v0.7, bf16[3,2,256,256]{3,2,1,0:T(8,128)(2,1)} %copy-done.10), custom_call_target="tpu_custom_call" | custom-call | bytes 4718592 | tf_op jit(solution)/shard_map/pack2/pallas_call | solution.py:77
  420.0 30.9 %collective-permute-start.2 = (bf16[3,2,256,256]{3,2,1,0:T(8,128)(2,1)}, bf16[3,2,256,256]{3,2,1,0:T(8,128)(2,1)S(1)}, u32[]{:S(2)}, u32[]{:S(2)}) collective-permute-start(bf16[3,2,256,256]{3,2,1,0:T(8,128)(2,1)} %get-tuple-element.35), channel_id=1, source_target_pairs={{0,4},{4,8},{8,12},{12,0},{1,5},{5,9},{9,13},{13,1},{2,6},{6,10},{... | collective-permute-start | bytes 2359304 | tf_op jit(solution)/shard_map/ppermute | solution.py:240
  462.2 9.1 %attention0.1 = (bf16[2,256,256]{2,1,0:T(8,128)(2,1)S(1)}, bf16[2,256,256]{2,1,0:T(8,128)(2,1)S(1)}, bf16[2,256,256]{2,1,0:T(8,128)(2,1)S(1)}, bf16[2,256,256]{2,1,0:T(8,128)(2,1)}) custom-call(s32[1]{0:T(128)} %bitcast.z_ref, bf16[2,256,4096]{2,1,0:T(8,128)(2,1)S(1)} %copy-done.2, bf16[2,256,4096]{2,1,0:T(8,128)(2,1)S(1)} %copy-done.4, ...), custom_call_target="tpu_custom_call" | custom-call | flops 2147483648 | bytes 4194304 | tf_op jit(solution)/shard_map/attention0/pallas_call | solution.py:129
  473.4 3.3 collective-permute-start.12
  476.7 72.6 %pack3.1 = (bf16[3,2,256,256]{3,2,1,0:T(8,128)(2,1)}, bf16[3,2,256,256]{3,2,1,0:T(8,128)(2,1)}, bf16[3,2,256,256]{3,2,1,0:T(8,128)(2,1)}) custom-call(s32[1]{0:T(128)} %bitcast.z_ref, bf16[2,256,4096]{2,1,0:T(8,128)(2,1)} %q0.7, bf16[2,256,4096]{2,1,0:T(8,128)(2,1)} %k0.7, bf16[2,256,4096]{2,1,0:T(8,128)(2,1)} %v0.7, bf16[3,2,256,256]{3,2,1,0:T(8,128)(2,1)} %copy-done.8), custom_call_target="tpu_custom_call" | custom-call | bytes 4718592 | tf_op jit(solution)/shard_map/pack3/pallas_call | solution.py:77
  549.3 37.9 %collective-permute-start.3 = (bf16[3,2,256,256]{3,2,1,0:T(8,128)(2,1)}, bf16[3,2,256,256]{3,2,1,0:T(8,128)(2,1)S(1)}, u32[]{:S(2)}, u32[]{:S(2)}) collective-permute-start(bf16[3,2,256,256]{3,2,1,0:T(8,128)(2,1)} %get-tuple-element.36), channel_id=1, source_target_pairs={{0,4},{4,8},{8,12},{12,0},{1,5},{5,9},{9,13},{13,1},{2,6},{6,10},{... | collective-permute-start | bytes 2359304 | tf_op jit(solution)/shard_map/ppermute | solution.py:240
  587.2 2.9 collective-permute-start.4
  598.6 8.6 %attention1.1 = (bf16[2,256,256]{2,1,0:T(8,128)(2,1)S(1)}, bf16[2,256,256]{2,1,0:T(8,128)(2,1)S(1)}, bf16[2,256,256]{2,1,0:T(8,128)(2,1)S(1)}, bf16[2,256,256]{2,1,0:T(8,128)(2,1)S(1)}) custom-call(s32[1]{0:T(128)} %bitcast.z_ref, bf16[2,256,4096]{2,1,0:T(8,128)(2,1)S(1)} %copy-done.3, bf16[2,256,4096]{2,1,0:T(8,128)(2,1)S(1)} %copy-done.5, ...), custom_call_target="tpu_custom_call" | custom-call | flops 2147483648 | bytes 4194304 | tf_op jit(solution)/shard_map/attention1/pallas_call | solution.py:129
  610.5 13.0 %collective-permute-start.23 = (bf16[2,256,256]{2,1,0:T(8,128)(2,1)S(1)}, bf16[2,256,256]{2,1,0:T(8,128)(2,1)S(1)}, u32[]{:S(2)}, u32[]{:S(2)}) collective-permute-start(bf16[2,256,256]{2,1,0:T(8,128)(2,1)S(1)} %get-tuple-element.58), channel_id=1, source_target_pairs={{0,4},{4,8},{8,12},{12,0},{1,5},{5,9},{9,13},{13,1},{2,6},{6,10},{... | collective-permute-start | bytes 786440 | tf_op jit(solution)/shard_map/ppermute | solution.py:246
  623.5 18.7 %collective-permute-done.4.r2 = bf16[3,2,256,256]{3,2,1,0:T(8,128)(2,1)S(1)} collective-permute-done((bf16[3,2,256,256]{3,2,1,0:T(8,128)(2,1)}, bf16[3,2,256,256]{3,2,1,0:T(8,128)(2,1)S(1)}, u32[]{:S(2)}, u32[]{:S(2)}) %collective-permute-start.4) | collective-permute-done | bytes 786464 | tf_op jit(solution)/shard_map/ppermute | solution.py:240
  642.2 14.5 %collective-permute-start.25 = (bf16[2,256,256]{2,1,0:T(8,128)(2,1)S(1)}, bf16[2,256,256]{2,1,0:T(8,128)(2,1)S(1)}, u32[]{:S(2)}, u32[]{:S(2)}) collective-permute-start(bf16[2,256,256]{2,1,0:T(8,128)(2,1)S(1)} %get-tuple-element.60), channel_id=1, source_target_pairs={{0,12},{4,0},{8,4},{12,8},{1,13},{5,1},{9,5},{13,9},{2,14},{6,2},{... | collective-permute-start | bytes 786440 | tf_op jit(solution)/shard_map/ppermute | solution.py:246
  656.7 8.0 %attention2.1 = (bf16[2,256,256]{2,1,0:T(8,128)(2,1)S(1)}, bf16[2,256,256]{2,1,0:T(8,128)(2,1)S(1)}, bf16[2,256,256]{2,1,0:T(8,128)(2,1)S(1)}, bf16[2,256,256]{2,1,0:T(8,128)(2,1)S(1)}) custom-call(s32[1]{0:T(128)} %bitcast.z_ref, bf16[2,256,4096]{2,1,0:T(8,128)(2,1)S(1)} %copy-done.3, bf16[2,256,4096]{2,1,0:T(8,128)(2,1)S(1)} %copy-done.5, ...), custom_call_target="tpu_custom_call" | custom-call | flops 2147483648 | bytes 4194304 | tf_op jit(solution)/shard_map/attention2/pallas_call | solution.py:129
  664.8 8.1 %attention3.1 = (bf16[2,256,256]{2,1,0:T(8,128)(2,1)S(1)}, bf16[2,256,256]{2,1,0:T(8,128)(2,1)S(1)}, bf16[2,256,256]{2,1,0:T(8,128)(2,1)S(1)}, bf16[2,256,256]{2,1,0:T(8,128)(2,1)S(1)}) custom-call(s32[1]{0:T(128)} %bitcast.z_ref, bf16[2,256,4096]{2,1,0:T(8,128)(2,1)S(1)} %copy-done.3, bf16[2,256,4096]{2,1,0:T(8,128)(2,1)S(1)} %copy-done.5, ...), custom_call_target="tpu_custom_call" | custom-call | flops 2147483648 | bytes 4194304 | tf_op jit(solution)/shard_map/attention3/pallas_call | solution.py:129
  681.3 24.9 %project01.1.refs_8_ = f32[2,256,6144]{2,1,0:T(8,128)} custom-call(s32[1]{0:T(128)} %bitcast.z_ref, bf16[2,256,256]{2,1,0:T(8,128)(2,1)} %copy-done.14, bf16[2,256,256]{2,1,0:T(8,128)(2,1)} %collective-permute-done.18.refs_1_, bf16[2,256,256]{2,1,0:T(8,128)(2,1)} %copy-done.20, bf16[2,256,256]{2,1,0:T(8,128)(2,1)} %copy-done.21, ...), custom_call_target="tpu_custom_call" | custom-call | flops 12884901888 | bytes 50331648 | tf_op jit(solution)/shard_map/project01/pallas_call | solution.py:191
  706.2 3.0 collective-permute-start.8
  710.0 19.5 %project2.1.refs_8_ = f32[2,256,6144]{2,1,0:T(8,128)} custom-call(s32[1]{0:T(128)} %bitcast.z_ref, bf16[2,256,256]{2,1,0:T(8,128)(2,1)} %copy-done.17, bf16[2,256,256]{2,1,0:T(8,128)(2,1)} %copy-done.25, bf16[2,256,256]{2,1,0:T(8,128)(2,1)} %copy-done.27, bf16[2,256,256]{2,1,0:T(8,128)(2,1)} %copy-done.29, bf16[4,4,256,1536]{3,2,1,0:T(8,128)(2,1)} %bitcast.10, ...), custom_call_target="tpu_custom_call" | custom-call | flops 6442450944 | bytes 37748736 | tf_op jit(solution)/shard_map/project2/pallas_call | solution.py:191
  731.0 17.9 %project3.1 = bf16[2,256,6144]{2,1,0:T(8,128)(2,1)} custom-call(s32[1]{0:T(128)} %bitcast.z_ref, bf16[2,256,256]{2,1,0:T(8,128)(2,1)} %copy-done.16, bf16[2,256,256]{2,1,0:T(8,128)(2,1)} %copy-done.26, bf16[2,256,256]{2,1,0:T(8,128)(2,1)} %copy-done.28, bf16[2,256,256]{2,1,0:T(8,128)(2,1)} %copy-done.30, bf16[4,4,256,1536]{3,2,1,0:T(8,128)(2,1)} %bitcast.11, ...), custom_call_target="tpu_custom_call" | custom-call | flops 6442450944 | bytes 37748736 | tf_op jit(solution)/shard_map/project3/pallas_call | solution.py:191
  (117 shorter events, 51.0 us)
Async XLA Ops:
  6.5 674.8 %all-gather.7.cloned.1.call-start = ((), (), s32[]{:S(2)}) async-start(), calls=%async_computation | async-start | bytes 14155776 | tf_op jit(solution)/shard_map/all_gather | solution.py:232
  9.7 671.6 %all-gather.9.cloned.1.call-start = ((), (), s32[]{:S(2)}) async-start(), calls=%async_computation.1 | async-start | bytes 14155776 | tf_op jit(solution)/shard_map/all_gather | solution.py:232
  9.7 72.5 %collective-permute-start.9 = (bf16[512,1536]{1,0:T(8,128)(2,1)}, bf16[512,1536]{1,0:T(8,128)(2,1)}, u32[]{:S(2)}, u32[]{:S(2)}) collective-permute-start(bf16[512,1536]{1,0:T(8,128)(2,1)} %constant_dynamic-slice_fusion), channel_id=1, source_target_pairs={{0,8},{4,12},{8,0},{12,4},{1,9},{5,13},{9,1},{13,5},{2,10},{6,14},... | collective-permute-start | bytes 4718600 | tf_op jit(solution)/shard_map/ppermute | solution.py:228
  82.3 599.0 %all-gather.11.cloned.1.call-start = ((), (), s32[]{:S(2)}) async-start(), calls=%async_computation.2 | async-start | bytes 14155776 | tf_op jit(solution)/shard_map/all_gather | solution.py:232
  84.3 69.2 %collective-permute-start.10 = (bf16[2,512,1536]{2,1,0:T(8,128)(2,1)S(1)}, bf16[2,512,1536]{2,1,0:T(8,128)(2,1)S(1)}, u32[]{:S(2)}, u32[]{:S(2)}) collective-permute-start(bf16[2,512,1536]{2,1,0:T(8,128)(2,1)S(1)} %pad_maximum_fusion), channel_id=1, source_target_pairs={{0,4},{4,0},{8,12},{12,8},{1,5},{5,1},{9,13},{13,9},{2,6},{6,2},{1... | collective-permute-start | bytes 9437192 | tf_op jit(solution)/shard_map/ppermute | solution.py:229
  155.4 525.9 %all-gather.13.cloned.1.call-start = ((), (), s32[]{:S(2)}) async-start(), calls=%async_computation.3 | async-start | bytes 14155776 | tf_op jit(solution)/shard_map/all_gather | solution.py:232
  323.9 131.8 %collective-permute-start.16 = (bf16[3,2,256,256]{3,2,1,0:T(8,128)(2,1)}, bf16[3,2,256,256]{3,2,1,0:T(8,128)(2,1)S(1)}, u32[]{:S(2)}, u32[]{:S(2)}) collective-permute-start(bf16[3,2,256,256]{3,2,1,0:T(8,128)(2,1)} %get-tuple-element.49), channel_id=1, source_target_pairs={{0,8},{4,12},{8,0},{12,4},{1,9},{5,13},{9,1},{13,5},{2,10},{6,14},... | collective-permute-start | bytes 2359304 | tf_op jit(solution)/shard_map/ppermute | solution.py:240
  326.2 129.5 %collective-permute-start.17 = (bf16[3,2,256,256]{3,2,1,0:T(8,128)(2,1)}, bf16[3,2,256,256]{3,2,1,0:T(8,128)(2,1)}, u32[]{:S(2)}, u32[]{:S(2)}) collective-permute-start(bf16[3,2,256,256]{3,2,1,0:T(8,128)(2,1)} %get-tuple-element.50), channel_id=1, source_target_pairs={{0,12},{4,0},{8,4},{12,8},{1,13},{5,1},{9,5},{13,9},{2,14},{6,2},{... | collective-permute-start | bytes 2359304 | tf_op jit(solution)/shard_map/ppermute | solution.py:240
  420.0 53.4 %collective-permute-start.2 = (bf16[3,2,256,256]{3,2,1,0:T(8,128)(2,1)}, bf16[3,2,256,256]{3,2,1,0:T(8,128)(2,1)S(1)}, u32[]{:S(2)}, u32[]{:S(2)}) collective-permute-start(bf16[3,2,256,256]{3,2,1,0:T(8,128)(2,1)} %get-tuple-element.35), channel_id=1, source_target_pairs={{0,4},{4,8},{8,12},{12,0},{1,5},{5,9},{9,13},{13,1},{2,6},{6,10},{... | collective-permute-start | bytes 2359304 | tf_op jit(solution)/shard_map/ppermute | solution.py:240
  450.9 136.3 %collective-permute-start.21 = (bf16[3,2,256,256]{3,2,1,0:T(8,128)(2,1)}, bf16[3,2,256,256]{3,2,1,0:T(8,128)(2,1)}, u32[]{:S(2)}, u32[]{:S(2)}) collective-permute-start(bf16[3,2,256,256]{3,2,1,0:T(8,128)(2,1)} %get-tuple-element.55), channel_id=1, source_target_pairs={{0,8},{4,12},{8,0},{12,4},{1,9},{5,13},{9,1},{13,5},{2,10},{6,14},... | collective-permute-start | bytes 2359304 | tf_op jit(solution)/shard_map/ppermute | solution.py:240
  452.8 137.4 %collective-permute-start.22 = (bf16[3,2,256,256]{3,2,1,0:T(8,128)(2,1)}, bf16[3,2,256,256]{3,2,1,0:T(8,128)(2,1)}, u32[]{:S(2)}, u32[]{:S(2)}) collective-permute-start(bf16[3,2,256,256]{3,2,1,0:T(8,128)(2,1)} %get-tuple-element.56), channel_id=1, source_target_pairs={{0,12},{4,0},{8,4},{12,8},{1,13},{5,1},{9,5},{13,9},{2,14},{6,2},{... | collective-permute-start | bytes 2359304 | tf_op jit(solution)/shard_map/ppermute | solution.py:240
  472.8 76.6 %collective-permute-start.18 = (bf16[2,256,256]{2,1,0:T(8,128)(2,1)}, bf16[2,256,256]{2,1,0:T(8,128)(2,1)}, u32[]{:S(2)}, u32[]{:S(2)}) collective-permute-start(bf16[2,256,256]{2,1,0:T(8,128)(2,1)} %get-tuple-element.52), channel_id=1, source_target_pairs={{0,4},{4,8},{8,12},{12,0},{1,5},{5,9},{9,13},{13,1},{2,6},{6,10},{... | collective-permute-start | bytes 786440 | tf_op jit(solution)/shard_map/ppermute | solution.py:246
  472.8 135.1 %collective-permute-start.11 = (bf16[3,2,256,256]{3,2,1,0:T(8,128)(2,1)}, bf16[3,2,256,256]{3,2,1,0:T(8,128)(2,1)S(1)}, u32[]{:S(2)}, u32[]{:S(2)}) collective-permute-start(bf16[3,2,256,256]{3,2,1,0:T(8,128)(2,1)} %get-tuple-element.43), channel_id=1, source_target_pairs={{0,8},{4,12},{8,0},{12,4},{1,9},{5,13},{9,1},{13,5},{2,10},{6,14},... | collective-permute-start | bytes 2359304 | tf_op jit(solution)/shard_map/ppermute | solution.py:240
  473.4 134.6 %collective-permute-start.12 = (bf16[3,2,256,256]{3,2,1,0:T(8,128)(2,1)}, bf16[3,2,256,256]{3,2,1,0:T(8,128)(2,1)S(1)}, u32[]{:S(2)}, u32[]{:S(2)}) collective-permute-start(bf16[3,2,256,256]{3,2,1,0:T(8,128)(2,1)} %get-tuple-element.44), channel_id=1, source_target_pairs={{0,12},{4,0},{8,4},{12,8},{1,13},{5,1},{9,5},{13,9},{2,14},{6,2},{... | collective-permute-start | bytes 2359304 | tf_op jit(solution)/shard_map/ppermute | solution.py:240
  549.3 61.2 %collective-permute-start.3 = (bf16[3,2,256,256]{3,2,1,0:T(8,128)(2,1)}, bf16[3,2,256,256]{3,2,1,0:T(8,128)(2,1)S(1)}, u32[]{:S(2)}, u32[]{:S(2)}) collective-permute-start(bf16[3,2,256,256]{3,2,1,0:T(8,128)(2,1)} %get-tuple-element.36), channel_id=1, source_target_pairs={{0,4},{4,8},{8,12},{12,0},{1,5},{5,9},{9,13},{13,1},{2,6},{6,10},{... | collective-permute-start | bytes 2359304 | tf_op jit(solution)/shard_map/ppermute | solution.py:240
  587.2 54.9 %collective-permute-start.4 = (bf16[3,2,256,256]{3,2,1,0:T(8,128)(2,1)}, bf16[3,2,256,256]{3,2,1,0:T(8,128)(2,1)S(1)}, u32[]{:S(2)}, u32[]{:S(2)}) collective-permute-start(bf16[3,2,256,256]{3,2,1,0:T(8,128)(2,1)} %get-tuple-element.37), channel_id=1, source_target_pairs={{0,8},{4,12},{8,0},{12,4},{1,9},{5,13},{9,1},{13,5},{2,10},{6,14},... | collective-permute-start | bytes 2359304 | tf_op jit(solution)/shard_map/ppermute | solution.py:240
  590.2 52.0 %collective-permute-start.5 = (bf16[3,2,256,256]{3,2,1,0:T(8,128)(2,1)}, bf16[3,2,256,256]{3,2,1,0:T(8,128)(2,1)S(1)}, u32[]{:S(2)}, u32[]{:S(2)}) collective-permute-start(bf16[3,2,256,256]{3,2,1,0:T(8,128)(2,1)} %get-tuple-element.38), channel_id=1, source_target_pairs={{0,12},{4,0},{8,4},{12,8},{1,13},{5,1},{9,5},{13,9},{2,14},{6,2},{... | collective-permute-start | bytes 2359304 | tf_op jit(solution)/shard_map/ppermute | solution.py:240
  607.9 65.7 %collective-permute-start.19 = (bf16[2,256,256]{2,1,0:T(8,128)(2,1)S(1)}, bf16[2,256,256]{2,1,0:T(8,128)(2,1)S(1)}, u32[]{:S(2)}, u32[]{:S(2)}) collective-permute-start(bf16[2,256,256]{2,1,0:T(8,128)(2,1)S(1)} %copy-done.19), channel_id=1, source_target_pairs={{0,8},{4,12},{8,0},{12,4},{1,9},{5,13},{9,1},{13,5},{2,10},{6,14},... | collective-permute-start | bytes 786440 | tf_op jit(solution)/shard_map/ppermute | solution.py:246
  607.9 67.5 %collective-permute-start.20 = (bf16[2,256,256]{2,1,0:T(8,128)(2,1)S(1)}, bf16[2,256,256]{2,1,0:T(8,128)(2,1)S(1)}, u32[]{:S(2)}, u32[]{:S(2)}) collective-permute-start(bf16[2,256,256]{2,1,0:T(8,128)(2,1)S(1)} %get-tuple-element.54), channel_id=1, source_target_pairs={{0,12},{4,0},{8,4},{12,8},{1,13},{5,1},{9,5},{13,9},{2,14},{6,2},{... | collective-permute-start | bytes 786440 | tf_op jit(solution)/shard_map/ppermute | solution.py:246
  610.5 66.4 %collective-permute-start.23 = (bf16[2,256,256]{2,1,0:T(8,128)(2,1)S(1)}, bf16[2,256,256]{2,1,0:T(8,128)(2,1)S(1)}, u32[]{:S(2)}, u32[]{:S(2)}) collective-permute-start(bf16[2,256,256]{2,1,0:T(8,128)(2,1)S(1)} %get-tuple-element.58), channel_id=1, source_target_pairs={{0,4},{4,8},{8,12},{12,0},{1,5},{5,9},{9,13},{13,1},{2,6},{6,10},{... | collective-permute-start | bytes 786440 | tf_op jit(solution)/shard_map/ppermute | solution.py:246
  642.2 37.6 %collective-permute-start.24 = (bf16[2,256,256]{2,1,0:T(8,128)(2,1)S(1)}, bf16[2,256,256]{2,1,0:T(8,128)(2,1)S(1)}, u32[]{:S(2)}, u32[]{:S(2)}) collective-permute-start(bf16[2,256,256]{2,1,0:T(8,128)(2,1)S(1)} %get-tuple-element.59), channel_id=1, source_target_pairs={{0,8},{4,12},{8,0},{12,4},{1,9},{5,13},{9,1},{13,5},{2,10},{6,14},... | collective-permute-start | bytes 786440 | tf_op jit(solution)/shard_map/ppermute | solution.py:246
  642.2 37.6 %collective-permute-start.25 = (bf16[2,256,256]{2,1,0:T(8,128)(2,1)S(1)}, bf16[2,256,256]{2,1,0:T(8,128)(2,1)S(1)}, u32[]{:S(2)}, u32[]{:S(2)}) collective-permute-start(bf16[2,256,256]{2,1,0:T(8,128)(2,1)S(1)} %get-tuple-element.60), channel_id=1, source_target_pairs={{0,12},{4,0},{8,4},{12,8},{1,13},{5,1},{9,5},{13,9},{2,14},{6,2},{... | collective-permute-start | bytes 786440 | tf_op jit(solution)/shard_map/ppermute | solution.py:246
  679.8 49.7 %collective-permute-start.6 = (bf16[2,256,256]{2,1,0:T(8,128)(2,1)S(1)}, bf16[2,256,256]{2,1,0:T(8,128)(2,1)S(1)}, u32[]{:S(2)}, u32[]{:S(2)}) collective-permute-start(bf16[2,256,256]{2,1,0:T(8,128)(2,1)S(1)} %get-tuple-element.40), channel_id=1, source_target_pairs={{0,4},{4,8},{8,12},{12,0},{1,5},{5,9},{9,13},{13,1},{2,6},{6,10},{... | collective-permute-start | bytes 786440 | tf_op jit(solution)/shard_map/ppermute | solution.py:246
  680.6 49.0 %collective-permute-start.7 = (bf16[2,256,256]{2,1,0:T(8,128)(2,1)S(1)}, bf16[2,256,256]{2,1,0:T(8,128)(2,1)S(1)}, u32[]{:S(2)}, u32[]{:S(2)}) collective-permute-start(bf16[2,256,256]{2,1,0:T(8,128)(2,1)S(1)} %get-tuple-element.41), channel_id=1, source_target_pairs={{0,8},{4,12},{8,0},{12,4},{1,9},{5,13},{9,1},{13,5},{2,10},{6,14},... | collective-permute-start | bytes 786440 | tf_op jit(solution)/shard_map/ppermute | solution.py:246
  (37 other events, 552.9 us)
Sparse Core Ops, SparseCore 0:
  9.8 74.8 all-gather.6
  86.6 72.1 all-gather.8
  160.6 72.1 all-gather.10
  234.5 72.1 all-gather.12

commit v2 on v0

v2 whole, which is shorter than its diff:
```python
import jax
import jax.numpy as jnp
from jax import lax
from jax.experimental import pallas as pl
from jax.experimental.pallas import tpu as pltpu
from jax.sharding import PartitionSpec as P

HEAD_DIM = 128
CHUNKS = 4
SEQ = 4
BF16 = jnp.bfloat16
F32 = jnp.float32
VMEM = 56 * 2**20
ATTENTION_COST = 400
PROJECT_COST = 15
GROUPS = ([1], [2], [3])


def attend(triple):
    query_rows, key_rows, value_rows = triple
    images_here, patches_all, row_width = query_rows.shape
    heads_here = row_width // HEAD_DIM
    query_heads = query_rows.reshape(images_here, patches_all, heads_here, HEAD_DIM)
    key_heads = key_rows.reshape(images_here, patches_all, heads_here, HEAD_DIM)
    value_heads = value_rows.reshape(images_here, patches_all, heads_here, HEAD_DIM)
    scores = jnp.einsum(
        "nqhd,nkhd->nhqk", query_heads, key_heads, preferred_element_type=F32
    )
    scores = scores * (1.0 / HEAD_DIM**0.5)
    weights = jax.nn.softmax(scores, axis=-1).astype(BF16)
    attended = jnp.einsum(
        "nhqk,nkhd->nqhd", weights, value_heads, preferred_element_type=F32
    )
    attended = attended.astype(BF16).reshape(images_here, patches_all, row_width)
    return lax.all_to_all(attended, "seq", split_axis=1, concat_axis=2, tiled=True)


def local_any(queries, keys, values, residual, out_weight):
    attended = attend(
        (
            lax.all_to_all(queries, "seq", split_axis=2, concat_axis=1, tiled=True),
            lax.all_to_all(keys, "seq", split_axis=2, concat_axis=1, tiled=True),
            lax.all_to_all(values, "seq", split_axis=2, concat_axis=1, tiled=True),
        )
    )
    head_block = lax.all_to_all(attended, "img", split_axis=2, concat_axis=0, tiled=True)
    partial_value = jnp.einsum(
        "ipc,cd->ipd",
        head_block,
        lax.all_gather(out_weight, "seq", axis=1, tiled=True),
        preferred_element_type=F32,
    )
    summed = lax.psum_scatter(
        partial_value.astype(BF16), "img", scatter_dimension=0, tiled=True
    ).astype(F32)
    return (residual.astype(F32) + summed).astype(BF16)


def tie(values, after):
    def body(*refs):
        pass

    anywhere = pl.BlockSpec(memory_space=pl.ANY)
    many = len(values)
    return pl.pallas_call(
        body,
        out_shape=[jax.ShapeDtypeStruct(v.shape, v.dtype) for v in values],
        in_specs=[anywhere] * (many + 1),
        out_specs=[anywhere] * many,
        input_output_aliases={i: i for i in range(many)},
        name="tie",
    )(*values, after)


def cost(microseconds, moved):
    return pl.CostEstimate(
        flops=int(microseconds * 1e9), bytes_accessed=moved, transcendentals=0
    )


def head_columns(rows, width, per_device, xor, at):
    return pl.BlockSpec(
        (1, rows, width),
        lambda i, h, z_ref: (
            i,
            0,
            jnp.bitwise_xor(z_ref[0], xor) * per_device + at + h,
        ),
    )


def pack_first(z, grp, queries, keys, values, out_weight, width):
    images, rows, columns = queries.shape
    tiles = out_weight.shape[1] // width

    def body(z_ref, *refs):
        ins, w, outs, half = refs[:9], refs[9], refs[10:13], refs[13]
        for m in range(SEQ - 1):
            for t in range(3):
                outs[m][t, 0] = ins[3 * m + t][0]
        for t in range(tiles):
            piece = w[:, t * width : (t + 1) * width]
            outs[0][3 + t, 0] = piece
            outs[1][3 + t, 0] = piece
            half[t, 0] = piece

    def message(blocks):
        return jax.ShapeDtypeStruct((blocks, images, rows, width), BF16)

    def message_spec(blocks):
        return pl.BlockSpec((blocks, 1, rows, width), lambda i, h, z_ref: (0, i, 0, 0))

    blocks = (3 + tiles, 3 + tiles, 3, tiles)
    *packs, half = pl.pallas_call(
        body,
        out_shape=[message(b) for b in blocks],
        grid_spec=pltpu.PrefetchScalarGridSpec(
            num_scalar_prefetch=1,
            grid=(images, 1),
            in_specs=[
                head_columns(rows, width, CHUNKS, m, 0) for m in range(1, SEQ) for _ in range(3)
            ]
            + [
                pl.BlockSpec(
                    (rows, tiles * width), lambda i, h, z_ref: (z_ref[1] * images + i, 0)
                )
            ],
            out_specs=[message_spec(b) for b in blocks],
        ),
        compiler_params=pltpu.CompilerParams(vmem_limit_bytes=VMEM),
        cost_estimate=cost(5, 10 * 2**20),
        name="pack0",
    )(jnp.concatenate([z, grp]), *[queries, keys, values] * (SEQ - 1), out_weight)
    return packs, half


def pack_second(z, queries, keys, values, came, width):
    images, rows, columns = queries.shape
    tiles = came.shape[0] - 3

    def body(z_ref, *refs):
        ins, came, outs = refs[:9], refs[9], refs[10:]
        for m in range(SEQ - 1):
            for t in range(3):
                outs[m][t, 0] = ins[3 * m + t][0]
        outs[0][3:, 0] = came[3:, 0]

    def message_spec(blocks):
        return pl.BlockSpec((blocks, 1, rows, width), lambda i, h, z_ref: (0, i, 0, 0))

    blocks = (3 + tiles, 3, 3)
    return pl.pallas_call(
        body,
        out_shape=[jax.ShapeDtypeStruct((b, images, rows, width), BF16) for b in blocks],
        grid_spec=pltpu.PrefetchScalarGridSpec(
            num_scalar_prefetch=1,
            grid=(images, 1),
            in_specs=[
                head_columns(rows, width, CHUNKS, m, 1) for m in range(1, SEQ) for _ in range(3)
            ]
            + [message_spec(3 + tiles)],
            out_specs=[message_spec(b) for b in blocks],
        ),
        compiler_params=pltpu.CompilerParams(vmem_limit_bytes=VMEM),
        cost_estimate=cost(5, 10 * 2**20),
        name="pack1",
    )(z, *[queries, keys, values] * (SEQ - 1), came)


def attention(z, queries, keys, values, received, chunk, width, after):
    images, rows, columns = queries.shape
    heads = width // HEAD_DIM
    per_device = columns // SEQ // HEAD_DIM
    more = 3 if chunk + 2 < CHUNKS else 0
    factor = 1.4426950408889634 / HEAD_DIM**0.5

    def body(z_ref, *refs):
        q0, k0, v0 = refs[:3]
        others = [refs[3 * m : 3 * m + 3] for m in range(1, SEQ)]
        passed = refs[3 * SEQ : 3 * SEQ + more * (SEQ - 1)]
        own_out, *outs = refs[-2 - SEQ : -2]
        k_all, v_all = refs[-2:]
        for m in range(more and SEQ - 1):
            for t in range(3):
                outs[m][t, 0] = passed[3 * m + t][0]
        k_all[0:rows] = k0[0]
        v_all[0:rows, 0:HEAD_DIM] = v0[0]
        for m, (_, k, v) in enumerate(others, 1):
            k_all[m * rows : (m + 1) * rows] = k[0, 0]
            v_all[m * rows : (m + 1) * rows, 0:HEAD_DIM] = v[0, 0]
        v_all[:, HEAD_DIM:] = jnp.ones((SEQ * rows, HEAD_DIM), BF16)
        for m in range(SEQ):
            q = others[m - 1][0][0, 0] if m else q0[0]
            scores = lax.dot_general(
                q, k_all[...], (((1,), (1,)), ((), ())), preferred_element_type=F32
            )
            most = jnp.max(scores, axis=-1, keepdims=True)
            weights = jnp.exp2((scores - most) * factor).astype(BF16)
            sums = jnp.dot(weights, v_all[...], preferred_element_type=F32)
            result = (sums[:, :HEAD_DIM] / sums[:, HEAD_DIM:]).astype(BF16)
            if m:
                outs[m - 1][more, 0] = result
            else:
                own_out[0] = result

    def of(t):
        return pl.BlockSpec((1, 1, rows, HEAD_DIM), lambda i, h, z_ref: (t, i, 0, h))

    own_spec = pl.BlockSpec((1, rows, HEAD_DIM), lambda i, h, z_ref: (i, 0, h))
    out_spec = pl.BlockSpec(
        (more + 1, 1, rows, HEAD_DIM), lambda i, h, z_ref: (0, i, 0, h)
    )
    own, *packs = pl.pallas_call(
        body,
        out_shape=[jax.ShapeDtypeStruct((images, rows, width), BF16)]
        + [jax.ShapeDtypeStruct((more + 1, images, rows, width), BF16)] * (SEQ - 1),
        grid_spec=pltpu.PrefetchScalarGridSpec(
            num_scalar_prefetch=1,
            grid=(images, heads),
            in_specs=[head_columns(rows, HEAD_DIM, per_device, 0, chunk * heads)] * 3
            + [of(t) for _ in range(1, SEQ) for t in range(3)]
            + [
                head_columns(rows, HEAD_DIM, per_device, m, (chunk + 2) * heads)
                for m in range(1, SEQ)
                for _ in range(more)
            ]
            + [pl.BlockSpec(memory_space=pl.ANY)] * len(after),
            out_specs=[own_spec] + [out_spec] * (SEQ - 1),
            scratch_shapes=[
                pltpu.VMEM((SEQ * rows, HEAD_DIM), BF16),
                pltpu.VMEM((SEQ * rows, 2 * HEAD_DIM), BF16),
            ],
        ),
        compiler_params=pltpu.CompilerParams(vmem_limit_bytes=VMEM),
        cost_estimate=cost(ATTENTION_COST, 10 * 2**20),
        name=f"attention{chunk}",
    )(
        z,
        queries,
        keys,
        values,
        *[r for r in received for _ in range(3)],
        *([queries, keys, values] * (SEQ - 1) if more else []),
        *after,
    )
    return own, packs


def project(z, attended, pieces, total, chunks, width, out_type):
    images, rows, model = total.shape
    tiles = pieces[0].shape[2]
    grouped = 2 if tiles % 2 == 0 else 1
    steps = tiles // grouped
    tile = grouped * width
    halves = pieces[0].shape[3]
    many = len(chunks)
    attended = [o for chunk in attended for o in chunk]
    n_w = SEQ * many

    def body(z_ref, *refs):
        o_refs = refs[: many * SEQ]
        w_refs = refs[many * SEQ : many * SEQ + n_w]
        total_ref, out_ref, rows_all = refs[-3:]
        at = pl.program_id(0)

        @pl.when(at == 0)
        def _():
            for i in range(many):
                for m in range(SEQ):
                    heads_of = jnp.bitwise_xor(z_ref[0], m)
                    cols = pl.ds(pl.multiple_of(heads_of * width, HEAD_DIM), width)
                    rows_all[i, :, cols] = o_refs[i * SEQ + m][...].reshape(
                        images * rows, width
                    )

        def step(p):
            for g in range(grouped):
                cols = slice(g * width, (g + 1) * width)
                value = total_ref[:, :, cols].astype(F32).reshape(images * rows, width)
                for i in range(many):
                    value += jnp.dot(
                        rows_all[i],
                        w_refs[i * SEQ + p][:, 0, g, 0].reshape(SEQ * width, width),
                        preferred_element_type=F32,
                    )
                out_ref[:, :, cols] = value.astype(out_type).reshape(images, rows, width)

        for p in range(SEQ):
            pl.when(at // steps == p)(lambda p=p: step(p))

    def column(at, z_ref):
        return (0, 0, jnp.bitwise_xor(z_ref[0], at // steps) * steps + at % steps)

    def weight_spec(chunk, p):
        return pl.BlockSpec(
            (SEQ, 1, grouped, 1, rows, width),
            lambda at, z_ref: (
                0,
                chunk // halves,
                jnp.clip(at - p * steps, 0, steps - 1),
                chunk % halves,
                0,
                0,
            ),
        )

    def attended_spec(array):
        if array.ndim == 3:
            return pl.BlockSpec((images, rows, width), lambda at, z_ref: (0, 0, 0))
        last = array.shape[0] - 1
        return pl.BlockSpec(
            (1, images, rows, width), lambda at, z_ref: (last, 0, 0, 0)
        )

    block = pl.BlockSpec((images, rows, tile), column)
    return pl.pallas_call(
        body,
        out_shape=jax.ShapeDtypeStruct((images, rows, model), out_type),
        grid_spec=pltpu.PrefetchScalarGridSpec(
            num_scalar_prefetch=1,
            grid=(SEQ * steps,),
            in_specs=[attended_spec(o) for o in attended]
            + [weight_spec(chunk, p) for chunk in chunks for p in range(SEQ)]
            + [block],
            out_specs=block,
            scratch_shapes=[pltpu.VMEM((many, images * rows, SEQ * width), BF16)],
        ),
        compiler_params=pltpu.CompilerParams(vmem_limit_bytes=VMEM),
        cost_estimate=cost(PROJECT_COST, 30 * 2**20),
        name="project" + "".join(str(c) for c in chunks),
    )(z, *attended, *[p for _ in chunks for p in pieces], total)


def local_line(queries, keys, values, residual, out_weight):
    images, rows, columns = queries.shape
    width = columns // SEQ // CHUNKS
    z = lax.axis_index("seq").astype(jnp.int32).reshape(1)
    grp = lax.axis_index("grp").astype(jnp.int32).reshape(1)

    def send(packs):
        came = [None] * (SEQ - 1)
        for m in (2, 3, 1):
            came[m - 1] = lax.ppermute(packs[m - 1], "seq", [(i, i ^ m) for i in range(SEQ)])
        return came

    def whole(piece):
        full = lax.all_gather(piece, ("img", "grp"), axis=0, tiled=True)
        return full.reshape(lax.axis_size("img"), lax.axis_size("grp"), *piece.shape)

    packs, half = pack_first(z, grp, queries, keys, values, out_weight, width)
    received = [send(packs)]
    near, far, _ = received[0]
    received.append(send(pack_second(z, queries, keys, values, far, width)))
    pieces = [whole(half), whole(near[3:]), whole(far[3:]), whole(received[1][0][3:])]

    def add(total, *chunks):
        attended = [[owns[c], *received[c + 2]] for c in chunks]
        kept = BF16 if chunks[-1] == CHUNKS - 1 else F32
        return project(z, attended, pieces, total, chunks, width, kept)

    owns = []
    total = residual
    for c in range(CHUNKS):
        after = []
        if c == CHUNKS - 1:
            total = add(total, 0)
            after = [total]
        own, packs = attention(z, queries, keys, values, received[c], c, width, after)
        owns.append(own)
        if c == CHUNKS - 2:
            packs = tie(packs, received[c + 1][1])
        received.append(send(packs))
    for chunks in GROUPS:
        total = add(total, *chunks)
    return total


def solution(mesh):
    in_specs = (
        P(("grp", "img"), "seq", None),
        P(("grp", "img"), "seq", None),
        P(("grp", "img"), "seq", None),
        P(("grp", "img"), "seq", None),
        P("img", "seq"),
    )
    out_specs = P(("grp", "img"), "seq", None)
    local = local_line if mesh.shape["seq"] == 4 else local_any
    return jax.shard_map(local, mesh=mesh, in_specs=in_specs, out_specs=out_specs, check_vma=False)
```

time: 915 us -> 491 us (0.54)
  waiting for transfers between devices: 514 us -> 246 us
  blocking collectives: 145 us -> 0 us
  Pallas kernels: 0 us -> 123 us
  local copies, waits for them, and re-layouts: 120 us -> 11.8 us
  matrix products: 93.2 us -> 0 us
  starting transfers between devices: 16.1 us -> 95.2 us
  other arithmetic: 9.96 us -> 0.57 us
    all_to_all x3 -> x0, waiting for transfers between devices: 335 us -> none  [the longest x1 171 us: local(): lax.all_to_all(values, 'seq', split_axis=2, concat_axis=1, tiled=True)]
    ppermute x0 -> x18, waiting for transfers between devices: none -> 239 us  [send(): lax.ppermute(packs[m - 1], 'seq', [(i, i ^ m) for i in range(SEQ)])]
    reduce_scatter x1 -> x0, waiting for transfers between devices: 179 us -> none  [local(): lax.psum_scatter(partial_value.astype(jnp.bfloat16), 'img', scatter_dimen...]
    all_to_all x2 -> x0, blocking collectives: 145 us -> none  [the longest x1 94.3 us: attend(): lax.all_to_all(attended, 'seq', split_axis=1, concat_axis=2, tiled=True)]
    pallas_call x0 -> x11, Pallas kernels: none -> 123 us  [the longest x4 75.2 us: project(): pl.pallas_call(body, out_shape=jax.ShapeDtypeStruct((images, rows, model)...]
    ppermute x0 -> x18, starting transfers between devices: none -> 94.9 us  [send(): lax.ppermute(packs[m - 1], 'seq', [(i, i ^ m) for i in range(SEQ)])]
    dot_general x2 -> x0, matrix products: 58.8 us -> none  [the longest x1 33.6 us: local(): jnp.einsum('ipc,cd->ipd', head_block, lax.all_gather(out_weight, 'seq', a...]
    all_to_all x8 -> x0, local copies, waits for them, and re-layouts: 56.8 us -> none  [the longest x3 18 us: attend(): lax.all_to_all(attended, 'seq', split_axis=1, concat_axis=2, tiled=True)]
  transfers between devices with their start and end apart: 5 -> 22, of which waited for: 4 -> 10; matrix products, arithmetic and copies ran while one was open for 19% -> 1% of each run, Pallas kernels for 0% -> 20%
where the time goes in v2:
time: 491 us; the launch traced here: 490 us
  waiting for transfers between devices  246 us (50%)
  Pallas kernels  123 us (25%)
  starting transfers between devices  95.2 us (19%)
  between operations  13.2 us (3%)
  local copies, waits for them, and re-layouts  11.8 us (2%)
    ppermute x18, waiting for transfers between devices, send(): lax.ppermute(packs[m - 1], 'seq', [(i, i ^ m) for i in range(SEQ)])  239 us
    ppermute x18, starting transfers between devices, send(): lax.ppermute(packs[m - 1], 'seq', [(i, i ^ m) for i in range(SEQ)])  94.9 us
    pallas_call x4, Pallas kernels, project(): pl.pallas_call(body, out_shape=jax.ShapeDtypeStruct((images, rows, model)...  75.2 us
    pallas_call x4, Pallas kernels, attention(): pl.pallas_call(body, out_shape=[jax.ShapeDtypeStruct((images, rows, width...  38.4 us
  transfers between devices with their start and end apart: 22, of which 10 were waited for; matrix products, arithmetic and copies ran while one was open for 1% of the time, Pallas kernels for 20%

profile of v2, /device:TPU:0, one launch (start us, length us, event | category | flops | bytes accessed | tf_op | source)
XLA Modules:
  0.0 490.0 jit_solution(15109596268353025534)
XLA Ops:
  7.1 5.5 %pack0.1 = (bf16[9,2,256,256]{3,2,1,0:T(8,128)(2,1)}, bf16[9,2,256,256]{3,2,1,0:T(8,128)(2,1)}, bf16[3,2,256,256]{3,2,1,0:T(8,128)(2,1)}, bf16[6,2,256,256]{3,2,1,0:T(8,128)(2,1)}) custom-call(s32[2]{0:T(128)} %pad_add_fusion.z_ref, bf16[2,256,4096]{2,1,0:T(8,128)(2,1)} %refs_0_.11, bf16[2,256,4096]{2,1,0:T(8,128)(2,1)} %refs_1_.11, ...), custom_call_target="tpu_custom_call" | custom-call | flops 5000000000 | bytes 10485760 | tf_op jit(solution)/shard_map/pack0/pallas_call | solution.py:114
  12.7 4.1 collective-permute-start
  18.4 102.2 %collective-permute-done.refs_9_.refs_6_.refs_7_.refs_8_ = bf16[9,2,256,256]{3,2,1,0:T(8,128)(2,1)S(1)} collective-permute-done((bf16[9,2,256,256]{3,2,1,0:T(8,128)(2,1)}, bf16[9,2,256,256]{3,2,1,0:T(8,128)(2,1)S(1)}, u32[]{:S(2)}, u32[]{:S(2)}) %collective-permute-start) | collective-permute-done | bytes 2359328 | tf_op jit(solution)/shard_map/ppermute | solution.py:343
  122.0 4.1 pack1.1
  133.3 4.7 collective-permute-done.8.refs_9_.refs_10_.refs_11_
  138.9 10.2 %attention0.1 = (bf16[2,256,256]{2,1,0:T(8,128)(2,1)}, bf16[4,2,256,256]{3,2,1,0:T(8,128)(2,1)}, bf16[4,2,256,256]{3,2,1,0:T(8,128)(2,1)}, bf16[4,2,256,256]{3,2,1,0:T(8,128)(2,1)}) custom-call(s32[1]{0:T(128)} %bitcast.z_ref, bf16[2,256,4096]{2,1,0:T(8,128)(2,1)} %refs_0_.11, bf16[2,256,4096]{2,1,0:T(8,128)(2,1)} %refs_1_.11, ...), custom_call_target="tpu_custom_call" | custom-call | flops 399999991808 | bytes 10485760 | tf_op jit(solution)/shard_map/attention0/pallas_call | solution.py:213
  149.1 16.4 %collective-permute-start.9 = (bf16[4,2,256,256]{3,2,1,0:T(8,128)(2,1)}, bf16[4,2,256,256]{3,2,1,0:T(8,128)(2,1)}, u32[]{:S(2)}, u32[]{:S(2)}) collective-permute-start(bf16[4,2,256,256]{3,2,1,0:T(8,128)(2,1)} %get-tuple-element.41), channel_id=1, source_target_pairs={{0,4},{4,0},{8,12},{12,8},{1,5},{5,1},{9,13},{13,9},{2,6},{6,2},{1... | collective-permute-start | bytes 3145736 | tf_op jit(solution)/shard_map/ppermute | solution.py:343
  168.4 35.4 %collective-permute-done.2.refs_6_.refs_7_.refs_8_ = bf16[3,2,256,256]{3,2,1,0:T(8,128)(2,1)} collective-permute-done((bf16[3,2,256,256]{3,2,1,0:T(8,128)(2,1)}, bf16[3,2,256,256]{3,2,1,0:T(8,128)(2,1)}, u32[]{:S(2)}, u32[]{:S(2)}) %collective-permute-start.2) | collective-permute-done | bytes 786464 | tf_op jit(solution)/shard_map/ppermute | solution.py:343
  205.0 17.4 %collective-permute-done.3.refs_9_.refs_10_.refs_11_ = bf16[3,2,256,256]{3,2,1,0:T(8,128)(2,1)} collective-permute-done((bf16[3,2,256,256]{3,2,1,0:T(8,128)(2,1)}, bf16[3,2,256,256]{3,2,1,0:T(8,128)(2,1)}, u32[]{:S(2)}, u32[]{:S(2)}) %collective-permute-start.3) | collective-permute-done | bytes 786464 | tf_op jit(solution)/shard_map/ppermute | solution.py:343
  222.4 21.1 %collective-permute-done.1.refs_3_.refs_4_.refs_5_ = bf16[9,2,256,256]{3,2,1,0:T(8,128)(2,1)} collective-permute-done((bf16[9,2,256,256]{3,2,1,0:T(8,128)(2,1)}, bf16[9,2,256,256]{3,2,1,0:T(8,128)(2,1)}, u32[]{:S(2)}, u32[]{:S(2)}) %collective-permute-start.1) | collective-permute-done | bytes 2359328 | tf_op jit(solution)/shard_map/ppermute | solution.py:343
  243.6 10.1 %attention1.1 = (bf16[2,256,256]{2,1,0:T(8,128)(2,1)}, bf16[4,2,256,256]{3,2,1,0:T(8,128)(2,1)}, bf16[4,2,256,256]{3,2,1,0:T(8,128)(2,1)}, bf16[4,2,256,256]{3,2,1,0:T(8,128)(2,1)}) custom-call(s32[1]{0:T(128)} %bitcast.z_ref, bf16[2,256,4096]{2,1,0:T(8,128)(2,1)} %refs_0_.11, bf16[2,256,4096]{2,1,0:T(8,128)(2,1)} %refs_1_.11, ...), custom_call_target="tpu_custom_call" | custom-call | flops 399999991808 | bytes 10485760 | tf_op jit(solution)/shard_map/attention1/pallas_call | solution.py:213
  256.5 10.6 %collective-permute-done.9.refs_1_.refs_3_.refs_4_.refs_5_ = bf16[4,2,256,256]{3,2,1,0:T(8,128)(2,1)} collective-permute-done((bf16[4,2,256,256]{3,2,1,0:T(8,128)(2,1)}, bf16[4,2,256,256]{3,2,1,0:T(8,128)(2,1)}, u32[]{:S(2)}, u32[]{:S(2)}) %collective-permute-start.9) | collective-permute-done | bytes 1048608 | tf_op jit(solution)/shard_map/ppermute | solution.py:343
  267.2 22.7 %collective-permute-done.11.refs_3_.refs_9_.refs_10_.refs_11_ = bf16[4,2,256,256]{3,2,1,0:T(8,128)(2,1)} collective-permute-done((bf16[4,2,256,256]{3,2,1,0:T(8,128)(2,1)}, bf16[4,2,256,256]{3,2,1,0:T(8,128)(2,1)}, u32[]{:S(2)}, u32[]{:S(2)}) %collective-permute-start.11) | collective-permute-done | bytes 1048608 | tf_op jit(solution)/shard_map/ppermute | solution.py:343
  289.9 9.1 %attention2.1 = (bf16[2,256,256]{2,1,0:T(8,128)(2,1)}, bf16[1,2,256,256]{3,2,1,0:T(8,128)(2,1)}, bf16[1,2,256,256]{3,2,1,0:T(8,128)(2,1)}, bf16[1,2,256,256]{3,2,1,0:T(8,128)(2,1)}) custom-call(s32[1]{0:T(128)} %bitcast.z_ref, bf16[2,256,4096]{2,1,0:T(8,128)(2,1)} %refs_0_.11, bf16[2,256,4096]{2,1,0:T(8,128)(2,1)} %refs_1_.11, ...), custom_call_target="tpu_custom_call" | custom-call | flops 399999991808 | bytes 10485760 | tf_op jit(solution)/shard_map/attention2/pallas_call | solution.py:213
  298.9 44.1 %collective-permute-start.4 = (bf16[4,2,256,256]{3,2,1,0:T(8,128)(2,1)}, bf16[4,2,256,256]{3,2,1,0:T(8,128)(2,1)S(1)}, u32[]{:S(2)}, u32[]{:S(2)}) collective-permute-start(bf16[4,2,256,256]{3,2,1,0:T(8,128)(2,1)} %get-tuple-element.35), channel_id=1, source_target_pairs={{0,4},{4,0},{8,12},{12,8},{1,5},{5,1},{9,13},{13,9},{2,6},{6,2},{1... | collective-permute-start | bytes 3145736 | tf_op jit(solution)/shard_map/ppermute | solution.py:343
  345.8 10.1 %collective-permute-done.5.refs_6_.refs_7_.refs_8_.refs_3_.refs_2_ = bf16[4,2,256,256]{3,2,1,0:T(8,128)(2,1)} collective-permute-done((bf16[4,2,256,256]{3,2,1,0:T(8,128)(2,1)}, bf16[4,2,256,256]{3,2,1,0:T(8,128)(2,1)}, u32[]{:S(2)}, u32[]{:S(2)}) %collective-permute-start.5) | collective-permute-done | bytes 1048608 | tf_op jit(solution)/shard_map/ppermute | solution.py:343
  360.3 6.7 %all-gather.11.cloned.1.call-done = bf16[48,2,256,256]{3,2,1,0:T(8,128)(2,1)} async-done(((bf16[6,2,256,256]{3,2,1,0:T(8,128)(2,1)}), bf16[48,2,256,256]{3,2,1,0:T(8,128)(2,1)}) %all-gather.11.cloned.1.call-update) | async-done | bytes 12582928 | tf_op jit(solution)/shard_map/all_gather | solution.py:347
  367.0 17.9 %project0.1.refs_12_.refs_8_ = f32[2,256,6144]{2,1,0:T(8,128)} custom-call(s32[1]{0:T(128)} %bitcast.z_ref, bf16[2,256,256]{2,1,0:T(8,128)(2,1)} %get-tuple-element.40.refs_0_, bf16[4,2,256,256]{3,2,1,0:T(8,128)(2,1)} %collective-permute-done.9.refs_1_.refs_3_.refs_4_.refs_5_, ...), custom_call_target="tpu_custom_call" | custom-call | flops 15000000512 | bytes 31457280 | tf_op jit(solution)/shard_map/project0/pallas_call | solution.py:316
  384.9 15.1 %collective-permute-done.4.refs_3_.refs_4_.refs_5_.refs_1_ = bf16[4,2,256,256]{3,2,1,0:T(8,128)(2,1)S(1)} collective-permute-done((bf16[4,2,256,256]{3,2,1,0:T(8,128)(2,1)}, bf16[4,2,256,256]{3,2,1,0:T(8,128)(2,1)S(1)}, u32[]{:S(2)}, u32[]{:S(2)}) %collective-permute-start.4) | collective-permute-done | bytes 1048608 | tf_op jit(solution)/shard_map/ppermute | solution.py:343
  401.9 9.0 %attention3.1 = (bf16[2,256,256]{2,1,0:T(8,128)(2,1)}, bf16[1,2,256,256]{3,2,1,0:T(8,128)(2,1)}, bf16[1,2,256,256]{3,2,1,0:T(8,128)(2,1)}, bf16[1,2,256,256]{3,2,1,0:T(8,128)(2,1)}) custom-call(s32[1]{0:T(128)} %bitcast.z_ref, bf16[2,256,4096]{2,1,0:T(8,128)(2,1)} %refs_0_.11, bf16[2,256,4096]{2,1,0:T(8,128)(2,1)} %refs_1_.11, ...), custom_call_target="tpu_custom_call" | custom-call | flops 399999991808 | bytes 10485760 | tf_op jit(solution)/shard_map/attention3/pallas_call | solution.py:213
  410.9 11.7 %collective-permute-start.12 = (bf16[1,2,256,256]{3,2,1,0:T(8,128)(2,1)}, bf16[1,2,256,256]{3,2,1,0:T(8,128)(2,1)S(1)}, u32[]{:S(2)}, u32[]{:S(2)}) collective-permute-start(bf16[1,2,256,256]{3,2,1,0:T(8,128)(2,1)} %get-tuple-element.46), channel_id=1, source_target_pairs={{0,4},{4,0},{8,12},{12,8},{1,5},{5,1},{9,13},{13,9},{2,6},{6,2},{1... | collective-permute-start | bytes 786440 | tf_op jit(solution)/shard_map/ppermute | solution.py:343
  423.9 19.7 %project1.1.refs_8_ = f32[2,256,6144]{2,1,0:T(8,128)} custom-call(s32[1]{0:T(128)} %bitcast.z_ref, bf16[2,256,256]{2,1,0:T(8,128)(2,1)} %get-tuple-element.56.refs_0_, bf16[4,2,256,256]{3,2,1,0:T(8,128)(2,1)} %copy-done.2, bf16[4,2,256,256]{3,2,1,0:T(8,128)(2,1)} %collective-permute-done.5.refs_6_.refs_7_.refs_8_.refs_3_.refs_2_, ...), custom_call_target="tpu_custom_call" | custom-call | flops 15000000512 | bytes 31457280 | tf_op jit(solution)/shard_map/project1/pallas_call | solution.py:316
  444.9 19.8 %project2.1.refs_8_ = f32[2,256,6144]{2,1,0:T(8,128)} custom-call(s32[1]{0:T(128)} %bitcast.z_ref, bf16[2,256,256]{2,1,0:T(8,128)(2,1)} %get-tuple-element.49.refs_0_, bf16[1,2,256,256]{3,2,1,0:T(8,128)(2,1)} %collective-permute-done.15.refs_1_, bf16[1,2,256,256]{3,2,1,0:T(8,128)(2,1)} %collective-permute-done.16.refs_2_, ...), custom_call_target="tpu_custom_call" | custom-call | flops 15000000512 | bytes 31457280 | tf_op jit(solution)/shard_map/project2/pallas_call | solution.py:316
  465.7 17.8 %project3.1 = bf16[2,256,6144]{2,1,0:T(8,128)(2,1)} custom-call(s32[1]{0:T(128)} %bitcast.z_ref, bf16[2,256,256]{2,1,0:T(8,128)(2,1)} %get-tuple-element.45.refs_0_, bf16[1,2,256,256]{3,2,1,0:T(8,128)(2,1)} %copy-done.5, bf16[1,2,256,256]{3,2,1,0:T(8,128)(2,1)} %copy-done.6, bf16[1,2,256,256]{3,2,1,0:T(8,128)(2,1)} %copy-done.7, ...), custom_call_target="tpu_custom_call" | custom-call | flops 15000000512 | bytes 31457280 | tf_op jit(solution)/shard_map/project3/pallas_call | solution.py:316
  (61 shorter events, 31.5 us)
Async XLA Ops:
  6.5 353.7 %all-gather.5.cloned.1.call-start = ((), (), s32[]{:S(2)}) async-start(), calls=%async_computation | async-start | bytes 14155776 | tf_op jit(solution)/shard_map/all_gather | solution.py:347
  12.6 347.6 %all-gather.7.cloned.1.call-start = ((), (), s32[]{:S(2)}) async-start(), calls=%async_computation.1 | async-start | bytes 14155776 | tf_op jit(solution)/shard_map/all_gather | solution.py:347
  12.7 107.9 %collective-permute-start = (bf16[9,2,256,256]{3,2,1,0:T(8,128)(2,1)}, bf16[9,2,256,256]{3,2,1,0:T(8,128)(2,1)S(1)}, u32[]{:S(2)}, u32[]{:S(2)}) collective-permute-start(bf16[9,2,256,256]{3,2,1,0:T(8,128)(2,1)} %get-tuple-element.31), channel_id=1, source_target_pairs={{0,8},{4,12},{8,0},{12,4},{1,9},{5,13},{9,1},{13,5},{2,10},{6,14},... | collective-permute-start | bytes 7077896 | tf_op jit(solution)/shard_map/ppermute | solution.py:343
  16.8 113.7 %collective-permute-start.7 = (bf16[9,2,256,256]{3,2,1,0:T(8,128)(2,1)}, bf16[9,2,256,256]{3,2,1,0:T(8,128)(2,1)S(1)}, u32[]{:S(2)}, u32[]{:S(2)}) collective-permute-start(bf16[9,2,256,256]{3,2,1,0:T(8,128)(2,1)} %get-tuple-element.38), channel_id=1, source_target_pairs={{0,4},{4,0},{8,12},{12,8},{1,5},{5,1},{9,13},{13,9},{2,6},{6,2},{1... | collective-permute-start | bytes 7077896 | tf_op jit(solution)/shard_map/ppermute | solution.py:343
  18.4 119.5 %collective-permute-start.8 = (bf16[3,2,256,256]{3,2,1,0:T(8,128)(2,1)}, bf16[3,2,256,256]{3,2,1,0:T(8,128)(2,1)S(1)}, u32[]{:S(2)}, u32[]{:S(2)}) collective-permute-start(bf16[3,2,256,256]{3,2,1,0:T(8,128)(2,1)} %get-tuple-element.39), channel_id=1, source_target_pairs={{0,12},{4,8},{8,4},{12,0},{1,13},{5,9},{9,5},{13,1},{2,14},{6,10},... | collective-permute-start | bytes 2359304 | tf_op jit(solution)/shard_map/ppermute | solution.py:343
  126.0 117.5 %collective-permute-start.1 = (bf16[9,2,256,256]{3,2,1,0:T(8,128)(2,1)}, bf16[9,2,256,256]{3,2,1,0:T(8,128)(2,1)}, u32[]{:S(2)}, u32[]{:S(2)}) collective-permute-start(bf16[9,2,256,256]{3,2,1,0:T(8,128)(2,1)} %get-tuple-element.32), channel_id=1, source_target_pairs={{0,4},{4,0},{8,12},{12,8},{1,5},{5,1},{9,13},{13,9},{2,6},{6,2},{1... | collective-permute-start | bytes 7077896 | tf_op jit(solution)/shard_map/ppermute | solution.py:343
  126.1 77.6 %collective-permute-start.2 = (bf16[3,2,256,256]{3,2,1,0:T(8,128)(2,1)}, bf16[3,2,256,256]{3,2,1,0:T(8,128)(2,1)}, u32[]{:S(2)}, u32[]{:S(2)}) collective-permute-start(bf16[3,2,256,256]{3,2,1,0:T(8,128)(2,1)} %get-tuple-element.33), channel_id=1, source_target_pairs={{0,8},{4,12},{8,0},{12,4},{1,9},{5,13},{9,1},{13,5},{2,10},{6,14},... | collective-permute-start | bytes 2359304 | tf_op jit(solution)/shard_map/ppermute | solution.py:343
  129.7 92.7 %collective-permute-start.3 = (bf16[3,2,256,256]{3,2,1,0:T(8,128)(2,1)}, bf16[3,2,256,256]{3,2,1,0:T(8,128)(2,1)}, u32[]{:S(2)}, u32[]{:S(2)}) collective-permute-start(bf16[3,2,256,256]{3,2,1,0:T(8,128)(2,1)} %get-tuple-element.34), channel_id=1, source_target_pairs={{0,12},{4,8},{8,4},{12,0},{1,13},{5,9},{9,5},{13,1},{2,14},{6,10},... | collective-permute-start | bytes 2359304 | tf_op jit(solution)/shard_map/ppermute | solution.py:343
  133.2 227.0 %all-gather.9.cloned.1.call-start = ((), (), s32[]{:S(2)}) async-start(), calls=%async_computation.2 | async-start | bytes 14155776 | tf_op jit(solution)/shard_map/all_gather | solution.py:347
  138.9 28.0 %copy-start.1 = (bf16[9,2,256,256]{3,2,1,0:T(8,128)(2,1)S(1)}, bf16[9,2,256,256]{3,2,1,0:T(8,128)(2,1)}, u32[]{:S(2)}) copy-start(bf16[9,2,256,256]{3,2,1,0:T(8,128)(2,1)} %copy-done) | copy-start | bytes 7077892
  149.1 118.1 %collective-permute-start.9 = (bf16[4,2,256,256]{3,2,1,0:T(8,128)(2,1)}, bf16[4,2,256,256]{3,2,1,0:T(8,128)(2,1)}, u32[]{:S(2)}, u32[]{:S(2)}) collective-permute-start(bf16[4,2,256,256]{3,2,1,0:T(8,128)(2,1)} %get-tuple-element.41), channel_id=1, source_target_pairs={{0,4},{4,0},{8,12},{12,8},{1,5},{5,1},{9,13},{13,9},{2,6},{6,2},{1... | collective-permute-start | bytes 3145736 | tf_op jit(solution)/shard_map/ppermute | solution.py:343
  165.5 101.7 %collective-permute-start.10 = (bf16[4,2,256,256]{3,2,1,0:T(8,128)(2,1)}, bf16[4,2,256,256]{3,2,1,0:T(8,128)(2,1)}, u32[]{:S(2)}, u32[]{:S(2)}) collective-permute-start(bf16[4,2,256,256]{3,2,1,0:T(8,128)(2,1)} %get-tuple-element.42), channel_id=1, source_target_pairs={{0,8},{4,12},{8,0},{12,4},{1,9},{5,13},{9,1},{13,5},{2,10},{6,14},... | collective-permute-start | bytes 3145736 | tf_op jit(solution)/shard_map/ppermute | solution.py:343
  168.2 198.8 %all-gather.11.cloned.1.call-start = ((), (), s32[]{:S(2)}) async-start(), calls=%async_computation.3 | async-start | bytes 14155776 | tf_op jit(solution)/shard_map/all_gather | solution.py:347
  203.8 86.1 %collective-permute-start.11 = (bf16[4,2,256,256]{3,2,1,0:T(8,128)(2,1)}, bf16[4,2,256,256]{3,2,1,0:T(8,128)(2,1)}, u32[]{:S(2)}, u32[]{:S(2)}) collective-permute-start(bf16[4,2,256,256]{3,2,1,0:T(8,128)(2,1)} %get-tuple-element.43), channel_id=1, source_target_pairs={{0,12},{4,8},{8,4},{12,0},{1,13},{5,9},{9,5},{13,1},{2,14},{6,10},... | collective-permute-start | bytes 3145736 | tf_op jit(solution)/shard_map/ppermute | solution.py:343
  253.7 102.2 %collective-permute-start.5 = (bf16[4,2,256,256]{3,2,1,0:T(8,128)(2,1)}, bf16[4,2,256,256]{3,2,1,0:T(8,128)(2,1)}, u32[]{:S(2)}, u32[]{:S(2)}) collective-permute-start(bf16[4,2,256,256]{3,2,1,0:T(8,128)(2,1)} %get-tuple-element.36), channel_id=1, source_target_pairs={{0,8},{4,12},{8,0},{12,4},{1,9},{5,13},{9,1},{13,5},{2,10},{6,14},... | collective-permute-start | bytes 3145736 | tf_op jit(solution)/shard_map/ppermute | solution.py:343
  289.9 53.1 %copy-start.8 = (bf16[4,2,256,256]{3,2,1,0:T(8,128)(2,1)S(1)}, bf16[4,2,256,256]{3,2,1,0:T(8,128)(2,1)}, u32[]{:S(2)}) copy-start(bf16[4,2,256,256]{3,2,1,0:T(8,128)(2,1)} %get-tuple-element.37) | copy-start | bytes 3145732
  298.9 101.0 %collective-permute-start.4 = (bf16[4,2,256,256]{3,2,1,0:T(8,128)(2,1)}, bf16[4,2,256,256]{3,2,1,0:T(8,128)(2,1)S(1)}, u32[]{:S(2)}, u32[]{:S(2)}) collective-permute-start(bf16[4,2,256,256]{3,2,1,0:T(8,128)(2,1)} %get-tuple-element.35), channel_id=1, source_target_pairs={{0,4},{4,0},{8,12},{12,8},{1,5},{5,1},{9,13},{13,9},{2,6},{6,2},{1... | collective-permute-start | bytes 3145736 | tf_op jit(solution)/shard_map/ppermute | solution.py:343
  343.0 56.9 %collective-permute-start.6 = (bf16[4,2,256,256]{3,2,1,0:T(8,128)(2,1)S(1)}, bf16[4,2,256,256]{3,2,1,0:T(8,128)(2,1)S(1)}, u32[]{:S(2)}, u32[]{:S(2)}) collective-permute-start(bf16[4,2,256,256]{3,2,1,0:T(8,128)(2,1)S(1)} %copy-done.8), channel_id=1, source_target_pairs={{0,12},{4,8},{8,4},{12,0},{1,13},{5,9},{9,5},{13,1},{2,14},{6,10},... | collective-permute-start | bytes 3145736 | tf_op jit(solution)/shard_map/ppermute | solution.py:343
  355.9 87.7 %collective-permute-start.15 = (bf16[1,2,256,256]{3,2,1,0:T(8,128)(2,1)}, bf16[1,2,256,256]{3,2,1,0:T(8,128)(2,1)}, u32[]{:S(2)}, u32[]{:S(2)}) collective-permute-start(bf16[1,2,256,256]{3,2,1,0:T(8,128)(2,1)} %get-tuple-element.53), channel_id=1, source_target_pairs={{0,4},{4,0},{8,12},{12,8},{1,5},{5,1},{9,13},{13,9},{2,6},{6,2},{1... | collective-permute-start | bytes 786440 | tf_op jit(solution)/shard_map/ppermute | solution.py:343
  355.9 89.1 %collective-permute-start.16 = (bf16[1,2,256,256]{3,2,1,0:T(8,128)(2,1)}, bf16[1,2,256,256]{3,2,1,0:T(8,128)(2,1)}, u32[]{:S(2)}, u32[]{:S(2)}) collective-permute-start(bf16[1,2,256,256]{3,2,1,0:T(8,128)(2,1)} %get-tuple-element.54), channel_id=1, source_target_pairs={{0,8},{4,12},{8,0},{12,4},{1,9},{5,13},{9,1},{13,5},{2,10},{6,14},... | collective-permute-start | bytes 786440 | tf_op jit(solution)/shard_map/ppermute | solution.py:343
  359.2 85.8 %collective-permute-start.17 = (bf16[1,2,256,256]{3,2,1,0:T(8,128)(2,1)}, bf16[1,2,256,256]{3,2,1,0:T(8,128)(2,1)}, u32[]{:S(2)}, u32[]{:S(2)}) collective-permute-start(bf16[1,2,256,256]{3,2,1,0:T(8,128)(2,1)} %get-tuple-element.55), channel_id=1, source_target_pairs={{0,12},{4,8},{8,4},{12,0},{1,13},{5,9},{9,5},{13,1},{2,14},{6,10},... | collective-permute-start | bytes 786440 | tf_op jit(solution)/shard_map/ppermute | solution.py:343
  410.9 53.9 %collective-permute-start.12 = (bf16[1,2,256,256]{3,2,1,0:T(8,128)(2,1)}, bf16[1,2,256,256]{3,2,1,0:T(8,128)(2,1)S(1)}, u32[]{:S(2)}, u32[]{:S(2)}) collective-permute-start(bf16[1,2,256,256]{3,2,1,0:T(8,128)(2,1)} %get-tuple-element.46), channel_id=1, source_target_pairs={{0,4},{4,0},{8,12},{12,8},{1,5},{5,1},{9,13},{13,9},{2,6},{6,2},{1... | collective-permute-start | bytes 786440 | tf_op jit(solution)/shard_map/ppermute | solution.py:343
  422.5 42.2 %collective-permute-start.13 = (bf16[1,2,256,256]{3,2,1,0:T(8,128)(2,1)}, bf16[1,2,256,256]{3,2,1,0:T(8,128)(2,1)S(1)}, u32[]{:S(2)}, u32[]{:S(2)}) collective-permute-start(bf16[1,2,256,256]{3,2,1,0:T(8,128)(2,1)} %get-tuple-element.47), channel_id=1, source_target_pairs={{0,8},{4,12},{8,0},{12,4},{1,9},{5,13},{9,1},{13,5},{2,10},{6,14},... | collective-permute-start | bytes 786440 | tf_op jit(solution)/shard_map/ppermute | solution.py:343
  443.6 21.2 %collective-permute-start.14 = (bf16[1,2,256,256]{3,2,1,0:T(8,128)(2,1)S(1)}, bf16[1,2,256,256]{3,2,1,0:T(8,128)(2,1)S(1)}, u32[]{:S(2)}, u32[]{:S(2)}) collective-permute-start(bf16[1,2,256,256]{3,2,1,0:T(8,128)(2,1)S(1)} %copy-done.10), channel_id=1, source_target_pairs={{0,12},{4,8},{8,4},{12,0},{1,13},{5,9},{9,5},{13,1},{2,14},{6,10},... | collective-permute-start | bytes 786440 | tf_op jit(solution)/shard_map/ppermute | solution.py:343
  (9 other events, 27.8 us)
Sparse Core Ops, SparseCore 0:
  12.8 74.8 all-gather.4
  133.3 85.6 all-gather.6
  220.9 72.1 all-gather.8
  294.8 72.1 all-gather.10

commit v3 on v2

--- a/solution.py
+++ b/solution.py
@@ -10,10 +10,9 @@
 SEQ = 4
 BF16 = jnp.bfloat16
 F32 = jnp.float32
-VMEM = 56 * 2**20
+MIB = 2**20
 ATTENTION_COST = 400
 PROJECT_COST = 15
-GROUPS = ([1], [2], [3])
 
 
 def attend(triple):
@@ -127,7 +126,7 @@
             ],
             out_specs=[message_spec(b) for b in blocks],
         ),
-        compiler_params=pltpu.CompilerParams(vmem_limit_bytes=VMEM),
+        compiler_params=pltpu.CompilerParams(vmem_limit_bytes=56 * MIB),
         cost_estimate=cost(5, 10 * 2**20),
         name="pack0",
     )(jnp.concatenate([z, grp]), *[queries, keys, values] * (SEQ - 1), out_weight)
@@ -161,7 +160,7 @@
             + [message_spec(3 + tiles)],
             out_specs=[message_spec(b) for b in blocks],
         ),
-        compiler_params=pltpu.CompilerParams(vmem_limit_bytes=VMEM),
+        compiler_params=pltpu.CompilerParams(vmem_limit_bytes=56 * MIB),
         cost_estimate=cost(5, 10 * 2**20),
         name="pack1",
     )(z, *[queries, keys, values] * (SEQ - 1), came)
@@ -231,7 +230,7 @@
                 pltpu.VMEM((SEQ * rows, 2 * HEAD_DIM), BF16),
             ],
         ),
-        compiler_params=pltpu.CompilerParams(vmem_limit_bytes=VMEM),
+        compiler_params=pltpu.CompilerParams(vmem_limit_bytes=56 * MIB),
         cost_estimate=cost(ATTENTION_COST, 10 * 2**20),
         name=f"attention{chunk}",
     )(
@@ -246,21 +245,27 @@
     return own, packs
 
 
-def project(z, attended, pieces, total, chunks, width, out_type):
-    images, rows, model = total.shape
+def project(z, attended, pieces, total, chunks, width, keep=None, kept=None):
+    last = kept is not None
+    images, rows = attended[0][0].shape[:2]
     tiles = pieces[0].shape[2]
     grouped = 2 if tiles % 2 == 0 else 1
     steps = tiles // grouped
     tile = grouped * width
+    model = SEQ * steps * tile
     halves = pieces[0].shape[3]
     many = len(chunks)
     attended = [o for chunk in attended for o in chunk]
-    n_w = SEQ * many
+    weight_chunks = [] if last else [*chunks] + [keep] * (keep is not None)
 
     def body(z_ref, *refs):
-        o_refs = refs[: many * SEQ]
-        w_refs = refs[many * SEQ : many * SEQ + n_w]
-        total_ref, out_ref, rows_all = refs[-3:]
+        refs = list(refs)
+        o_refs = [refs.pop(0) for _ in attended]
+        w_refs = [[refs.pop(0) for _ in range(SEQ)] for _ in weight_chunks]
+        kept_ref = refs.pop(0) if last else None
+        total_ref, out_ref = refs.pop(0), refs.pop(0)
+        keep_ref = refs.pop(0) if keep is not None else None
+        rows_all = refs.pop(0)
         at = pl.program_id(0)
 
         @pl.when(at == 0)
@@ -276,17 +281,27 @@
         def step(p):
             for g in range(grouped):
                 cols = slice(g * width, (g + 1) * width)
-                value = total_ref[:, :, cols].astype(F32).reshape(images * rows, width)
+                value = total_ref[at, :, :, cols] if last else total_ref[:, :, cols]
+                value = value.astype(F32).reshape(images * rows, width)
                 for i in range(many):
+                    w = kept_ref[at, :, g] if last else w_refs[i][p][:, 0, g, 0]
                     value += jnp.dot(
                         rows_all[i],
-                        w_refs[i * SEQ + p][:, 0, g, 0].reshape(SEQ * width, width),
+                        w.reshape(SEQ * width, width),
                         preferred_element_type=F32,
                     )
-                out_ref[:, :, cols] = value.astype(out_type).reshape(images, rows, width)
-
-        for p in range(SEQ):
-            pl.when(at // steps == p)(lambda p=p: step(p))
+                value = value.reshape(images, rows, width)
+                if keep is None:
+                    out_ref[:, :, cols] = value.astype(out_ref.dtype)
+                else:
+                    out_ref[at, :, :, cols] = value
+                    keep_ref[at, :, g] = w_refs[many][p][:, 0, g, 0]
+
+        if last:
+            step(0)
+        else:
+            for p in range(SEQ):
+                pl.when(at // steps == p)(lambda p=p: step(p))
 
     def column(at, z_ref):
         return (0, 0, jnp.bitwise_xor(z_ref[0], at // steps) * steps + at % steps)
@@ -307,28 +322,43 @@
     def attended_spec(array):
         if array.ndim == 3:
             return pl.BlockSpec((images, rows, width), lambda at, z_ref: (0, 0, 0))
-        last = array.shape[0] - 1
+        end = array.shape[0] - 1
         return pl.BlockSpec(
-            (1, images, rows, width), lambda at, z_ref: (last, 0, 0, 0)
+            (1, images, rows, width), lambda at, z_ref: (end, 0, 0, 0)
         )
 
     block = pl.BlockSpec((images, rows, tile), column)
-    return pl.pallas_call(
+    inside = pl.BlockSpec(memory_space=pltpu.VMEM)
+    sums = pltpu.VMEM((SEQ * steps, images, rows, tile), F32)
+    rows_kept = pltpu.VMEM((SEQ * steps, SEQ, grouped, rows, width), BF16)
+    whole = jax.ShapeDtypeStruct((images, rows, model), BF16 if last else F32)
+    operands = [
+        z,
+        *attended,
+        *[p for _ in weight_chunks for p in pieces],
+        *([kept] if last else []),
+        total,
+    ]
+    out = pl.pallas_call(
         body,
-        out_shape=jax.ShapeDtypeStruct((images, rows, model), out_type),
+        out_shape=[whole] if keep is None else [sums, rows_kept],
         grid_spec=pltpu.PrefetchScalarGridSpec(
             num_scalar_prefetch=1,
             grid=(SEQ * steps,),
             in_specs=[attended_spec(o) for o in attended]
-            + [weight_spec(chunk, p) for chunk in chunks for p in range(SEQ)]
-            + [block],
-            out_specs=block,
+            + [weight_spec(chunk, p) for chunk in weight_chunks for p in range(SEQ)]
+            + ([inside] if last else [])
+            + [inside if last else block],
+            out_specs=[block] if keep is None else [inside, inside],
             scratch_shapes=[pltpu.VMEM((many, images * rows, SEQ * width), BF16)],
         ),
-        compiler_params=pltpu.CompilerParams(vmem_limit_bytes=VMEM),
+        compiler_params=pltpu.CompilerParams(
+            vmem_limit_bytes=8 * MIB if last else 38 * MIB
+        ),
         cost_estimate=cost(PROJECT_COST, 30 * 2**20),
         name="project" + "".join(str(c) for c in chunks),
-    )(z, *attended, *[p for _ in chunks for p in pieces], total)
+    )(*operands)
+    return out if keep is not None else out[0]
 
 
 def local_line(queries, keys, values, residual, out_weight):
@@ -337,9 +367,9 @@
     z = lax.axis_index("seq").astype(jnp.int32).reshape(1)
     grp = lax.axis_index("grp").astype(jnp.int32).reshape(1)
 
-    def send(packs):
+    def send(packs, order=(2, 3, 1)):
         came = [None] * (SEQ - 1)
-        for m in (2, 3, 1):
+        for m in order:
             came[m - 1] = lax.ppermute(packs[m - 1], "seq", [(i, i ^ m) for i in range(SEQ)])
         return came
 
@@ -353,26 +383,27 @@
     received.append(send(pack_second(z, queries, keys, values, far, width)))
     pieces = [whole(half), whole(near[3:]), whole(far[3:]), whole(received[1][0][3:])]
 
-    def add(total, *chunks):
+    def add(total, *chunks, **kwargs):
         attended = [[owns[c], *received[c + 2]] for c in chunks]
-        kept = BF16 if chunks[-1] == CHUNKS - 1 else F32
-        return project(z, attended, pieces, total, chunks, width, kept)
+        return project(z, attended, pieces, total, chunks, width, **kwargs)
 
     owns = []
-    total = residual
     for c in range(CHUNKS):
         after = []
         if c == CHUNKS - 1:
-            total = add(total, 0)
+            total = add(residual, 0)
             after = [total]
         own, packs = attention(z, queries, keys, values, received[c], c, width, after)
         owns.append(own)
+        order = (2, 3, 1)
         if c == CHUNKS - 2:
             packs = tie(packs, received[c + 1][1])
-        received.append(send(packs))
-    for chunks in GROUPS:
-        total = add(total, *chunks)
-    return total
+            order = (1, 2, 3)
+        elif c == CHUNKS - 1:
+            packs = tie(packs, received[c + 1][0])
+        received.append(send(packs, order))
+    total, kept = add(total, *range(1, CHUNKS - 1), keep=CHUNKS - 1)
+    return add(total, CHUNKS - 1, kept=kept)
 
 
 def solution(mesh):

time: 491 us -> 472 us (0.961)
  waiting for transfers between devices: 246 us -> 221 us
  starting transfers between devices: 95.2 us -> 119 us
  Pallas kernels: 123 us -> 101 us
    ppermute x18, waiting for transfers between devices: 239 us -> 188 us  [send(): lax.ppermute(packs[m - 1], 'seq', [(i, i ^ m) for i in range(SEQ)])]
    all_gather x4, waiting for transfers between devices: 6.74 us -> 32.8 us  [whole(): full = lax.all_gather(piece, ('img', 'grp'), axis=0, tiled=True)]
    ppermute x18, starting transfers between devices: 94.9 us -> 119 us  [send(): lax.ppermute(packs[m - 1], 'seq', [(i, i ^ m) for i in range(SEQ)])]
    pallas_call x4 -> x3, Pallas kernels: 75.2 us -> 52.9 us  [project(): pl.pallas_call(body, out_shape=[whole] if keep is None else [sums, rows_k...]
  transfers between devices with their start and end apart: 22 -> 22, of which waited for: 10 -> 8; matrix products, arithmetic and copies ran while one was open for 1% -> 2% of each run, Pallas kernels for 20% -> 18%
where the time goes in v3:
time: 472 us; the launch traced here: 471 us
  waiting for transfers between devices  221 us (47%)
  starting transfers between devices  119 us (25%)
  Pallas kernels  101 us (21%)
  local copies, waits for them, and re-layouts  15.4 us (3%)
  between operations  13.3 us (3%)
    ppermute x18, waiting for transfers between devices, send(): lax.ppermute(packs[m - 1], 'seq', [(i, i ^ m) for i in range(SEQ)])  188 us
    ppermute x18, starting transfers between devices, send(): lax.ppermute(packs[m - 1], 'seq', [(i, i ^ m) for i in range(SEQ)])  119 us
    pallas_call x3, Pallas kernels, project(): pl.pallas_call(body, out_shape=[whole] if keep is None else [sums, rows_k...  52.9 us
    pallas_call x4, Pallas kernels, attention(): pl.pallas_call(body, out_shape=[jax.ShapeDtypeStruct((images, rows, width...  38.5 us
    all_gather x4, waiting for transfers between devices, whole(): full = lax.all_gather(piece, ('img', 'grp'), axis=0, tiled=True)  32.8 us
  transfers between devices with their start and end apart: 22, of which 8 were waited for; matrix products, arithmetic and copies ran while one was open for 2% of the time, Pallas kernels for 18%

profile of v3, /device:TPU:0, one launch (start us, length us, event | category | flops | bytes accessed | tf_op | source)
XLA Modules:
  0.0 470.9 jit_solution(15382251752699527211)
XLA Ops:
  7.2 5.5 %pack0.1 = (bf16[9,2,256,256]{3,2,1,0:T(8,128)(2,1)}, bf16[9,2,256,256]{3,2,1,0:T(8,128)(2,1)}, bf16[3,2,256,256]{3,2,1,0:T(8,128)(2,1)}, bf16[6,2,256,256]{3,2,1,0:T(8,128)(2,1)}) custom-call(s32[2]{0:T(128)} %pad_add_fusion.z_ref, bf16[2,256,4096]{2,1,0:T(8,128)(2,1)} %refs_0_.11, bf16[2,256,4096]{2,1,0:T(8,128)(2,1)} %refs_1_.11, ...), custom_call_target="tpu_custom_call" | custom-call | flops 5000000000 | bytes 10485760 | tf_op jit(solution)/shard_map/pack0/pallas_call | solution.py:113
  12.8 4.1 collective-permute-start
  18.5 102.2 %collective-permute-done.refs_9_.refs_6_.refs_7_.refs_8_ = bf16[9,2,256,256]{3,2,1,0:T(8,128)(2,1)S(1)} collective-permute-done((bf16[9,2,256,256]{3,2,1,0:T(8,128)(2,1)}, bf16[9,2,256,256]{3,2,1,0:T(8,128)(2,1)S(1)}, u32[]{:S(2)}, u32[]{:S(2)}) %collective-permute-start) | collective-permute-done | bytes 2359328 | tf_op jit(solution)/shard_map/ppermute | solution.py:373
  122.2 4.1 pack1.1
  126.4 3.1 collective-permute-start.3
  132.8 5.3 %collective-permute-done.8.refs_9_.refs_10_.refs_11_ = bf16[3,2,256,256]{3,2,1,0:T(8,128)(2,1)S(1)} collective-permute-done((bf16[3,2,256,256]{3,2,1,0:T(8,128)(2,1)}, bf16[3,2,256,256]{3,2,1,0:T(8,128)(2,1)S(1)}, u32[]{:S(2)}, u32[]{:S(2)}) %collective-permute-start.8) | collective-permute-done | bytes 786464 | tf_op jit(solution)/shard_map/ppermute | solution.py:373
  139.0 10.1 %attention0.1 = (bf16[2,256,256]{2,1,0:T(8,128)(2,1)}, bf16[4,2,256,256]{3,2,1,0:T(8,128)(2,1)}, bf16[4,2,256,256]{3,2,1,0:T(8,128)(2,1)}, bf16[4,2,256,256]{3,2,1,0:T(8,128)(2,1)}) custom-call(s32[1]{0:T(128)} %bitcast.z_ref, bf16[2,256,4096]{2,1,0:T(8,128)(2,1)} %refs_0_.11, bf16[2,256,4096]{2,1,0:T(8,128)(2,1)} %refs_1_.11, ...), custom_call_target="tpu_custom_call" | custom-call | flops 399999991808 | bytes 10485760 | tf_op jit(solution)/shard_map/attention0/pallas_call | solution.py:212
  149.1 49.8 %collective-permute-start.9 = (bf16[4,2,256,256]{3,2,1,0:T(8,128)(2,1)}, bf16[4,2,256,256]{3,2,1,0:T(8,128)(2,1)}, u32[]{:S(2)}, u32[]{:S(2)}) collective-permute-start(bf16[4,2,256,256]{3,2,1,0:T(8,128)(2,1)} %get-tuple-element.46), channel_id=1, source_target_pairs={{0,4},{4,0},{8,12},{12,8},{1,5},{5,1},{9,13},{13,9},{2,6},{6,2},{1... | collective-permute-start | bytes 3145736 | tf_op jit(solution)/shard_map/ppermute | solution.py:373
  207.0 36.7 %collective-permute-done.1.refs_3_.refs_4_.refs_5_ = bf16[9,2,256,256]{3,2,1,0:T(8,128)(2,1)} collective-permute-done((bf16[9,2,256,256]{3,2,1,0:T(8,128)(2,1)}, bf16[9,2,256,256]{3,2,1,0:T(8,128)(2,1)}, u32[]{:S(2)}, u32[]{:S(2)}) %collective-permute-start.1) | collective-permute-done | bytes 2359328 | tf_op jit(solution)/shard_map/ppermute | solution.py:373
  243.7 10.3 %attention1.1 = (bf16[2,256,256]{2,1,0:T(8,128)(2,1)}, bf16[4,2,256,256]{3,2,1,0:T(8,128)(2,1)}, bf16[4,2,256,256]{3,2,1,0:T(8,128)(2,1)}, bf16[4,2,256,256]{3,2,1,0:T(8,128)(2,1)}) custom-call(s32[1]{0:T(128)} %bitcast.z_ref, bf16[2,256,4096]{2,1,0:T(8,128)(2,1)} %refs_0_.11, bf16[2,256,4096]{2,1,0:T(8,128)(2,1)} %refs_1_.11, ...), custom_call_target="tpu_custom_call" | custom-call | flops 399999991808 | bytes 10485760 | tf_op jit(solution)/shard_map/attention1/pallas_call | solution.py:212
  254.1 2.9 slice.14
  257.1 10.2 %collective-permute-done.9.refs_1_.refs_3_.refs_4_.refs_5_ = bf16[4,2,256,256]{3,2,1,0:T(8,128)(2,1)} collective-permute-done((bf16[4,2,256,256]{3,2,1,0:T(8,128)(2,1)}, bf16[4,2,256,256]{3,2,1,0:T(8,128)(2,1)}, u32[]{:S(2)}, u32[]{:S(2)}) %collective-permute-start.9) | collective-permute-done | bytes 1048608 | tf_op jit(solution)/shard_map/ppermute | solution.py:373
  267.3 22.6 %collective-permute-done.11.refs_3_.refs_9_.refs_10_.refs_11_ = bf16[4,2,256,256]{3,2,1,0:T(8,128)(2,1)} collective-permute-done((bf16[4,2,256,256]{3,2,1,0:T(8,128)(2,1)}, bf16[4,2,256,256]{3,2,1,0:T(8,128)(2,1)}, u32[]{:S(2)}, u32[]{:S(2)}) %collective-permute-start.11) | collective-permute-done | bytes 1048608 | tf_op jit(solution)/shard_map/ppermute | solution.py:373
  290.0 9.1 %attention2.1 = (bf16[2,256,256]{2,1,0:T(8,128)(2,1)}, bf16[1,2,256,256]{3,2,1,0:T(8,128)(2,1)}, bf16[1,2,256,256]{3,2,1,0:T(8,128)(2,1)}, bf16[1,2,256,256]{3,2,1,0:T(8,128)(2,1)}) custom-call(s32[1]{0:T(128)} %bitcast.z_ref, bf16[2,256,4096]{2,1,0:T(8,128)(2,1)} %refs_0_.11, bf16[2,256,4096]{2,1,0:T(8,128)(2,1)} %refs_1_.11, ...), custom_call_target="tpu_custom_call" | custom-call | flops 399999991808 | bytes 10485760 | tf_op jit(solution)/shard_map/attention2/pallas_call | solution.py:212
  299.0 44.1 %collective-permute-start.4 = (bf16[4,2,256,256]{3,2,1,0:T(8,128)(2,1)}, bf16[4,2,256,256]{3,2,1,0:T(8,128)(2,1)S(1)}, u32[]{:S(2)}, u32[]{:S(2)}) collective-permute-start(bf16[4,2,256,256]{3,2,1,0:T(8,128)(2,1)} %get-tuple-element.40), channel_id=1, source_target_pairs={{0,4},{4,0},{8,12},{12,8},{1,5},{5,1},{9,13},{13,9},{2,6},{6,2},{1... | collective-permute-start | bytes 3145736 | tf_op jit(solution)/shard_map/ppermute | solution.py:373
  343.2 2.8 collective-permute-start.6
  345.9 10.0 %collective-permute-done.5.refs_6_.refs_7_.refs_8_.refs_3_.refs_2_ = bf16[4,2,256,256]{3,2,1,0:T(8,128)(2,1)} collective-permute-done((bf16[4,2,256,256]{3,2,1,0:T(8,128)(2,1)}, bf16[4,2,256,256]{3,2,1,0:T(8,128)(2,1)}, u32[]{:S(2)}, u32[]{:S(2)}) %collective-permute-start.5) | collective-permute-done | bytes 1048608 | tf_op jit(solution)/shard_map/ppermute | solution.py:373
  356.0 3.3 collective-permute-start.16
  360.4 32.8 %all-gather.11.cloned.1.call-done = bf16[48,2,256,256]{3,2,1,0:T(8,128)(2,1)} async-done(((bf16[6,2,256,256]{3,2,1,0:T(8,128)(2,1)}), bf16[48,2,256,256]{3,2,1,0:T(8,128)(2,1)}) %all-gather.11.cloned.1.call-update) | async-done | bytes 12582928 | tf_op jit(solution)/shard_map/all_gather | solution.py:377
  393.2 2.8 copy-done
  396.0 16.6 %project0.1.refs_12_.refs_20_ = f32[2,256,6144]{2,1,0:T(8,128)} custom-call(s32[1]{0:T(128)} %bitcast.z_ref, bf16[2,256,256]{2,1,0:T(8,128)(2,1)S(1)} %copy-done.1, bf16[4,2,256,256]{3,2,1,0:T(8,128)(2,1)} %collective-permute-done.9.refs_1_.refs_3_.refs_4_.refs_5_, bf16[4,2,256,256]{3,2,1,0:T(8,128)(2,1)} %collective-permute-done.10.refs_2_.refs_6_.refs_7_.refs_8_, ...), custom_call_target="tpu_custom_call" | custom-call | flops 15000000512 | bytes 31457280 | tf_op jit(solution)/shard_map/project0/pallas_call | solution.py:342
  414.5 9.0 %attention3.1 = (bf16[2,256,256]{2,1,0:T(8,128)(2,1)}, bf16[1,2,256,256]{3,2,1,0:T(8,128)(2,1)}, bf16[1,2,256,256]{3,2,1,0:T(8,128)(2,1)}, bf16[1,2,256,256]{3,2,1,0:T(8,128)(2,1)}) custom-call(s32[1]{0:T(128)} %bitcast.z_ref, bf16[2,256,4096]{2,1,0:T(8,128)(2,1)} %refs_0_.11, bf16[2,256,4096]{2,1,0:T(8,128)(2,1)} %refs_1_.11, ...), custom_call_target="tpu_custom_call" | custom-call | flops 399999991808 | bytes 10485760 | tf_op jit(solution)/shard_map/attention3/pallas_call | solution.py:212
  428.0 26.4 %project12.1 = (f32[12,2,256,512]{3,2,1,0:T(8,128)S(1)}, bf16[12,4,2,256,256]{4,3,2,1,0:T(8,128)(2,1)S(1)}) custom-call(s32[1]{0:T(128)} %bitcast.z_ref, bf16[2,256,256]{2,1,0:T(8,128)(2,1)} %get-tuple-element.61.refs_0_, bf16[4,2,256,256]{3,2,1,0:T(8,128)(2,1)} %copy-done.4, ...), custom_call_target="tpu_custom_call" | custom-call | flops 15000000512 | bytes 31457280 | tf_op jit(solution)/shard_map/project12/pallas_call | solution.py:342
  454.4 10.0 %project3.1 = bf16[2,256,6144]{2,1,0:T(8,128)(2,1)} custom-call(s32[1]{0:T(128)} %bitcast.z_ref, bf16[2,256,256]{2,1,0:T(8,128)(2,1)S(1)} %copy-done.2, bf16[1,2,256,256]{3,2,1,0:T(8,128)(2,1)S(1)} %collective-permute-done.13.refs_1_, bf16[1,2,256,256]{3,2,1,0:T(8,128)(2,1)S(1)} %collective-permute-done.14.refs_2_, ...), custom_call_target="tpu_custom_call" | custom-call | flops 15000000512 | bytes 31457280 | tf_op jit(solution)/shard_map/project3/pallas_call | solution.py:342
  (55 shorter events, 23.7 us)
Async XLA Ops:
  6.5 353.8 %all-gather.5.cloned.1.call-start = ((), (), s32[]{:S(2)}) async-start(), calls=%async_computation | async-start | bytes 14155776 | tf_op jit(solution)/shard_map/all_gather | solution.py:377
  12.8 347.6 %all-gather.9.cloned.1.call-start = ((), (), s32[]{:S(2)}) async-start(), calls=%async_computation.2 | async-start | bytes 14155776 | tf_op jit(solution)/shard_map/all_gather | solution.py:377
  12.8 107.9 %collective-permute-start = (bf16[9,2,256,256]{3,2,1,0:T(8,128)(2,1)}, bf16[9,2,256,256]{3,2,1,0:T(8,128)(2,1)S(1)}, u32[]{:S(2)}, u32[]{:S(2)}) collective-permute-start(bf16[9,2,256,256]{3,2,1,0:T(8,128)(2,1)} %get-tuple-element.36), channel_id=1, source_target_pairs={{0,8},{4,12},{8,0},{12,4},{1,9},{5,13},{9,1},{13,5},{2,10},{6,14},... | collective-permute-start | bytes 7077896 | tf_op jit(solution)/shard_map/ppermute | solution.py:373
  16.9 121.2 %collective-permute-start.7 = (bf16[9,2,256,256]{3,2,1,0:T(8,128)(2,1)}, bf16[9,2,256,256]{3,2,1,0:T(8,128)(2,1)}, u32[]{:S(2)}, u32[]{:S(2)}) collective-permute-start(bf16[9,2,256,256]{3,2,1,0:T(8,128)(2,1)} %get-tuple-element.43), channel_id=1, source_target_pairs={{0,4},{4,0},{8,12},{12,8},{1,5},{5,1},{9,13},{13,9},{2,6},{6,2},{1... | collective-permute-start | bytes 7077896 | tf_op jit(solution)/shard_map/ppermute | solution.py:373
  18.5 119.6 %collective-permute-start.8 = (bf16[3,2,256,256]{3,2,1,0:T(8,128)(2,1)}, bf16[3,2,256,256]{3,2,1,0:T(8,128)(2,1)S(1)}, u32[]{:S(2)}, u32[]{:S(2)}) collective-permute-start(bf16[3,2,256,256]{3,2,1,0:T(8,128)(2,1)} %get-tuple-element.44), channel_id=1, source_target_pairs={{0,12},{4,8},{8,4},{12,0},{1,13},{5,9},{9,5},{13,1},{2,14},{6,10},... | collective-permute-start | bytes 2359304 | tf_op jit(solution)/shard_map/ppermute | solution.py:373
  126.3 77.9 %collective-permute-start.2 = (bf16[3,2,256,256]{3,2,1,0:T(8,128)(2,1)}, bf16[3,2,256,256]{3,2,1,0:T(8,128)(2,1)}, u32[]{:S(2)}, u32[]{:S(2)}) collective-permute-start(bf16[3,2,256,256]{3,2,1,0:T(8,128)(2,1)} %get-tuple-element.38), channel_id=1, source_target_pairs={{0,8},{4,12},{8,0},{12,4},{1,9},{5,13},{9,1},{13,5},{2,10},{6,14},... | collective-permute-start | bytes 2359304 | tf_op jit(solution)/shard_map/ppermute | solution.py:373
  126.4 80.6 %collective-permute-start.3 = (bf16[3,2,256,256]{3,2,1,0:T(8,128)(2,1)}, bf16[3,2,256,256]{3,2,1,0:T(8,128)(2,1)}, u32[]{:S(2)}, u32[]{:S(2)}) collective-permute-start(bf16[3,2,256,256]{3,2,1,0:T(8,128)(2,1)} %get-tuple-element.39), channel_id=1, source_target_pairs={{0,12},{4,8},{8,4},{12,0},{1,13},{5,9},{9,5},{13,1},{2,14},{6,10},... | collective-permute-start | bytes 2359304 | tf_op jit(solution)/shard_map/ppermute | solution.py:373
  129.5 114.2 %collective-permute-start.1 = (bf16[9,2,256,256]{3,2,1,0:T(8,128)(2,1)}, bf16[9,2,256,256]{3,2,1,0:T(8,128)(2,1)}, u32[]{:S(2)}, u32[]{:S(2)}) collective-permute-start(bf16[9,2,256,256]{3,2,1,0:T(8,128)(2,1)} %get-tuple-element.37), channel_id=1, source_target_pairs={{0,4},{4,0},{8,12},{12,8},{1,5},{5,1},{9,13},{13,9},{2,6},{6,2},{1... | collective-permute-start | bytes 7077896 | tf_op jit(solution)/shard_map/ppermute | solution.py:373
  132.7 227.6 %all-gather.7.cloned.1.call-start = ((), (), s32[]{:S(2)}) async-start(), calls=%async_computation.1 | async-start | bytes 14155776 | tf_op jit(solution)/shard_map/all_gather | solution.py:377
  149.1 118.2 %collective-permute-start.9 = (bf16[4,2,256,256]{3,2,1,0:T(8,128)(2,1)}, bf16[4,2,256,256]{3,2,1,0:T(8,128)(2,1)}, u32[]{:S(2)}, u32[]{:S(2)}) collective-permute-start(bf16[4,2,256,256]{3,2,1,0:T(8,128)(2,1)} %get-tuple-element.46), channel_id=1, source_target_pairs={{0,4},{4,0},{8,12},{12,8},{1,5},{5,1},{9,13},{13,9},{2,6},{6,2},{1... | collective-permute-start | bytes 3145736 | tf_op jit(solution)/shard_map/ppermute | solution.py:373
  198.8 68.5 %collective-permute-start.10 = (bf16[4,2,256,256]{3,2,1,0:T(8,128)(2,1)}, bf16[4,2,256,256]{3,2,1,0:T(8,128)(2,1)}, u32[]{:S(2)}, u32[]{:S(2)}) collective-permute-start(bf16[4,2,256,256]{3,2,1,0:T(8,128)(2,1)} %get-tuple-element.47), channel_id=1, source_target_pairs={{0,8},{4,12},{8,0},{12,4},{1,9},{5,13},{9,1},{13,5},{2,10},{6,14},... | collective-permute-start | bytes 3145736 | tf_op jit(solution)/shard_map/ppermute | solution.py:373
  202.9 190.3 %all-gather.11.cloned.1.call-start = ((), (), s32[]{:S(2)}) async-start(), calls=%async_computation.3 | async-start | bytes 14155776 | tf_op jit(solution)/shard_map/all_gather | solution.py:377
  204.2 85.7 %collective-permute-start.11 = (bf16[4,2,256,256]{3,2,1,0:T(8,128)(2,1)}, bf16[4,2,256,256]{3,2,1,0:T(8,128)(2,1)}, u32[]{:S(2)}, u32[]{:S(2)}) collective-permute-start(bf16[4,2,256,256]{3,2,1,0:T(8,128)(2,1)} %get-tuple-element.48), channel_id=1, source_target_pairs={{0,12},{4,8},{8,4},{12,0},{1,13},{5,9},{9,5},{13,1},{2,14},{6,10},... | collective-permute-start | bytes 3145736 | tf_op jit(solution)/shard_map/ppermute | solution.py:373
  254.0 101.9 %collective-permute-start.5 = (bf16[4,2,256,256]{3,2,1,0:T(8,128)(2,1)}, bf16[4,2,256,256]{3,2,1,0:T(8,128)(2,1)}, u32[]{:S(2)}, u32[]{:S(2)}) collective-permute-start(bf16[4,2,256,256]{3,2,1,0:T(8,128)(2,1)} %get-tuple-element.41), channel_id=1, source_target_pairs={{0,8},{4,12},{8,0},{12,4},{1,9},{5,13},{9,1},{13,5},{2,10},{6,14},... | collective-permute-start | bytes 3145736 | tf_op jit(solution)/shard_map/ppermute | solution.py:373
  290.0 53.2 %copy-start.6 = (bf16[4,2,256,256]{3,2,1,0:T(8,128)(2,1)S(1)}, bf16[4,2,256,256]{3,2,1,0:T(8,128)(2,1)}, u32[]{:S(2)}) copy-start(bf16[4,2,256,256]{3,2,1,0:T(8,128)(2,1)} %get-tuple-element.42) | copy-start | bytes 3145732
  290.0 103.2 %copy-start.1 = (bf16[2,256,256]{2,1,0:T(8,128)(2,1)S(1)}, bf16[2,256,256]{2,1,0:T(8,128)(2,1)}, u32[]{:S(2)}) copy-start(bf16[2,256,256]{2,1,0:T(8,128)(2,1)} %get-tuple-element.45.refs_0_) | copy-start | bytes 786436
  299.0 113.5 %collective-permute-start.4 = (bf16[4,2,256,256]{3,2,1,0:T(8,128)(2,1)}, bf16[4,2,256,256]{3,2,1,0:T(8,128)(2,1)S(1)}, u32[]{:S(2)}, u32[]{:S(2)}) collective-permute-start(bf16[4,2,256,256]{3,2,1,0:T(8,128)(2,1)} %get-tuple-element.40), channel_id=1, source_target_pairs={{0,4},{4,0},{8,12},{12,8},{1,5},{5,1},{9,13},{13,9},{2,6},{6,2},{1... | collective-permute-start | bytes 3145736 | tf_op jit(solution)/shard_map/ppermute | solution.py:373
  343.2 69.4 %collective-permute-start.6 = (bf16[4,2,256,256]{3,2,1,0:T(8,128)(2,1)S(1)}, bf16[4,2,256,256]{3,2,1,0:T(8,128)(2,1)S(1)}, u32[]{:S(2)}, u32[]{:S(2)}) collective-permute-start(bf16[4,2,256,256]{3,2,1,0:T(8,128)(2,1)S(1)} %copy-done.6), channel_id=1, source_target_pairs={{0,12},{4,8},{8,4},{12,0},{1,13},{5,9},{9,5},{13,1},{2,14},{6,10},... | collective-permute-start | bytes 3145736 | tf_op jit(solution)/shard_map/ppermute | solution.py:373
  356.0 67.6 %collective-permute-start.12 = (bf16[1,2,256,256]{3,2,1,0:T(8,128)(2,1)}, bf16[1,2,256,256]{3,2,1,0:T(8,128)(2,1)}, u32[]{:S(2)}, u32[]{:S(2)}) collective-permute-start(bf16[1,2,256,256]{3,2,1,0:T(8,128)(2,1)} %get-tuple-element.57), channel_id=1, source_target_pairs={{0,4},{4,0},{8,12},{12,8},{1,5},{5,1},{9,13},{13,9},{2,6},{6,2},{1... | collective-permute-start | bytes 786440 | tf_op jit(solution)/shard_map/ppermute | solution.py:373
  356.0 72.0 %collective-permute-start.16 = (bf16[1,2,256,256]{3,2,1,0:T(8,128)(2,1)}, bf16[1,2,256,256]{3,2,1,0:T(8,128)(2,1)}, u32[]{:S(2)}, u32[]{:S(2)}) collective-permute-start(bf16[1,2,256,256]{3,2,1,0:T(8,128)(2,1)} %get-tuple-element.63), channel_id=1, source_target_pairs={{0,8},{4,12},{8,0},{12,4},{1,9},{5,13},{9,1},{13,5},{2,10},{6,14},... | collective-permute-start | bytes 786440 | tf_op jit(solution)/shard_map/ppermute | solution.py:373
  359.3 68.7 %collective-permute-start.17 = (bf16[1,2,256,256]{3,2,1,0:T(8,128)(2,1)}, bf16[1,2,256,256]{3,2,1,0:T(8,128)(2,1)}, u32[]{:S(2)}, u32[]{:S(2)}) collective-permute-start(bf16[1,2,256,256]{3,2,1,0:T(8,128)(2,1)} %get-tuple-element.64), channel_id=1, source_target_pairs={{0,12},{4,8},{8,4},{12,0},{1,13},{5,9},{9,5},{13,1},{2,14},{6,10},... | collective-permute-start | bytes 786440 | tf_op jit(solution)/shard_map/ppermute | solution.py:373
  423.6 30.8 %collective-permute-start.13 = (bf16[1,2,256,256]{3,2,1,0:T(8,128)(2,1)}, bf16[1,2,256,256]{3,2,1,0:T(8,128)(2,1)S(1)}, u32[]{:S(2)}, u32[]{:S(2)}) collective-permute-start(bf16[1,2,256,256]{3,2,1,0:T(8,128)(2,1)} %get-tuple-element.58), channel_id=1, source_target_pairs={{0,4},{4,0},{8,12},{12,8},{1,5},{5,1},{9,13},{13,9},{2,6},{6,2},{1... | collective-permute-start | bytes 786440 | tf_op jit(solution)/shard_map/ppermute | solution.py:373
  425.2 29.2 %collective-permute-start.14 = (bf16[1,2,256,256]{3,2,1,0:T(8,128)(2,1)}, bf16[1,2,256,256]{3,2,1,0:T(8,128)(2,1)S(1)}, u32[]{:S(2)}, u32[]{:S(2)}) collective-permute-start(bf16[1,2,256,256]{3,2,1,0:T(8,128)(2,1)} %get-tuple-element.59), channel_id=1, source_target_pairs={{0,8},{4,12},{8,0},{12,4},{1,9},{5,13},{9,1},{13,5},{2,10},{6,14},... | collective-permute-start | bytes 786440 | tf_op jit(solution)/shard_map/ppermute | solution.py:373
  427.5 26.9 %collective-permute-start.15 = (bf16[1,2,256,256]{3,2,1,0:T(8,128)(2,1)}, bf16[1,2,256,256]{3,2,1,0:T(8,128)(2,1)S(1)}, u32[]{:S(2)}, u32[]{:S(2)}) collective-permute-start(bf16[1,2,256,256]{3,2,1,0:T(8,128)(2,1)} %get-tuple-element.60), channel_id=1, source_target_pairs={{0,12},{4,8},{8,4},{12,0},{1,13},{5,9},{9,5},{13,1},{2,14},{6,10},... | collective-permute-start | bytes 786440 | tf_op jit(solution)/shard_map/ppermute | solution.py:373
  (6 other events, 33.6 us)
Sparse Core Ops, SparseCore 0:
  12.9 74.8 all-gather.4
  132.8 112.3 all-gather.8
  247.1 72.1 all-gather.6
  321.0 72.1 all-gather.10

commit v4 on v2

--- a/solution.py
+++ b/solution.py
@@ -10,10 +10,9 @@
 SEQ = 4
 BF16 = jnp.bfloat16
 F32 = jnp.float32
-VMEM = 56 * 2**20
-ATTENTION_COST = 400
+MIB = 2**20
+ATTENTION_COST = (400, 400, 400, 400)
 PROJECT_COST = 15
-GROUPS = ([1], [2], [3])
 
 
 def attend(triple):
@@ -127,7 +126,7 @@
             ],
             out_specs=[message_spec(b) for b in blocks],
         ),
-        compiler_params=pltpu.CompilerParams(vmem_limit_bytes=VMEM),
+        compiler_params=pltpu.CompilerParams(vmem_limit_bytes=56 * MIB),
         cost_estimate=cost(5, 10 * 2**20),
         name="pack0",
     )(jnp.concatenate([z, grp]), *[queries, keys, values] * (SEQ - 1), out_weight)
@@ -161,7 +160,7 @@
             + [message_spec(3 + tiles)],
             out_specs=[message_spec(b) for b in blocks],
         ),
-        compiler_params=pltpu.CompilerParams(vmem_limit_bytes=VMEM),
+        compiler_params=pltpu.CompilerParams(vmem_limit_bytes=56 * MIB),
         cost_estimate=cost(5, 10 * 2**20),
         name="pack1",
     )(z, *[queries, keys, values] * (SEQ - 1), came)
@@ -231,8 +230,8 @@
                 pltpu.VMEM((SEQ * rows, 2 * HEAD_DIM), BF16),
             ],
         ),
-        compiler_params=pltpu.CompilerParams(vmem_limit_bytes=VMEM),
-        cost_estimate=cost(ATTENTION_COST, 10 * 2**20),
+        compiler_params=pltpu.CompilerParams(vmem_limit_bytes=56 * MIB),
+        cost_estimate=cost(ATTENTION_COST[chunk], 10 * 2**20),
         name=f"attention{chunk}",
     )(
         z,
@@ -246,52 +245,51 @@
     return own, packs
 
 
-def project(z, attended, pieces, total, chunks, width, out_type):
-    images, rows, model = total.shape
-    tiles = pieces[0].shape[2]
+def attended_rows(z_ref, o_refs, rows_all, width):
+    for m, o_ref in enumerate(o_refs):
+        heads_of = jnp.bitwise_xor(z_ref[0], m)
+        cols = pl.ds(pl.multiple_of(heads_of * width, HEAD_DIM), width)
+        rows_all[:, cols] = o_ref[...].reshape(rows_all.shape[0], width)
+
+
+def attended_spec(array):
+    if array.ndim == 3:
+        return pl.BlockSpec(array.shape, lambda *_: (0, 0, 0))
+    end = array.shape[0] - 1
+    return pl.BlockSpec((1, *array.shape[1:]), lambda *_: (end, 0, 0, 0))
+
+
+def project_first(z, attended, pieces, residual, chunk, width):
+    images, rows, model = residual.shape
+    tiles, halves = pieces[0].shape[2:4]
     grouped = 2 if tiles % 2 == 0 else 1
     steps = tiles // grouped
     tile = grouped * width
-    halves = pieces[0].shape[3]
-    many = len(chunks)
-    attended = [o for chunk in attended for o in chunk]
-    n_w = SEQ * many
 
     def body(z_ref, *refs):
-        o_refs = refs[: many * SEQ]
-        w_refs = refs[many * SEQ : many * SEQ + n_w]
-        total_ref, out_ref, rows_all = refs[-3:]
+        o_refs, w_refs = refs[:SEQ], refs[SEQ : 2 * SEQ]
+        residual_ref, out_ref, rows_all = refs[2 * SEQ :]
         at = pl.program_id(0)
 
         @pl.when(at == 0)
         def _():
-            for i in range(many):
-                for m in range(SEQ):
-                    heads_of = jnp.bitwise_xor(z_ref[0], m)
-                    cols = pl.ds(pl.multiple_of(heads_of * width, HEAD_DIM), width)
-                    rows_all[i, :, cols] = o_refs[i * SEQ + m][...].reshape(
-                        images * rows, width
-                    )
-
-        def step(p):
+            attended_rows(z_ref, o_refs, rows_all, width)
+
+        def step(w_ref):
             for g in range(grouped):
                 cols = slice(g * width, (g + 1) * width)
-                value = total_ref[:, :, cols].astype(F32).reshape(images * rows, width)
-                for i in range(many):
-                    value += jnp.dot(
-                        rows_all[i],
-                        w_refs[i * SEQ + p][:, 0, g, 0].reshape(SEQ * width, width),
-                        preferred_element_type=F32,
-                    )
-                out_ref[:, :, cols] = value.astype(out_type).reshape(images, rows, width)
+                value = residual_ref[:, :, cols].astype(F32).reshape(images * rows, width)
+                value += jnp.dot(
+                    rows_all[...],
+                    w_ref[:, 0, g, 0].reshape(SEQ * width, width),
+                    preferred_element_type=F32,
+                )
+                out_ref[:, :, cols] = value.reshape(images, rows, width)
 
         for p in range(SEQ):
-            pl.when(at // steps == p)(lambda p=p: step(p))
-
-    def column(at, z_ref):
-        return (0, 0, jnp.bitwise_xor(z_ref[0], at // steps) * steps + at % steps)
-
-    def weight_spec(chunk, p):
+            pl.when(at // steps == p)(lambda p=p: step(w_refs[p]))
+
+    def weight_spec(p):
         return pl.BlockSpec(
             (SEQ, 1, grouped, 1, rows, width),
             lambda at, z_ref: (
@@ -304,31 +302,166 @@
             ),
         )
 
-    def attended_spec(array):
-        if array.ndim == 3:
-            return pl.BlockSpec((images, rows, width), lambda at, z_ref: (0, 0, 0))
-        last = array.shape[0] - 1
-        return pl.BlockSpec(
-            (1, images, rows, width), lambda at, z_ref: (last, 0, 0, 0)
-        )
-
-    block = pl.BlockSpec((images, rows, tile), column)
+    block = pl.BlockSpec(
+        (images, rows, tile),
+        lambda at, z_ref: (0, 0, jnp.bitwise_xor(z_ref[0], at // steps) * steps + at % steps),
+    )
     return pl.pallas_call(
         body,
-        out_shape=jax.ShapeDtypeStruct((images, rows, model), out_type),
+        out_shape=jax.ShapeDtypeStruct((images, rows, model), F32),
         grid_spec=pltpu.PrefetchScalarGridSpec(
             num_scalar_prefetch=1,
             grid=(SEQ * steps,),
             in_specs=[attended_spec(o) for o in attended]
-            + [weight_spec(chunk, p) for chunk in chunks for p in range(SEQ)]
+            + [weight_spec(p) for p in range(SEQ)]
             + [block],
             out_specs=block,
-            scratch_shapes=[pltpu.VMEM((many, images * rows, SEQ * width), BF16)],
-        ),
-        compiler_params=pltpu.CompilerParams(vmem_limit_bytes=VMEM),
+            scratch_shapes=[pltpu.VMEM((images * rows, SEQ * width), BF16)],
+        ),
+        compiler_params=pltpu.CompilerParams(vmem_limit_bytes=38 * MIB),
+        cost_estimate=cost(PROJECT_COST, 30 * 2**20),
+        name=f"project{chunk}",
+    )(z, *attended, *pieces, residual)
+
+
+def project_middle(z, attended, pieces, total, chunks, keep, width):
+    images, rows, model = total.shape
+    tiles, halves = pieces[0].shape[2:4]
+    grouped = 2 if tiles % 2 == 0 else 1
+    steps = tiles // grouped
+    tile = grouped * width
+    many = len(chunks)
+    count = SEQ * steps
+    block = (SEQ, grouped, rows, width)
+
+    def body(z_ref, *refs):
+        o_refs, w_refs = refs[: many * SEQ], refs[many * SEQ : (many + 1) * SEQ]
+        total_ref, sums, kept, weights, rows_all, sems = refs[(many + 1) * SEQ :]
+
+        def weight_copy(i, at):
+            chunk = (*chunks, keep)[i]
+            source = w_refs[at // steps].at[
+                :,
+                chunk // halves,
+                pl.ds(at % steps * grouped, grouped),
+                chunk % halves,
+            ]
+            target = kept.at[at] if i == many else weights.at[i, at]
+            return pltpu.make_async_copy(source, target, sems.at[i, at])
+
+        def total_copy(at):
+            start = (jnp.bitwise_xor(z_ref[0], at // steps) * steps + at % steps) * tile
+            cols = pl.ds(pl.multiple_of(start, tile), tile)
+            return pltpu.make_async_copy(
+                total_ref.at[:, :, cols], sums.at[at], sems.at[many + 1, at]
+            )
+
+        for at in range(count):
+            for i in range(many):
+                weight_copy(i, at).start()
+            total_copy(at).start()
+        for at in range(count):
+            weight_copy(many, at).start()
+        for i in range(many):
+            attended_rows(
+                z_ref, o_refs[i * SEQ : (i + 1) * SEQ], rows_all.at[i], width
+            )
+
+        @pl.loop(0, count)
+        def _(at):
+            for i in range(many):
+                pltpu.make_async_copy(weights.at[i, at], weights.at[i, at], sems.at[i, at]).wait()
+            total_copy(at).wait()
+            for g in range(grouped):
+                cols = slice(g * width, (g + 1) * width)
+                value = sums[at, :, :, cols].reshape(images * rows, width)
+                for i in range(many):
+                    value += jnp.dot(
+                        rows_all[i],
+                        weights[i, at, :, g].reshape(SEQ * width, width),
+                        preferred_element_type=F32,
+                    )
+                sums[at, :, :, cols] = value.reshape(images, rows, width)
+
+        for at in range(count):
+            weight_copy(many, at).wait()
+
+    flat = [o for chunk in attended for o in chunk]
+    anywhere = pl.BlockSpec(memory_space=pl.ANY)
+    inside = pl.BlockSpec(memory_space=pltpu.VMEM)
+    return pl.pallas_call(
+        body,
+        out_shape=[
+            pltpu.VMEM((count, images, rows, tile), F32),
+            pltpu.VMEM((count, *block), BF16),
+        ],
+        grid_spec=pltpu.PrefetchScalarGridSpec(
+            num_scalar_prefetch=1,
+            grid=(1,),
+            in_specs=[attended_spec(o) for o in flat] + [anywhere] * (SEQ + 1),
+            out_specs=[inside, inside],
+            scratch_shapes=[
+                pltpu.VMEM((many, count, *block), BF16),
+                pltpu.VMEM((many, images * rows, SEQ * width), BF16),
+                pltpu.SemaphoreType.DMA((many + 2, count)),
+            ],
+        ),
+        compiler_params=pltpu.CompilerParams(vmem_limit_bytes=36 * MIB),
         cost_estimate=cost(PROJECT_COST, 30 * 2**20),
         name="project" + "".join(str(c) for c in chunks),
-    )(z, *attended, *[p for _ in chunks for p in pieces], total)
+    )(z, *flat, *pieces, total)
+
+
+def project_last(z, attended, sums, kept, width):
+    count, images, rows, tile = sums.shape
+    grouped = kept.shape[2]
+    steps = count // SEQ
+
+    def body(z_ref, *refs):
+        o_refs, (sums, kept, out, rows_all, rounded, sems) = refs[:SEQ], refs[SEQ:]
+        attended_rows(z_ref, o_refs, rows_all, width)
+
+        def copy(at):
+            start = (jnp.bitwise_xor(z_ref[0], at // steps) * steps + at % steps) * tile
+            cols = pl.ds(pl.multiple_of(start, tile), tile)
+            return pltpu.make_async_copy(rounded.at[at], out.at[:, :, cols], sems.at[at])
+
+        @pl.loop(0, count)
+        def _(at):
+            for g in range(grouped):
+                cols = slice(g * width, (g + 1) * width)
+                value = sums[at, :, :, cols].reshape(images * rows, width)
+                value += jnp.dot(
+                    rows_all[...],
+                    kept[at, :, g].reshape(SEQ * width, width),
+                    preferred_element_type=F32,
+                )
+                rounded[at, :, :, cols] = value.astype(BF16).reshape(images, rows, width)
+            copy(at).start()
+
+        @pl.loop(0, count)
+        def _(at):
+            copy(at).wait()
+
+    inside = pl.BlockSpec(memory_space=pltpu.VMEM)
+    return pl.pallas_call(
+        body,
+        out_shape=jax.ShapeDtypeStruct((images, rows, count * tile), BF16),
+        grid_spec=pltpu.PrefetchScalarGridSpec(
+            num_scalar_prefetch=1,
+            grid=(1,),
+            in_specs=[attended_spec(o) for o in attended] + [inside] * 2,
+            out_specs=pl.BlockSpec(memory_space=pl.ANY),
+            scratch_shapes=[
+                pltpu.VMEM((images * rows, SEQ * width), BF16),
+                pltpu.VMEM((count, images, rows, tile), BF16),
+                pltpu.SemaphoreType.DMA((count,)),
+            ],
+        ),
+        compiler_params=pltpu.CompilerParams(vmem_limit_bytes=10 * MIB),
+        cost_estimate=cost(PROJECT_COST, 6 * 2**20),
+        name="projectlast",
+    )(z, *attended, sums, kept)
 
 
 def local_line(queries, keys, values, residual, out_weight):
@@ -337,9 +470,9 @@
     z = lax.axis_index("seq").astype(jnp.int32).reshape(1)
     grp = lax.axis_index("grp").astype(jnp.int32).reshape(1)
 
-    def send(packs):
+    def send(packs, order=(2, 3, 1)):
         came = [None] * (SEQ - 1)
-        for m in (2, 3, 1):
+        for m in order:
             came[m - 1] = lax.ppermute(packs[m - 1], "seq", [(i, i ^ m) for i in range(SEQ)])
         return came
 
@@ -353,26 +486,29 @@
     received.append(send(pack_second(z, queries, keys, values, far, width)))
     pieces = [whole(half), whole(near[3:]), whole(far[3:]), whole(received[1][0][3:])]
 
-    def add(total, *chunks):
-        attended = [[owns[c], *received[c + 2]] for c in chunks]
-        kept = BF16 if chunks[-1] == CHUNKS - 1 else F32
-        return project(z, attended, pieces, total, chunks, width, kept)
+    def back(chunk):
+        return [owns[chunk], *received[chunk + 2]]
 
     owns = []
-    total = residual
     for c in range(CHUNKS):
         after = []
         if c == CHUNKS - 1:
-            total = add(total, 0)
+            total = project_first(z, back(0), pieces, residual, 0, width)
             after = [total]
         own, packs = attention(z, queries, keys, values, received[c], c, width, after)
         owns.append(own)
+        order = (2, 3, 1)
         if c == CHUNKS - 2:
             packs = tie(packs, received[c + 1][1])
-        received.append(send(packs))
-    for chunks in GROUPS:
-        total = add(total, *chunks)
-    return total
+            order = (1, 2, 3)
+        elif c == CHUNKS - 1:
+            packs = tie(packs, received[c + 1][0])
+        received.append(send(packs, order))
+    middle = range(1, CHUNKS - 1)
+    sums, kept = project_middle(
+        z, [back(c) for c in middle], pieces, total, middle, CHUNKS - 1, width
+    )
+    return project_last(z, back(CHUNKS - 1), sums, kept, width)
 
 
 def solution(mesh):

time: 491 us -> 466 us (0.949)
  Pallas kernels: 123 us -> 93.1 us
  waiting for transfers between devices: 246 us -> 221 us
  starting transfers between devices: 95.2 us -> 119 us
    ppermute x18, waiting for transfers between devices: 239 us -> 188 us  [send(): lax.ppermute(packs[m - 1], 'seq', [(i, i ^ m) for i in range(SEQ)])]
    pallas_call x4 -> x3, Pallas kernels: 75.2 us -> 45.1 us  [the longest x1 18.9 us: project_middle(): pl.pallas_call(body, out_shape=[pltpu.VMEM((count, images, rows, tile), F...]
    all_gather x4, waiting for transfers between devices: 6.74 us -> 32.8 us  [whole(): full = lax.all_gather(piece, ('img', 'grp'), axis=0, tiled=True)]
    ppermute x18, starting transfers between devices: 94.9 us -> 119 us  [send(): lax.ppermute(packs[m - 1], 'seq', [(i, i ^ m) for i in range(SEQ)])]
  transfers between devices with their start and end apart: 22 -> 22, of which waited for: 10 -> 8; matrix products, arithmetic and copies ran while one was open for 1% -> 2% of each run, Pallas kernels for 20% -> 17%
where the time goes in v4:
time: 466 us; the launch traced here: 463 us
  waiting for transfers between devices  221 us (47%)
  starting transfers between devices  119 us (26%)
  Pallas kernels  93.1 us (20%)
  local copies, waits for them, and re-layouts  15.4 us (3%)
  between operations  13.3 us (3%)
    ppermute x18, waiting for transfers between devices, send(): lax.ppermute(packs[m - 1], 'seq', [(i, i ^ m) for i in range(SEQ)])  188 us
    ppermute x18, starting transfers between devices, send(): lax.ppermute(packs[m - 1], 'seq', [(i, i ^ m) for i in range(SEQ)])  119 us
    pallas_call x4, Pallas kernels, attention(): pl.pallas_call(body, out_shape=[jax.ShapeDtypeStruct((images, rows, width...  38.3 us
    all_gather x4, waiting for transfers between devices, whole(): full = lax.all_gather(piece, ('img', 'grp'), axis=0, tiled=True)  32.8 us
    pallas_call x1, Pallas kernels, project_middle(): pl.pallas_call(body, out_shape=[pltpu.VMEM((count, images, rows, tile), F...  18.9 us
    pallas_call x1, Pallas kernels, project_first(): pl.pallas_call(body, out_shape=jax.ShapeDtypeStruct((images, rows, model)...  16.6 us
    pallas_call x1, Pallas kernels, project_last(): pl.pallas_call(body, out_shape=jax.ShapeDtypeStruct((images, rows, count...  9.59 us
  transfers between devices with their start and end apart: 22, of which 8 were waited for; matrix products, arithmetic and copies ran while one was open for 2% of the time, Pallas kernels for 17%

profile of v4, /device:TPU:0, one launch (start us, length us, event | category | flops | bytes accessed | tf_op | source)
XLA Modules:
  0.0 463.1 jit_solution(1764483899253795170)
XLA Ops:
  7.2 5.5 %pack0.1 = (bf16[9,2,256,256]{3,2,1,0:T(8,128)(2,1)}, bf16[9,2,256,256]{3,2,1,0:T(8,128)(2,1)}, bf16[3,2,256,256]{3,2,1,0:T(8,128)(2,1)}, bf16[6,2,256,256]{3,2,1,0:T(8,128)(2,1)}) custom-call(s32[2]{0:T(128)} %pad_add_fusion.z_ref, bf16[2,256,4096]{2,1,0:T(8,128)(2,1)} %refs_0_.11, bf16[2,256,4096]{2,1,0:T(8,128)(2,1)} %refs_1_.11, ...), custom_call_target="tpu_custom_call" | custom-call | flops 5000000000 | bytes 10485760 | tf_op jit(solution)/shard_map/pack0/pallas_call | solution.py:113
  12.8 4.1 collective-permute-start
  18.5 102.2 %collective-permute-done.refs_9_.refs_6_.refs_7_.refs_8_ = bf16[9,2,256,256]{3,2,1,0:T(8,128)(2,1)S(1)} collective-permute-done((bf16[9,2,256,256]{3,2,1,0:T(8,128)(2,1)}, bf16[9,2,256,256]{3,2,1,0:T(8,128)(2,1)S(1)}, u32[]{:S(2)}, u32[]{:S(2)}) %collective-permute-start) | collective-permute-done | bytes 2359328 | tf_op jit(solution)/shard_map/ppermute | solution.py:476
  122.2 4.1 pack1.1
  126.4 3.1 collective-permute-start.3
  132.8 5.3 %collective-permute-done.8.refs_9_.refs_10_.refs_11_ = bf16[3,2,256,256]{3,2,1,0:T(8,128)(2,1)S(1)} collective-permute-done((bf16[3,2,256,256]{3,2,1,0:T(8,128)(2,1)}, bf16[3,2,256,256]{3,2,1,0:T(8,128)(2,1)S(1)}, u32[]{:S(2)}, u32[]{:S(2)}) %collective-permute-start.8) | collective-permute-done | bytes 786464 | tf_op jit(solution)/shard_map/ppermute | solution.py:476
  139.0 10.1 %attention0.1 = (bf16[2,256,256]{2,1,0:T(8,128)(2,1)}, bf16[4,2,256,256]{3,2,1,0:T(8,128)(2,1)}, bf16[4,2,256,256]{3,2,1,0:T(8,128)(2,1)}, bf16[4,2,256,256]{3,2,1,0:T(8,128)(2,1)}) custom-call(s32[1]{0:T(128)} %bitcast.z_ref, bf16[2,256,4096]{2,1,0:T(8,128)(2,1)} %refs_0_.11, bf16[2,256,4096]{2,1,0:T(8,128)(2,1)} %refs_1_.11, ...), custom_call_target="tpu_custom_call" | custom-call | flops 399999991808 | bytes 10485760 | tf_op jit(solution)/shard_map/attention0/pallas_call | solution.py:212
  149.1 49.8 %collective-permute-start.9 = (bf16[4,2,256,256]{3,2,1,0:T(8,128)(2,1)}, bf16[4,2,256,256]{3,2,1,0:T(8,128)(2,1)}, u32[]{:S(2)}, u32[]{:S(2)}) collective-permute-start(bf16[4,2,256,256]{3,2,1,0:T(8,128)(2,1)} %get-tuple-element.46), channel_id=1, source_target_pairs={{0,4},{4,0},{8,12},{12,8},{1,5},{5,1},{9,13},{13,9},{2,6},{6,2},{1... | collective-permute-start | bytes 3145736 | tf_op jit(solution)/shard_map/ppermute | solution.py:476
  207.0 36.7 %collective-permute-done.1.refs_3_.refs_4_.refs_5_ = bf16[9,2,256,256]{3,2,1,0:T(8,128)(2,1)} collective-permute-done((bf16[9,2,256,256]{3,2,1,0:T(8,128)(2,1)}, bf16[9,2,256,256]{3,2,1,0:T(8,128)(2,1)}, u32[]{:S(2)}, u32[]{:S(2)}) %collective-permute-start.1) | collective-permute-done | bytes 2359328 | tf_op jit(solution)/shard_map/ppermute | solution.py:476
  243.7 10.2 %attention1.1 = (bf16[2,256,256]{2,1,0:T(8,128)(2,1)}, bf16[4,2,256,256]{3,2,1,0:T(8,128)(2,1)}, bf16[4,2,256,256]{3,2,1,0:T(8,128)(2,1)}, bf16[4,2,256,256]{3,2,1,0:T(8,128)(2,1)}) custom-call(s32[1]{0:T(128)} %bitcast.z_ref, bf16[2,256,4096]{2,1,0:T(8,128)(2,1)} %refs_0_.11, bf16[2,256,4096]{2,1,0:T(8,128)(2,1)} %refs_1_.11, ...), custom_call_target="tpu_custom_call" | custom-call | flops 399999991808 | bytes 10485760 | tf_op jit(solution)/shard_map/attention1/pallas_call | solution.py:212
  253.9 2.9 slice.14
  256.9 10.4 %collective-permute-done.9.refs_1_.refs_3_.refs_4_.refs_5_ = bf16[4,2,256,256]{3,2,1,0:T(8,128)(2,1)} collective-permute-done((bf16[4,2,256,256]{3,2,1,0:T(8,128)(2,1)}, bf16[4,2,256,256]{3,2,1,0:T(8,128)(2,1)}, u32[]{:S(2)}, u32[]{:S(2)}) %collective-permute-start.9) | collective-permute-done | bytes 1048608 | tf_op jit(solution)/shard_map/ppermute | solution.py:476
  267.3 22.6 %collective-permute-done.11.refs_3_.refs_9_.refs_10_.refs_11_ = bf16[4,2,256,256]{3,2,1,0:T(8,128)(2,1)} collective-permute-done((bf16[4,2,256,256]{3,2,1,0:T(8,128)(2,1)}, bf16[4,2,256,256]{3,2,1,0:T(8,128)(2,1)}, u32[]{:S(2)}, u32[]{:S(2)}) %collective-permute-start.11) | collective-permute-done | bytes 1048608 | tf_op jit(solution)/shard_map/ppermute | solution.py:476
  290.0 9.1 %attention2.1 = (bf16[2,256,256]{2,1,0:T(8,128)(2,1)}, bf16[1,2,256,256]{3,2,1,0:T(8,128)(2,1)}, bf16[1,2,256,256]{3,2,1,0:T(8,128)(2,1)}, bf16[1,2,256,256]{3,2,1,0:T(8,128)(2,1)}) custom-call(s32[1]{0:T(128)} %bitcast.z_ref, bf16[2,256,4096]{2,1,0:T(8,128)(2,1)} %refs_0_.11, bf16[2,256,4096]{2,1,0:T(8,128)(2,1)} %refs_1_.11, ...), custom_call_target="tpu_custom_call" | custom-call | flops 399999991808 | bytes 10485760 | tf_op jit(solution)/shard_map/attention2/pallas_call | solution.py:212
  299.0 44.1 %collective-permute-start.4 = (bf16[4,2,256,256]{3,2,1,0:T(8,128)(2,1)}, bf16[4,2,256,256]{3,2,1,0:T(8,128)(2,1)S(1)}, u32[]{:S(2)}, u32[]{:S(2)}) collective-permute-start(bf16[4,2,256,256]{3,2,1,0:T(8,128)(2,1)} %get-tuple-element.40), channel_id=1, source_target_pairs={{0,4},{4,0},{8,12},{12,8},{1,5},{5,1},{9,13},{13,9},{2,6},{6,2},{1... | collective-permute-start | bytes 3145736 | tf_op jit(solution)/shard_map/ppermute | solution.py:476
  343.2 2.8 collective-permute-start.6
  345.9 10.0 %collective-permute-done.5.refs_6_.refs_7_.refs_8_.refs_3_.refs_2_ = bf16[4,2,256,256]{3,2,1,0:T(8,128)(2,1)} collective-permute-done((bf16[4,2,256,256]{3,2,1,0:T(8,128)(2,1)}, bf16[4,2,256,256]{3,2,1,0:T(8,128)(2,1)}, u32[]{:S(2)}, u32[]{:S(2)}) %collective-permute-start.5) | collective-permute-done | bytes 1048608 | tf_op jit(solution)/shard_map/ppermute | solution.py:476
  356.0 3.3 collective-permute-start.16
  360.4 32.8 %all-gather.11.cloned.1.call-done = bf16[48,2,256,256]{3,2,1,0:T(8,128)(2,1)} async-done(((bf16[6,2,256,256]{3,2,1,0:T(8,128)(2,1)}), bf16[48,2,256,256]{3,2,1,0:T(8,128)(2,1)}) %all-gather.11.cloned.1.call-update) | async-done | bytes 12582928 | tf_op jit(solution)/shard_map/all_gather | solution.py:480
  393.2 2.8 copy-done
  396.0 16.6 %project0.1.refs_12_ = f32[2,256,6144]{2,1,0:T(8,128)} custom-call(s32[1]{0:T(128)} %bitcast.z_ref, bf16[2,256,256]{2,1,0:T(8,128)(2,1)S(1)} %copy-done.1, bf16[4,2,256,256]{3,2,1,0:T(8,128)(2,1)} %collective-permute-done.9.refs_1_.refs_3_.refs_4_.refs_5_, bf16[4,2,256,256]{3,2,1,0:T(8,128)(2,1)} %collective-permute-done.10.refs_2_.refs_6_.refs_7_.refs_8_, ...), custom_call_target="tpu_custom_call" | custom-call | flops 15000000512 | bytes 31457280 | tf_op jit(solution)/shard_map/project0/pallas_call | solution.py:309
  414.5 9.0 %attention3.1 = (bf16[2,256,256]{2,1,0:T(8,128)(2,1)}, bf16[1,2,256,256]{3,2,1,0:T(8,128)(2,1)}, bf16[1,2,256,256]{3,2,1,0:T(8,128)(2,1)}, bf16[1,2,256,256]{3,2,1,0:T(8,128)(2,1)}) custom-call(s32[1]{0:T(128)} %bitcast.z_ref, bf16[2,256,4096]{2,1,0:T(8,128)(2,1)} %refs_0_.11, bf16[2,256,4096]{2,1,0:T(8,128)(2,1)} %refs_1_.11, ...), custom_call_target="tpu_custom_call" | custom-call | flops 399999991808 | bytes 10485760 | tf_op jit(solution)/shard_map/attention3/pallas_call | solution.py:212
  428.0 18.9 %project12.1 = (f32[12,2,256,512]{3,2,1,0:T(8,128)S(1)}, bf16[12,4,2,256,256]{4,3,2,1,0:T(8,128)(2,1)S(1)}) custom-call(s32[1]{0:T(128)} %bitcast.z_ref, bf16[2,256,256]{2,1,0:T(8,128)(2,1)} %get-tuple-element.61.refs_0_, bf16[4,2,256,256]{3,2,1,0:T(8,128)(2,1)} %copy-done.4, ...), custom_call_target="tpu_custom_call" | custom-call | flops 15000000512 | bytes 31457280 | tf_op jit(solution)/shard_map/project12/pallas_call | solution.py:392
  447.0 9.6 %projectlast.1 = bf16[2,256,6144]{2,1,0:T(8,128)(2,1)} custom-call(s32[1]{0:T(128)} %bitcast.z_ref, bf16[2,256,256]{2,1,0:T(8,128)(2,1)S(1)} %copy-done.2, bf16[1,2,256,256]{3,2,1,0:T(8,128)(2,1)S(1)} %collective-permute-done.13.refs_1_, bf16[1,2,256,256]{3,2,1,0:T(8,128)(2,1)S(1)} %collective-permute-done.14.refs_2_, ...), custom_call_target="tpu_custom_call" | custom-call | flops 15000000512 | bytes 6291456 | tf_op jit(solution)/shard_map/projectlast/pallas_call | solution.py:447
  (55 shorter events, 23.7 us)
Async XLA Ops:
  6.5 353.8 %all-gather.5.cloned.1.call-start = ((), (), s32[]{:S(2)}) async-start(), calls=%async_computation | async-start | bytes 14155776 | tf_op jit(solution)/shard_map/all_gather | solution.py:480
  12.8 347.6 %all-gather.9.cloned.1.call-start = ((), (), s32[]{:S(2)}) async-start(), calls=%async_computation.2 | async-start | bytes 14155776 | tf_op jit(solution)/shard_map/all_gather | solution.py:480
  12.8 107.9 %collective-permute-start = (bf16[9,2,256,256]{3,2,1,0:T(8,128)(2,1)}, bf16[9,2,256,256]{3,2,1,0:T(8,128)(2,1)S(1)}, u32[]{:S(2)}, u32[]{:S(2)}) collective-permute-start(bf16[9,2,256,256]{3,2,1,0:T(8,128)(2,1)} %get-tuple-element.36), channel_id=1, source_target_pairs={{0,8},{4,12},{8,0},{12,4},{1,9},{5,13},{9,1},{13,5},{2,10},{6,14},... | collective-permute-start | bytes 7077896 | tf_op jit(solution)/shard_map/ppermute | solution.py:476
  16.9 121.2 %collective-permute-start.7 = (bf16[9,2,256,256]{3,2,1,0:T(8,128)(2,1)}, bf16[9,2,256,256]{3,2,1,0:T(8,128)(2,1)}, u32[]{:S(2)}, u32[]{:S(2)}) collective-permute-start(bf16[9,2,256,256]{3,2,1,0:T(8,128)(2,1)} %get-tuple-element.43), channel_id=1, source_target_pairs={{0,4},{4,0},{8,12},{12,8},{1,5},{5,1},{9,13},{13,9},{2,6},{6,2},{1... | collective-permute-start | bytes 7077896 | tf_op jit(solution)/shard_map/ppermute | solution.py:476
  18.5 119.6 %collective-permute-start.8 = (bf16[3,2,256,256]{3,2,1,0:T(8,128)(2,1)}, bf16[3,2,256,256]{3,2,1,0:T(8,128)(2,1)S(1)}, u32[]{:S(2)}, u32[]{:S(2)}) collective-permute-start(bf16[3,2,256,256]{3,2,1,0:T(8,128)(2,1)} %get-tuple-element.44), channel_id=1, source_target_pairs={{0,12},{4,8},{8,4},{12,0},{1,13},{5,9},{9,5},{13,1},{2,14},{6,10},... | collective-permute-start | bytes 2359304 | tf_op jit(solution)/shard_map/ppermute | solution.py:476
  126.3 77.9 %collective-permute-start.2 = (bf16[3,2,256,256]{3,2,1,0:T(8,128)(2,1)}, bf16[3,2,256,256]{3,2,1,0:T(8,128)(2,1)}, u32[]{:S(2)}, u32[]{:S(2)}) collective-permute-start(bf16[3,2,256,256]{3,2,1,0:T(8,128)(2,1)} %get-tuple-element.38), channel_id=1, source_target_pairs={{0,8},{4,12},{8,0},{12,4},{1,9},{5,13},{9,1},{13,5},{2,10},{6,14},... | collective-permute-start | bytes 2359304 | tf_op jit(solution)/shard_map/ppermute | solution.py:476
  126.4 80.6 %collective-permute-start.3 = (bf16[3,2,256,256]{3,2,1,0:T(8,128)(2,1)}, bf16[3,2,256,256]{3,2,1,0:T(8,128)(2,1)}, u32[]{:S(2)}, u32[]{:S(2)}) collective-permute-start(bf16[3,2,256,256]{3,2,1,0:T(8,128)(2,1)} %get-tuple-element.39), channel_id=1, source_target_pairs={{0,12},{4,8},{8,4},{12,0},{1,13},{5,9},{9,5},{13,1},{2,14},{6,10},... | collective-permute-start | bytes 2359304 | tf_op jit(solution)/shard_map/ppermute | solution.py:476
  129.5 114.2 %collective-permute-start.1 = (bf16[9,2,256,256]{3,2,1,0:T(8,128)(2,1)}, bf16[9,2,256,256]{3,2,1,0:T(8,128)(2,1)}, u32[]{:S(2)}, u32[]{:S(2)}) collective-permute-start(bf16[9,2,256,256]{3,2,1,0:T(8,128)(2,1)} %get-tuple-element.37), channel_id=1, source_target_pairs={{0,4},{4,0},{8,12},{12,8},{1,5},{5,1},{9,13},{13,9},{2,6},{6,2},{1... | collective-permute-start | bytes 7077896 | tf_op jit(solution)/shard_map/ppermute | solution.py:476
  132.7 227.6 %all-gather.7.cloned.1.call-start = ((), (), s32[]{:S(2)}) async-start(), calls=%async_computation.1 | async-start | bytes 14155776 | tf_op jit(solution)/shard_map/all_gather | solution.py:480
  149.1 118.2 %collective-permute-start.9 = (bf16[4,2,256,256]{3,2,1,0:T(8,128)(2,1)}, bf16[4,2,256,256]{3,2,1,0:T(8,128)(2,1)}, u32[]{:S(2)}, u32[]{:S(2)}) collective-permute-start(bf16[4,2,256,256]{3,2,1,0:T(8,128)(2,1)} %get-tuple-element.46), channel_id=1, source_target_pairs={{0,4},{4,0},{8,12},{12,8},{1,5},{5,1},{9,13},{13,9},{2,6},{6,2},{1... | collective-permute-start | bytes 3145736 | tf_op jit(solution)/shard_map/ppermute | solution.py:476
  198.8 68.5 %collective-permute-start.10 = (bf16[4,2,256,256]{3,2,1,0:T(8,128)(2,1)}, bf16[4,2,256,256]{3,2,1,0:T(8,128)(2,1)}, u32[]{:S(2)}, u32[]{:S(2)}) collective-permute-start(bf16[4,2,256,256]{3,2,1,0:T(8,128)(2,1)} %get-tuple-element.47), channel_id=1, source_target_pairs={{0,8},{4,12},{8,0},{12,4},{1,9},{5,13},{9,1},{13,5},{2,10},{6,14},... | collective-permute-start | bytes 3145736 | tf_op jit(solution)/shard_map/ppermute | solution.py:476
  202.9 190.3 %all-gather.11.cloned.1.call-start = ((), (), s32[]{:S(2)}) async-start(), calls=%async_computation.3 | async-start | bytes 14155776 | tf_op jit(solution)/shard_map/all_gather | solution.py:480
  204.2 85.7 %collective-permute-start.11 = (bf16[4,2,256,256]{3,2,1,0:T(8,128)(2,1)}, bf16[4,2,256,256]{3,2,1,0:T(8,128)(2,1)}, u32[]{:S(2)}, u32[]{:S(2)}) collective-permute-start(bf16[4,2,256,256]{3,2,1,0:T(8,128)(2,1)} %get-tuple-element.48), channel_id=1, source_target_pairs={{0,12},{4,8},{8,4},{12,0},{1,13},{5,9},{9,5},{13,1},{2,14},{6,10},... | collective-permute-start | bytes 3145736 | tf_op jit(solution)/shard_map/ppermute | solution.py:476
  253.9 102.1 %collective-permute-start.5 = (bf16[4,2,256,256]{3,2,1,0:T(8,128)(2,1)}, bf16[4,2,256,256]{3,2,1,0:T(8,128)(2,1)}, u32[]{:S(2)}, u32[]{:S(2)}) collective-permute-start(bf16[4,2,256,256]{3,2,1,0:T(8,128)(2,1)} %get-tuple-element.41), channel_id=1, source_target_pairs={{0,8},{4,12},{8,0},{12,4},{1,9},{5,13},{9,1},{13,5},{2,10},{6,14},... | collective-permute-start | bytes 3145736 | tf_op jit(solution)/shard_map/ppermute | solution.py:476
  290.0 53.2 %copy-start.6 = (bf16[4,2,256,256]{3,2,1,0:T(8,128)(2,1)S(1)}, bf16[4,2,256,256]{3,2,1,0:T(8,128)(2,1)}, u32[]{:S(2)}) copy-start(bf16[4,2,256,256]{3,2,1,0:T(8,128)(2,1)} %get-tuple-element.42) | copy-start | bytes 3145732
  290.0 103.2 %copy-start.1 = (bf16[2,256,256]{2,1,0:T(8,128)(2,1)S(1)}, bf16[2,256,256]{2,1,0:T(8,128)(2,1)}, u32[]{:S(2)}) copy-start(bf16[2,256,256]{2,1,0:T(8,128)(2,1)} %get-tuple-element.45.refs_0_) | copy-start | bytes 786436
  299.0 113.5 %collective-permute-start.4 = (bf16[4,2,256,256]{3,2,1,0:T(8,128)(2,1)}, bf16[4,2,256,256]{3,2,1,0:T(8,128)(2,1)S(1)}, u32[]{:S(2)}, u32[]{:S(2)}) collective-permute-start(bf16[4,2,256,256]{3,2,1,0:T(8,128)(2,1)} %get-tuple-element.40), channel_id=1, source_target_pairs={{0,4},{4,0},{8,12},{12,8},{1,5},{5,1},{9,13},{13,9},{2,6},{6,2},{1... | collective-permute-start | bytes 3145736 | tf_op jit(solution)/shard_map/ppermute | solution.py:476
  343.2 69.4 %collective-permute-start.6 = (bf16[4,2,256,256]{3,2,1,0:T(8,128)(2,1)S(1)}, bf16[4,2,256,256]{3,2,1,0:T(8,128)(2,1)S(1)}, u32[]{:S(2)}, u32[]{:S(2)}) collective-permute-start(bf16[4,2,256,256]{3,2,1,0:T(8,128)(2,1)S(1)} %copy-done.6), channel_id=1, source_target_pairs={{0,12},{4,8},{8,4},{12,0},{1,13},{5,9},{9,5},{13,1},{2,14},{6,10},... | collective-permute-start | bytes 3145736 | tf_op jit(solution)/shard_map/ppermute | solution.py:476
  356.0 67.6 %collective-permute-start.12 = (bf16[1,2,256,256]{3,2,1,0:T(8,128)(2,1)}, bf16[1,2,256,256]{3,2,1,0:T(8,128)(2,1)}, u32[]{:S(2)}, u32[]{:S(2)}) collective-permute-start(bf16[1,2,256,256]{3,2,1,0:T(8,128)(2,1)} %get-tuple-element.57), channel_id=1, source_target_pairs={{0,4},{4,0},{8,12},{12,8},{1,5},{5,1},{9,13},{13,9},{2,6},{6,2},{1... | collective-permute-start | bytes 786440 | tf_op jit(solution)/shard_map/ppermute | solution.py:476
  356.0 72.0 %collective-permute-start.16 = (bf16[1,2,256,256]{3,2,1,0:T(8,128)(2,1)}, bf16[1,2,256,256]{3,2,1,0:T(8,128)(2,1)}, u32[]{:S(2)}, u32[]{:S(2)}) collective-permute-start(bf16[1,2,256,256]{3,2,1,0:T(8,128)(2,1)} %get-tuple-element.63), channel_id=1, source_target_pairs={{0,8},{4,12},{8,0},{12,4},{1,9},{5,13},{9,1},{13,5},{2,10},{6,14},... | collective-permute-start | bytes 786440 | tf_op jit(solution)/shard_map/ppermute | solution.py:476
  359.3 68.7 %collective-permute-start.17 = (bf16[1,2,256,256]{3,2,1,0:T(8,128)(2,1)}, bf16[1,2,256,256]{3,2,1,0:T(8,128)(2,1)}, u32[]{:S(2)}, u32[]{:S(2)}) collective-permute-start(bf16[1,2,256,256]{3,2,1,0:T(8,128)(2,1)} %get-tuple-element.64), channel_id=1, source_target_pairs={{0,12},{4,8},{8,4},{12,0},{1,13},{5,9},{9,5},{13,1},{2,14},{6,10},... | collective-permute-start | bytes 786440 | tf_op jit(solution)/shard_map/ppermute | solution.py:476
  423.6 23.4 %collective-permute-start.13 = (bf16[1,2,256,256]{3,2,1,0:T(8,128)(2,1)}, bf16[1,2,256,256]{3,2,1,0:T(8,128)(2,1)S(1)}, u32[]{:S(2)}, u32[]{:S(2)}) collective-permute-start(bf16[1,2,256,256]{3,2,1,0:T(8,128)(2,1)} %get-tuple-element.58), channel_id=1, source_target_pairs={{0,4},{4,0},{8,12},{12,8},{1,5},{5,1},{9,13},{13,9},{2,6},{6,2},{1... | collective-permute-start | bytes 786440 | tf_op jit(solution)/shard_map/ppermute | solution.py:476
  425.2 21.8 %collective-permute-start.14 = (bf16[1,2,256,256]{3,2,1,0:T(8,128)(2,1)}, bf16[1,2,256,256]{3,2,1,0:T(8,128)(2,1)S(1)}, u32[]{:S(2)}, u32[]{:S(2)}) collective-permute-start(bf16[1,2,256,256]{3,2,1,0:T(8,128)(2,1)} %get-tuple-element.59), channel_id=1, source_target_pairs={{0,8},{4,12},{8,0},{12,4},{1,9},{5,13},{9,1},{13,5},{2,10},{6,14},... | collective-permute-start | bytes 786440 | tf_op jit(solution)/shard_map/ppermute | solution.py:476
  427.5 19.5 %collective-permute-start.15 = (bf16[1,2,256,256]{3,2,1,0:T(8,128)(2,1)}, bf16[1,2,256,256]{3,2,1,0:T(8,128)(2,1)S(1)}, u32[]{:S(2)}, u32[]{:S(2)}) collective-permute-start(bf16[1,2,256,256]{3,2,1,0:T(8,128)(2,1)} %get-tuple-element.60), channel_id=1, source_target_pairs={{0,12},{4,8},{8,4},{12,0},{1,13},{5,9},{9,5},{13,1},{2,14},{6,10},... | collective-permute-start | bytes 786440 | tf_op jit(solution)/shard_map/ppermute | solution.py:476
  (6 other events, 26.1 us)
Sparse Core Ops, SparseCore 0:
  12.9 74.8 all-gather.4
  132.8 112.3 all-gather.8
  247.1 72.1 all-gather.6
  321.0 72.1 all-gather.10

commit v5 on v4

--- a/solution.py
+++ b/solution.py
@@ -80,7 +80,7 @@
 def head_columns(rows, width, per_device, xor, at):
     return pl.BlockSpec(
         (1, rows, width),
-        lambda i, h, z_ref: (
+        lambda i, h, z_ref, *_: (
             i,
             0,
             jnp.bitwise_xor(z_ref[0], xor) * per_device + at + h,
@@ -92,7 +92,7 @@
     images, rows, columns = queries.shape
     tiles = out_weight.shape[1] // width
 
-    def body(z_ref, *refs):
+    def body(z_ref, grp_ref, *refs):
         ins, w, outs, half = refs[:9], refs[9], refs[10:13], refs[13]
         for m in range(SEQ - 1):
             for t in range(3):
@@ -107,21 +107,21 @@
         return jax.ShapeDtypeStruct((blocks, images, rows, width), BF16)
 
     def message_spec(blocks):
-        return pl.BlockSpec((blocks, 1, rows, width), lambda i, h, z_ref: (0, i, 0, 0))
+        return pl.BlockSpec((blocks, 1, rows, width), lambda i, h, *_: (0, i, 0, 0))
 
     blocks = (3 + tiles, 3 + tiles, 3, tiles)
     *packs, half = pl.pallas_call(
         body,
         out_shape=[message(b) for b in blocks],
         grid_spec=pltpu.PrefetchScalarGridSpec(
-            num_scalar_prefetch=1,
+            num_scalar_prefetch=2,
             grid=(images, 1),
             in_specs=[
                 head_columns(rows, width, CHUNKS, m, 0) for m in range(1, SEQ) for _ in range(3)
             ]
             + [
                 pl.BlockSpec(
-                    (rows, tiles * width), lambda i, h, z_ref: (z_ref[1] * images + i, 0)
+                    (rows, tiles * width), lambda i, h, z_ref, grp_ref: (grp_ref[0] * images + i, 0)
                 )
             ],
             out_specs=[message_spec(b) for b in blocks],
@@ -129,7 +129,7 @@
         compiler_params=pltpu.CompilerParams(vmem_limit_bytes=56 * MIB),
         cost_estimate=cost(5, 10 * 2**20),
         name="pack0",
-    )(jnp.concatenate([z, grp]), *[queries, keys, values] * (SEQ - 1), out_weight)
+    )(z, grp, *[queries, keys, values] * (SEQ - 1), out_weight)
     return packs, half
 
 
@@ -426,7 +426,7 @@
             cols = pl.ds(pl.multiple_of(start, tile), tile)
             return pltpu.make_async_copy(rounded.at[at], out.at[:, :, cols], sems.at[at])
 
-        @pl.loop(0, count)
+        @pl.loop(0, count, unroll=count)
         def _(at):
             for g in range(grouped):
                 cols = slice(g * width, (g + 1) * width)

time: 466 us -> 463 us (level)
  no operation moved by 1% of the time
where the time goes in v5:
time: 463 us; the launch traced here: 460 us
  waiting for transfers between devices  221 us (48%)
  starting transfers between devices  119 us (26%)
  Pallas kernels  90.8 us (20%)
  local copies, waits for them, and re-layouts  15.4 us (3%)
  between operations  13.3 us (3%)
    ppermute x18, waiting for transfers between devices, send(): lax.ppermute(packs[m - 1], 'seq', [(i, i ^ m) for i in range(SEQ)])  188 us
    ppermute x18, starting transfers between devices, send(): lax.ppermute(packs[m - 1], 'seq', [(i, i ^ m) for i in range(SEQ)])  119 us
    pallas_call x4, Pallas kernels, attention(): pl.pallas_call(body, out_shape=[jax.ShapeDtypeStruct((images, rows, width...  38.3 us
    all_gather x4, waiting for transfers between devices, whole(): full = lax.all_gather(piece, ('img', 'grp'), axis=0, tiled=True)  32.8 us
    pallas_call x1, Pallas kernels, project_middle(): pl.pallas_call(body, out_shape=[pltpu.VMEM((count, images, rows, tile), F...  19.1 us
    pallas_call x1, Pallas kernels, project_first(): pl.pallas_call(body, out_shape=jax.ShapeDtypeStruct((images, rows, model)...  16.6 us
  transfers between devices with their start and end apart: 22, of which 8 were waited for; matrix products, arithmetic and copies ran while one was open for 2% of the time, Pallas kernels for 17%

profile of v5, /device:TPU:0, one launch (start us, length us, event | category | flops | bytes accessed | tf_op | source)
XLA Modules:
  0.0 460.1 jit_solution(2476815309571918612)
XLA Ops:
  6.5 4.9 %pack0.1 = (bf16[9,2,256,256]{3,2,1,0:T(8,128)(2,1)}, bf16[9,2,256,256]{3,2,1,0:T(8,128)(2,1)}, bf16[3,2,256,256]{3,2,1,0:T(8,128)(2,1)}, bf16[6,2,256,256]{3,2,1,0:T(8,128)(2,1)}) custom-call(s32[1]{0:T(128)} %bitcast.z_ref, s32[1]{0:T(128)} %bitcast.1.grp_ref, bf16[2,256,4096]{2,1,0:T(8,128)(2,1)} %refs_0_.11, bf16[2,256,4096]{2,1,0:T(8,128)(2,1)} %refs_1_.11, ...), custom_call_target="tpu_custom_call" | custom-call | flops 5000000000 | bytes 10485760 | tf_op jit(solution)/shard_map/pack0/pallas_call | solution.py:113
  11.5 4.1 collective-permute-start
  17.2 102.2 %collective-permute-done.refs_9_.refs_6_.refs_7_.refs_8_ = bf16[9,2,256,256]{3,2,1,0:T(8,128)(2,1)S(1)} collective-permute-done((bf16[9,2,256,256]{3,2,1,0:T(8,128)(2,1)}, bf16[9,2,256,256]{3,2,1,0:T(8,128)(2,1)S(1)}, u32[]{:S(2)}, u32[]{:S(2)}) %collective-permute-start) | collective-permute-done | bytes 2359328 | tf_op jit(solution)/shard_map/ppermute | solution.py:476
  120.9 4.1 pack1.1
  125.1 3.1 collective-permute-start.3
  131.5 5.3 %collective-permute-done.8.refs_9_.refs_10_.refs_11_ = bf16[3,2,256,256]{3,2,1,0:T(8,128)(2,1)S(1)} collective-permute-done((bf16[3,2,256,256]{3,2,1,0:T(8,128)(2,1)}, bf16[3,2,256,256]{3,2,1,0:T(8,128)(2,1)S(1)}, u32[]{:S(2)}, u32[]{:S(2)}) %collective-permute-start.8) | collective-permute-done | bytes 786464 | tf_op jit(solution)/shard_map/ppermute | solution.py:476
  137.6 10.1 %attention0.1 = (bf16[2,256,256]{2,1,0:T(8,128)(2,1)}, bf16[4,2,256,256]{3,2,1,0:T(8,128)(2,1)}, bf16[4,2,256,256]{3,2,1,0:T(8,128)(2,1)}, bf16[4,2,256,256]{3,2,1,0:T(8,128)(2,1)}) custom-call(s32[1]{0:T(128)} %bitcast.z_ref, bf16[2,256,4096]{2,1,0:T(8,128)(2,1)} %refs_0_.11, bf16[2,256,4096]{2,1,0:T(8,128)(2,1)} %refs_1_.11, ...), custom_call_target="tpu_custom_call" | custom-call | flops 399999991808 | bytes 10485760 | tf_op jit(solution)/shard_map/attention0/pallas_call | solution.py:212
  147.8 49.7 %collective-permute-start.9 = (bf16[4,2,256,256]{3,2,1,0:T(8,128)(2,1)}, bf16[4,2,256,256]{3,2,1,0:T(8,128)(2,1)}, u32[]{:S(2)}, u32[]{:S(2)}) collective-permute-start(bf16[4,2,256,256]{3,2,1,0:T(8,128)(2,1)} %get-tuple-element.46), channel_id=1, source_target_pairs={{0,4},{4,0},{8,12},{12,8},{1,5},{5,1},{9,13},{13,9},{2,6},{6,2},{1... | collective-permute-start | bytes 3145736 | tf_op jit(solution)/shard_map/ppermute | solution.py:476
  202.9 2.8 collective-permute-start.11
  205.7 36.7 %collective-permute-done.1.refs_3_.refs_4_.refs_5_ = bf16[9,2,256,256]{3,2,1,0:T(8,128)(2,1)} collective-permute-done((bf16[9,2,256,256]{3,2,1,0:T(8,128)(2,1)}, bf16[9,2,256,256]{3,2,1,0:T(8,128)(2,1)}, u32[]{:S(2)}, u32[]{:S(2)}) %collective-permute-start.1) | collective-permute-done | bytes 2359328 | tf_op jit(solution)/shard_map/ppermute | solution.py:476
  242.4 10.2 %attention1.1 = (bf16[2,256,256]{2,1,0:T(8,128)(2,1)}, bf16[4,2,256,256]{3,2,1,0:T(8,128)(2,1)}, bf16[4,2,256,256]{3,2,1,0:T(8,128)(2,1)}, bf16[4,2,256,256]{3,2,1,0:T(8,128)(2,1)}) custom-call(s32[1]{0:T(128)} %bitcast.z_ref, bf16[2,256,4096]{2,1,0:T(8,128)(2,1)} %refs_0_.11, bf16[2,256,4096]{2,1,0:T(8,128)(2,1)} %refs_1_.11, ...), custom_call_target="tpu_custom_call" | custom-call | flops 399999991808 | bytes 10485760 | tf_op jit(solution)/shard_map/attention1/pallas_call | solution.py:212
  252.6 2.9 slice.14
  255.6 10.4 %collective-permute-done.9.refs_1_.refs_3_.refs_4_.refs_5_ = bf16[4,2,256,256]{3,2,1,0:T(8,128)(2,1)} collective-permute-done((bf16[4,2,256,256]{3,2,1,0:T(8,128)(2,1)}, bf16[4,2,256,256]{3,2,1,0:T(8,128)(2,1)}, u32[]{:S(2)}, u32[]{:S(2)}) %collective-permute-start.9) | collective-permute-done | bytes 1048608 | tf_op jit(solution)/shard_map/ppermute | solution.py:476
  266.0 22.6 %collective-permute-done.11.refs_3_.refs_9_.refs_10_.refs_11_ = bf16[4,2,256,256]{3,2,1,0:T(8,128)(2,1)} collective-permute-done((bf16[4,2,256,256]{3,2,1,0:T(8,128)(2,1)}, bf16[4,2,256,256]{3,2,1,0:T(8,128)(2,1)}, u32[]{:S(2)}, u32[]{:S(2)}) %collective-permute-start.11) | collective-permute-done | bytes 1048608 | tf_op jit(solution)/shard_map/ppermute | solution.py:476
  288.6 9.1 %attention2.1 = (bf16[2,256,256]{2,1,0:T(8,128)(2,1)}, bf16[1,2,256,256]{3,2,1,0:T(8,128)(2,1)}, bf16[1,2,256,256]{3,2,1,0:T(8,128)(2,1)}, bf16[1,2,256,256]{3,2,1,0:T(8,128)(2,1)}) custom-call(s32[1]{0:T(128)} %bitcast.z_ref, bf16[2,256,4096]{2,1,0:T(8,128)(2,1)} %refs_0_.11, bf16[2,256,4096]{2,1,0:T(8,128)(2,1)} %refs_1_.11, ...), custom_call_target="tpu_custom_call" | custom-call | flops 399999991808 | bytes 10485760 | tf_op jit(solution)/shard_map/attention2/pallas_call | solution.py:212
  297.7 44.1 %collective-permute-start.4 = (bf16[4,2,256,256]{3,2,1,0:T(8,128)(2,1)}, bf16[4,2,256,256]{3,2,1,0:T(8,128)(2,1)S(1)}, u32[]{:S(2)}, u32[]{:S(2)}) collective-permute-start(bf16[4,2,256,256]{3,2,1,0:T(8,128)(2,1)} %get-tuple-element.40), channel_id=1, source_target_pairs={{0,4},{4,0},{8,12},{12,8},{1,5},{5,1},{9,13},{13,9},{2,6},{6,2},{1... | collective-permute-start | bytes 3145736 | tf_op jit(solution)/shard_map/ppermute | solution.py:476
  344.6 10.0 %collective-permute-done.5.refs_6_.refs_7_.refs_8_.refs_3_.refs_2_ = bf16[4,2,256,256]{3,2,1,0:T(8,128)(2,1)} collective-permute-done((bf16[4,2,256,256]{3,2,1,0:T(8,128)(2,1)}, bf16[4,2,256,256]{3,2,1,0:T(8,128)(2,1)}, u32[]{:S(2)}, u32[]{:S(2)}) %collective-permute-start.5) | collective-permute-done | bytes 1048608 | tf_op jit(solution)/shard_map/ppermute | solution.py:476
  354.7 3.3 collective-permute-start.16
  359.0 32.8 %all-gather.11.cloned.1.call-done = bf16[48,2,256,256]{3,2,1,0:T(8,128)(2,1)} async-done(((bf16[6,2,256,256]{3,2,1,0:T(8,128)(2,1)}), bf16[48,2,256,256]{3,2,1,0:T(8,128)(2,1)}) %all-gather.11.cloned.1.call-update) | async-done | bytes 12582928 | tf_op jit(solution)/shard_map/all_gather | solution.py:480
  391.8 2.8 copy-done
  394.6 16.6 %project0.1.refs_12_ = f32[2,256,6144]{2,1,0:T(8,128)} custom-call(s32[1]{0:T(128)} %bitcast.z_ref, bf16[2,256,256]{2,1,0:T(8,128)(2,1)S(1)} %copy-done.1, bf16[4,2,256,256]{3,2,1,0:T(8,128)(2,1)} %collective-permute-done.9.refs_1_.refs_3_.refs_4_.refs_5_, bf16[4,2,256,256]{3,2,1,0:T(8,128)(2,1)} %collective-permute-done.10.refs_2_.refs_6_.refs_7_.refs_8_, ...), custom_call_target="tpu_custom_call" | custom-call | flops 15000000512 | bytes 31457280 | tf_op jit(solution)/shard_map/project0/pallas_call | solution.py:309
  413.2 9.0 %attention3.1 = (bf16[2,256,256]{2,1,0:T(8,128)(2,1)}, bf16[1,2,256,256]{3,2,1,0:T(8,128)(2,1)}, bf16[1,2,256,256]{3,2,1,0:T(8,128)(2,1)}, bf16[1,2,256,256]{3,2,1,0:T(8,128)(2,1)}) custom-call(s32[1]{0:T(128)} %bitcast.z_ref, bf16[2,256,4096]{2,1,0:T(8,128)(2,1)} %refs_0_.11, bf16[2,256,4096]{2,1,0:T(8,128)(2,1)} %refs_1_.11, ...), custom_call_target="tpu_custom_call" | custom-call | flops 399999991808 | bytes 10485760 | tf_op jit(solution)/shard_map/attention3/pallas_call | solution.py:212
  426.7 19.1 %project12.1 = (f32[12,2,256,512]{3,2,1,0:T(8,128)S(1)}, bf16[12,4,2,256,256]{4,3,2,1,0:T(8,128)(2,1)S(1)}) custom-call(s32[1]{0:T(128)} %bitcast.z_ref, bf16[2,256,256]{2,1,0:T(8,128)(2,1)} %get-tuple-element.61.refs_0_, bf16[4,2,256,256]{3,2,1,0:T(8,128)(2,1)} %copy-done.4, ...), custom_call_target="tpu_custom_call" | custom-call | flops 15000000512 | bytes 31457280 | tf_op jit(solution)/shard_map/project12/pallas_call | solution.py:392
  445.9 7.7 %projectlast.1 = bf16[2,256,6144]{2,1,0:T(8,128)(2,1)} custom-call(s32[1]{0:T(128)} %bitcast.z_ref, bf16[2,256,256]{2,1,0:T(8,128)(2,1)S(1)} %copy-done.2, bf16[1,2,256,256]{3,2,1,0:T(8,128)(2,1)S(1)} %collective-permute-done.13.refs_1_, bf16[1,2,256,256]{3,2,1,0:T(8,128)(2,1)S(1)} %collective-permute-done.14.refs_2_, ...), custom_call_target="tpu_custom_call" | custom-call | flops 15000000512 | bytes 6291456 | tf_op jit(solution)/shard_map/projectlast/pallas_call | solution.py:447
  (54 shorter events, 23.1 us)
Async XLA Ops:
  6.5 352.5 %all-gather.5.cloned.1.call-start = ((), (), s32[]{:S(2)}) async-start(), calls=%async_computation | async-start | bytes 14155776 | tf_op jit(solution)/shard_map/all_gather | solution.py:480
  11.4 347.6 %all-gather.9.cloned.1.call-start = ((), (), s32[]{:S(2)}) async-start(), calls=%async_computation.2 | async-start | bytes 14155776 | tf_op jit(solution)/shard_map/all_gather | solution.py:480
  11.5 107.9 %collective-permute-start = (bf16[9,2,256,256]{3,2,1,0:T(8,128)(2,1)}, bf16[9,2,256,256]{3,2,1,0:T(8,128)(2,1)S(1)}, u32[]{:S(2)}, u32[]{:S(2)}) collective-permute-start(bf16[9,2,256,256]{3,2,1,0:T(8,128)(2,1)} %get-tuple-element.36), channel_id=1, source_target_pairs={{0,8},{4,12},{8,0},{12,4},{1,9},{5,13},{9,1},{13,5},{2,10},{6,14},... | collective-permute-start | bytes 7077896 | tf_op jit(solution)/shard_map/ppermute | solution.py:476
  15.6 121.2 %collective-permute-start.7 = (bf16[9,2,256,256]{3,2,1,0:T(8,128)(2,1)}, bf16[9,2,256,256]{3,2,1,0:T(8,128)(2,1)}, u32[]{:S(2)}, u32[]{:S(2)}) collective-permute-start(bf16[9,2,256,256]{3,2,1,0:T(8,128)(2,1)} %get-tuple-element.43), channel_id=1, source_target_pairs={{0,4},{4,0},{8,12},{12,8},{1,5},{5,1},{9,13},{13,9},{2,6},{6,2},{1... | collective-permute-start | bytes 7077896 | tf_op jit(solution)/shard_map/ppermute | solution.py:476
  17.2 119.6 %collective-permute-start.8 = (bf16[3,2,256,256]{3,2,1,0:T(8,128)(2,1)}, bf16[3,2,256,256]{3,2,1,0:T(8,128)(2,1)S(1)}, u32[]{:S(2)}, u32[]{:S(2)}) collective-permute-start(bf16[3,2,256,256]{3,2,1,0:T(8,128)(2,1)} %get-tuple-element.44), channel_id=1, source_target_pairs={{0,12},{4,8},{8,4},{12,0},{1,13},{5,9},{9,5},{13,1},{2,14},{6,10},... | collective-permute-start | bytes 2359304 | tf_op jit(solution)/shard_map/ppermute | solution.py:476
  125.0 77.9 %collective-permute-start.2 = (bf16[3,2,256,256]{3,2,1,0:T(8,128)(2,1)}, bf16[3,2,256,256]{3,2,1,0:T(8,128)(2,1)}, u32[]{:S(2)}, u32[]{:S(2)}) collective-permute-start(bf16[3,2,256,256]{3,2,1,0:T(8,128)(2,1)} %get-tuple-element.38), channel_id=1, source_target_pairs={{0,8},{4,12},{8,0},{12,4},{1,9},{5,13},{9,1},{13,5},{2,10},{6,14},... | collective-permute-start | bytes 2359304 | tf_op jit(solution)/shard_map/ppermute | solution.py:476
  125.1 80.6 %collective-permute-start.3 = (bf16[3,2,256,256]{3,2,1,0:T(8,128)(2,1)}, bf16[3,2,256,256]{3,2,1,0:T(8,128)(2,1)}, u32[]{:S(2)}, u32[]{:S(2)}) collective-permute-start(bf16[3,2,256,256]{3,2,1,0:T(8,128)(2,1)} %get-tuple-element.39), channel_id=1, source_target_pairs={{0,12},{4,8},{8,4},{12,0},{1,13},{5,9},{9,5},{13,1},{2,14},{6,10},... | collective-permute-start | bytes 2359304 | tf_op jit(solution)/shard_map/ppermute | solution.py:476
  128.2 114.2 %collective-permute-start.1 = (bf16[9,2,256,256]{3,2,1,0:T(8,128)(2,1)}, bf16[9,2,256,256]{3,2,1,0:T(8,128)(2,1)}, u32[]{:S(2)}, u32[]{:S(2)}) collective-permute-start(bf16[9,2,256,256]{3,2,1,0:T(8,128)(2,1)} %get-tuple-element.37), channel_id=1, source_target_pairs={{0,4},{4,0},{8,12},{12,8},{1,5},{5,1},{9,13},{13,9},{2,6},{6,2},{1... | collective-permute-start | bytes 7077896 | tf_op jit(solution)/shard_map/ppermute | solution.py:476
  131.4 227.6 %all-gather.7.cloned.1.call-start = ((), (), s32[]{:S(2)}) async-start(), calls=%async_computation.1 | async-start | bytes 14155776 | tf_op jit(solution)/shard_map/all_gather | solution.py:480
  147.8 118.2 %collective-permute-start.9 = (bf16[4,2,256,256]{3,2,1,0:T(8,128)(2,1)}, bf16[4,2,256,256]{3,2,1,0:T(8,128)(2,1)}, u32[]{:S(2)}, u32[]{:S(2)}) collective-permute-start(bf16[4,2,256,256]{3,2,1,0:T(8,128)(2,1)} %get-tuple-element.46), channel_id=1, source_target_pairs={{0,4},{4,0},{8,12},{12,8},{1,5},{5,1},{9,13},{13,9},{2,6},{6,2},{1... | collective-permute-start | bytes 3145736 | tf_op jit(solution)/shard_map/ppermute | solution.py:476
  197.5 68.5 %collective-permute-start.10 = (bf16[4,2,256,256]{3,2,1,0:T(8,128)(2,1)}, bf16[4,2,256,256]{3,2,1,0:T(8,128)(2,1)}, u32[]{:S(2)}, u32[]{:S(2)}) collective-permute-start(bf16[4,2,256,256]{3,2,1,0:T(8,128)(2,1)} %get-tuple-element.47), channel_id=1, source_target_pairs={{0,8},{4,12},{8,0},{12,4},{1,9},{5,13},{9,1},{13,5},{2,10},{6,14},... | collective-permute-start | bytes 3145736 | tf_op jit(solution)/shard_map/ppermute | solution.py:476
  201.6 190.3 %all-gather.11.cloned.1.call-start = ((), (), s32[]{:S(2)}) async-start(), calls=%async_computation.3 | async-start | bytes 14155776 | tf_op jit(solution)/shard_map/all_gather | solution.py:480
  202.9 85.7 %collective-permute-start.11 = (bf16[4,2,256,256]{3,2,1,0:T(8,128)(2,1)}, bf16[4,2,256,256]{3,2,1,0:T(8,128)(2,1)}, u32[]{:S(2)}, u32[]{:S(2)}) collective-permute-start(bf16[4,2,256,256]{3,2,1,0:T(8,128)(2,1)} %get-tuple-element.48), channel_id=1, source_target_pairs={{0,12},{4,8},{8,4},{12,0},{1,13},{5,9},{9,5},{13,1},{2,14},{6,10},... | collective-permute-start | bytes 3145736 | tf_op jit(solution)/shard_map/ppermute | solution.py:476
  252.5 102.1 %collective-permute-start.5 = (bf16[4,2,256,256]{3,2,1,0:T(8,128)(2,1)}, bf16[4,2,256,256]{3,2,1,0:T(8,128)(2,1)}, u32[]{:S(2)}, u32[]{:S(2)}) collective-permute-start(bf16[4,2,256,256]{3,2,1,0:T(8,128)(2,1)} %get-tuple-element.41), channel_id=1, source_target_pairs={{0,8},{4,12},{8,0},{12,4},{1,9},{5,13},{9,1},{13,5},{2,10},{6,14},... | collective-permute-start | bytes 3145736 | tf_op jit(solution)/shard_map/ppermute | solution.py:476
  288.6 53.2 %copy-start.6 = (bf16[4,2,256,256]{3,2,1,0:T(8,128)(2,1)S(1)}, bf16[4,2,256,256]{3,2,1,0:T(8,128)(2,1)}, u32[]{:S(2)}) copy-start(bf16[4,2,256,256]{3,2,1,0:T(8,128)(2,1)} %get-tuple-element.42) | copy-start | bytes 3145732
  288.6 103.2 %copy-start.1 = (bf16[2,256,256]{2,1,0:T(8,128)(2,1)S(1)}, bf16[2,256,256]{2,1,0:T(8,128)(2,1)}, u32[]{:S(2)}) copy-start(bf16[2,256,256]{2,1,0:T(8,128)(2,1)} %get-tuple-element.45.refs_0_) | copy-start | bytes 786436
  297.7 113.5 %collective-permute-start.4 = (bf16[4,2,256,256]{3,2,1,0:T(8,128)(2,1)}, bf16[4,2,256,256]{3,2,1,0:T(8,128)(2,1)S(1)}, u32[]{:S(2)}, u32[]{:S(2)}) collective-permute-start(bf16[4,2,256,256]{3,2,1,0:T(8,128)(2,1)} %get-tuple-element.40), channel_id=1, source_target_pairs={{0,4},{4,0},{8,12},{12,8},{1,5},{5,1},{9,13},{13,9},{2,6},{6,2},{1... | collective-permute-start | bytes 3145736 | tf_op jit(solution)/shard_map/ppermute | solution.py:476
  341.8 69.4 %collective-permute-start.6 = (bf16[4,2,256,256]{3,2,1,0:T(8,128)(2,1)S(1)}, bf16[4,2,256,256]{3,2,1,0:T(8,128)(2,1)S(1)}, u32[]{:S(2)}, u32[]{:S(2)}) collective-permute-start(bf16[4,2,256,256]{3,2,1,0:T(8,128)(2,1)S(1)} %copy-done.6), channel_id=1, source_target_pairs={{0,12},{4,8},{8,4},{12,0},{1,13},{5,9},{9,5},{13,1},{2,14},{6,10},... | collective-permute-start | bytes 3145736 | tf_op jit(solution)/shard_map/ppermute | solution.py:476
  354.7 67.6 %collective-permute-start.12 = (bf16[1,2,256,256]{3,2,1,0:T(8,128)(2,1)}, bf16[1,2,256,256]{3,2,1,0:T(8,128)(2,1)}, u32[]{:S(2)}, u32[]{:S(2)}) collective-permute-start(bf16[1,2,256,256]{3,2,1,0:T(8,128)(2,1)} %get-tuple-element.57), channel_id=1, source_target_pairs={{0,4},{4,0},{8,12},{12,8},{1,5},{5,1},{9,13},{13,9},{2,6},{6,2},{1... | collective-permute-start | bytes 786440 | tf_op jit(solution)/shard_map/ppermute | solution.py:476
  354.7 72.0 %collective-permute-start.16 = (bf16[1,2,256,256]{3,2,1,0:T(8,128)(2,1)}, bf16[1,2,256,256]{3,2,1,0:T(8,128)(2,1)}, u32[]{:S(2)}, u32[]{:S(2)}) collective-permute-start(bf16[1,2,256,256]{3,2,1,0:T(8,128)(2,1)} %get-tuple-element.63), channel_id=1, source_target_pairs={{0,8},{4,12},{8,0},{12,4},{1,9},{5,13},{9,1},{13,5},{2,10},{6,14},... | collective-permute-start | bytes 786440 | tf_op jit(solution)/shard_map/ppermute | solution.py:476
  358.0 68.7 %collective-permute-start.17 = (bf16[1,2,256,256]{3,2,1,0:T(8,128)(2,1)}, bf16[1,2,256,256]{3,2,1,0:T(8,128)(2,1)}, u32[]{:S(2)}, u32[]{:S(2)}) collective-permute-start(bf16[1,2,256,256]{3,2,1,0:T(8,128)(2,1)} %get-tuple-element.64), channel_id=1, source_target_pairs={{0,12},{4,8},{8,4},{12,0},{1,13},{5,9},{9,5},{13,1},{2,14},{6,10},... | collective-permute-start | bytes 786440 | tf_op jit(solution)/shard_map/ppermute | solution.py:476
  422.2 23.6 %collective-permute-start.13 = (bf16[1,2,256,256]{3,2,1,0:T(8,128)(2,1)}, bf16[1,2,256,256]{3,2,1,0:T(8,128)(2,1)S(1)}, u32[]{:S(2)}, u32[]{:S(2)}) collective-permute-start(bf16[1,2,256,256]{3,2,1,0:T(8,128)(2,1)} %get-tuple-element.58), channel_id=1, source_target_pairs={{0,4},{4,0},{8,12},{12,8},{1,5},{5,1},{9,13},{13,9},{2,6},{6,2},{1... | collective-permute-start | bytes 786440 | tf_op jit(solution)/shard_map/ppermute | solution.py:476
  423.9 22.0 %collective-permute-start.14 = (bf16[1,2,256,256]{3,2,1,0:T(8,128)(2,1)}, bf16[1,2,256,256]{3,2,1,0:T(8,128)(2,1)S(1)}, u32[]{:S(2)}, u32[]{:S(2)}) collective-permute-start(bf16[1,2,256,256]{3,2,1,0:T(8,128)(2,1)} %get-tuple-element.59), channel_id=1, source_target_pairs={{0,8},{4,12},{8,0},{12,4},{1,9},{5,13},{9,1},{13,5},{2,10},{6,14},... | collective-permute-start | bytes 786440 | tf_op jit(solution)/shard_map/ppermute | solution.py:476
  426.2 19.7 %collective-permute-start.15 = (bf16[1,2,256,256]{3,2,1,0:T(8,128)(2,1)}, bf16[1,2,256,256]{3,2,1,0:T(8,128)(2,1)S(1)}, u32[]{:S(2)}, u32[]{:S(2)}) collective-permute-start(bf16[1,2,256,256]{3,2,1,0:T(8,128)(2,1)} %get-tuple-element.60), channel_id=1, source_target_pairs={{0,12},{4,8},{8,4},{12,0},{1,13},{5,9},{9,5},{13,1},{2,14},{6,10},... | collective-permute-start | bytes 786440 | tf_op jit(solution)/shard_map/ppermute | solution.py:476
  (6 other events, 26.3 us)
Sparse Core Ops, SparseCore 0:
  11.6 74.8 all-gather.4
  131.5 112.3 all-gather.8
  245.8 72.1 all-gather.6
  319.7 72.1 all-gather.10

commit v6 on v5

--- a/solution.py
+++ b/solution.py
@@ -265,60 +265,77 @@
     grouped = 2 if tiles % 2 == 0 else 1
     steps = tiles // grouped
     tile = grouped * width
+    count = SEQ * steps
 
     def body(z_ref, *refs):
         o_refs, w_refs = refs[:SEQ], refs[SEQ : 2 * SEQ]
-        residual_ref, out_ref, rows_all = refs[2 * SEQ :]
-        at = pl.program_id(0)
-
-        @pl.when(at == 0)
-        def _():
-            attended_rows(z_ref, o_refs, rows_all, width)
-
-        def step(w_ref):
+        residual_ref, out, weights, rows_all, parts, sums, sems = refs[2 * SEQ :]
+
+        def columns(at):
+            start = (jnp.bitwise_xor(z_ref[0], at // steps) * steps + at % steps) * tile
+            return pl.ds(pl.multiple_of(start, tile), tile)
+
+        def weight_copy(at):
+            source = w_refs[at // steps].at[
+                :,
+                chunk // halves,
+                pl.ds(at % steps * grouped, grouped),
+                chunk % halves,
+            ]
+            return pltpu.make_async_copy(source, weights.at[at], sems.at[0, at])
+
+        def residual_copy(at):
+            return pltpu.make_async_copy(
+                residual_ref.at[:, :, columns(at)], parts.at[at], sems.at[1, at]
+            )
+
+        def out_copy(at):
+            return pltpu.make_async_copy(
+                sums.at[at], out.at[:, :, columns(at)], sems.at[2, at]
+            )
+
+        for at in range(count):
+            weight_copy(at).start()
+            residual_copy(at).start()
+        attended_rows(z_ref, o_refs, rows_all, width)
+
+        @pl.loop(0, count)
+        def _(at):
+            pltpu.make_async_copy(weights.at[at], weights.at[at], sems.at[0, at]).wait()
+            residual_copy(at).wait()
             for g in range(grouped):
                 cols = slice(g * width, (g + 1) * width)
-                value = residual_ref[:, :, cols].astype(F32).reshape(images * rows, width)
+                value = parts[at, :, :, cols].astype(F32).reshape(images * rows, width)
                 value += jnp.dot(
                     rows_all[...],
-                    w_ref[:, 0, g, 0].reshape(SEQ * width, width),
+                    weights[at, :, g].reshape(SEQ * width, width),
                     preferred_element_type=F32,
                 )
-                out_ref[:, :, cols] = value.reshape(images, rows, width)
-
-        for p in range(SEQ):
-            pl.when(at // steps == p)(lambda p=p: step(w_refs[p]))
-
-    def weight_spec(p):
-        return pl.BlockSpec(
-            (SEQ, 1, grouped, 1, rows, width),
-            lambda at, z_ref: (
-                0,
-                chunk // halves,
-                jnp.clip(at - p * steps, 0, steps - 1),
-                chunk % halves,
-                0,
-                0,
-            ),
-        )
-
-    block = pl.BlockSpec(
-        (images, rows, tile),
-        lambda at, z_ref: (0, 0, jnp.bitwise_xor(z_ref[0], at // steps) * steps + at % steps),
-    )
+                sums[at, :, :, cols] = value.reshape(images, rows, width)
+            out_copy(at).start()
+
+        @pl.loop(0, count)
+        def _(at):
+            out_copy(at).wait()
+
+    anywhere = pl.BlockSpec(memory_space=pl.ANY)
     return pl.pallas_call(
         body,
         out_shape=jax.ShapeDtypeStruct((images, rows, model), F32),
         grid_spec=pltpu.PrefetchScalarGridSpec(
             num_scalar_prefetch=1,
-            grid=(SEQ * steps,),
-            in_specs=[attended_spec(o) for o in attended]
-            + [weight_spec(p) for p in range(SEQ)]
-            + [block],
-            out_specs=block,
-            scratch_shapes=[pltpu.VMEM((images * rows, SEQ * width), BF16)],
-        ),
-        compiler_params=pltpu.CompilerParams(vmem_limit_bytes=38 * MIB),
+            grid=(1,),
+            in_specs=[attended_spec(o) for o in attended] + [anywhere] * (SEQ + 1),
+            out_specs=anywhere,
+            scratch_shapes=[
+                pltpu.VMEM((count, SEQ, grouped, rows, width), BF16),
+                pltpu.VMEM((images * rows, SEQ * width), BF16),
+                pltpu.VMEM((count, images, rows, tile), BF16),
+                pltpu.VMEM((count, images, rows, tile), F32),
+                pltpu.SemaphoreType.DMA((3, count)),
+            ],
+        ),
+        compiler_params=pltpu.CompilerParams(vmem_limit_bytes=56 * MIB),
         cost_estimate=cost(PROJECT_COST, 30 * 2**20),
         name=f"project{chunk}",
     )(z, *attended, *pieces, residual)

time: 463 us -> 460 us (level)
  transfers between devices with their start and end apart: 22 -> 22, of which waited for: 8 -> 8; matrix products, arithmetic and copies ran while one was open for 2% -> 2% of each run, Pallas kernels for 17% -> 16%
where the time goes in v6:
time: 460 us; the launch traced here: 458 us
  waiting for transfers between devices  221 us (48%)
  starting transfers between devices  123 us (27%)
  Pallas kernels  87.1 us (19%)
  between operations  13.3 us (3%)
  local copies, waits for them, and re-layouts  12.7 us (3%)
    ppermute x18, waiting for transfers between devices, send(): lax.ppermute(packs[m - 1], 'seq', [(i, i ^ m) for i in range(SEQ)])  188 us
    ppermute x18, starting transfers between devices, send(): lax.ppermute(packs[m - 1], 'seq', [(i, i ^ m) for i in range(SEQ)])  123 us
    pallas_call x4, Pallas kernels, attention(): pl.pallas_call(body, out_shape=[jax.ShapeDtypeStruct((images, rows, width...  38.3 us
    all_gather x4, waiting for transfers between devices, whole(): full = lax.all_gather(piece, ('img', 'grp'), axis=0, tiled=True)  32.8 us
    pallas_call x1, Pallas kernels, project_middle(): pl.pallas_call(body, out_shape=[pltpu.VMEM((count, images, rows, tile), F...  19.1 us
    pallas_call x1, Pallas kernels, project_first(): pl.pallas_call(body, out_shape=jax.ShapeDtypeStruct((images, rows, model)...  13 us
  transfers between devices with their start and end apart: 22, of which 8 were waited for; matrix products, arithmetic and copies ran while one was open for 2% of the time, Pallas kernels for 16%

profile of v6, /device:TPU:0, one launch (start us, length us, event | category | flops | bytes accessed | tf_op | source)
XLA Modules:
  0.0 457.6 jit_solution(7215383645620788786)
XLA Ops:
  6.5 4.9 %pack0.1 = (bf16[9,2,256,256]{3,2,1,0:T(8,128)(2,1)}, bf16[9,2,256,256]{3,2,1,0:T(8,128)(2,1)}, bf16[3,2,256,256]{3,2,1,0:T(8,128)(2,1)}, bf16[6,2,256,256]{3,2,1,0:T(8,128)(2,1)}) custom-call(s32[1]{0:T(128)} %bitcast.z_ref, s32[1]{0:T(128)} %bitcast.1.grp_ref, bf16[2,256,4096]{2,1,0:T(8,128)(2,1)} %refs_0_.11, bf16[2,256,4096]{2,1,0:T(8,128)(2,1)} %refs_1_.11, ...), custom_call_target="tpu_custom_call" | custom-call | flops 5000000000 | bytes 10485760 | tf_op jit(solution)/shard_map/pack0/pallas_call | solution.py:113
  11.5 4.1 collective-permute-start
  17.2 102.2 %collective-permute-done.refs_9_.refs_6_.refs_7_.refs_8_ = bf16[9,2,256,256]{3,2,1,0:T(8,128)(2,1)S(1)} collective-permute-done((bf16[9,2,256,256]{3,2,1,0:T(8,128)(2,1)}, bf16[9,2,256,256]{3,2,1,0:T(8,128)(2,1)S(1)}, u32[]{:S(2)}, u32[]{:S(2)}) %collective-permute-start) | collective-permute-done | bytes 2359328 | tf_op jit(solution)/shard_map/ppermute | solution.py:493
  120.9 4.1 pack1.1
  125.1 3.1 collective-permute-start.3
  131.4 5.3 %collective-permute-done.8.refs_9_.refs_10_.refs_11_ = bf16[3,2,256,256]{3,2,1,0:T(8,128)(2,1)S(1)} collective-permute-done((bf16[3,2,256,256]{3,2,1,0:T(8,128)(2,1)}, bf16[3,2,256,256]{3,2,1,0:T(8,128)(2,1)S(1)}, u32[]{:S(2)}, u32[]{:S(2)}) %collective-permute-start.8) | collective-permute-done | bytes 786464 | tf_op jit(solution)/shard_map/ppermute | solution.py:493
  137.7 10.1 %attention0.1 = (bf16[2,256,256]{2,1,0:T(8,128)(2,1)}, bf16[4,2,256,256]{3,2,1,0:T(8,128)(2,1)}, bf16[4,2,256,256]{3,2,1,0:T(8,128)(2,1)}, bf16[4,2,256,256]{3,2,1,0:T(8,128)(2,1)}) custom-call(s32[1]{0:T(128)} %bitcast.z_ref, bf16[2,256,4096]{2,1,0:T(8,128)(2,1)} %refs_0_.11, bf16[2,256,4096]{2,1,0:T(8,128)(2,1)} %refs_1_.11, ...), custom_call_target="tpu_custom_call" | custom-call | flops 399999991808 | bytes 10485760 | tf_op jit(solution)/shard_map/attention0/pallas_call | solution.py:212
  147.8 49.8 %collective-permute-start.9 = (bf16[4,2,256,256]{3,2,1,0:T(8,128)(2,1)}, bf16[4,2,256,256]{3,2,1,0:T(8,128)(2,1)}, u32[]{:S(2)}, u32[]{:S(2)}) collective-permute-start(bf16[4,2,256,256]{3,2,1,0:T(8,128)(2,1)} %get-tuple-element.46), channel_id=1, source_target_pairs={{0,4},{4,0},{8,12},{12,8},{1,5},{5,1},{9,13},{13,9},{2,6},{6,2},{1... | collective-permute-start | bytes 3145736 | tf_op jit(solution)/shard_map/ppermute | solution.py:493
  202.9 2.8 collective-permute-start.11
  205.7 36.7 %collective-permute-done.1.refs_3_.refs_4_.refs_5_ = bf16[9,2,256,256]{3,2,1,0:T(8,128)(2,1)} collective-permute-done((bf16[9,2,256,256]{3,2,1,0:T(8,128)(2,1)}, bf16[9,2,256,256]{3,2,1,0:T(8,128)(2,1)}, u32[]{:S(2)}, u32[]{:S(2)}) %collective-permute-start.1) | collective-permute-done | bytes 2359328 | tf_op jit(solution)/shard_map/ppermute | solution.py:493
  242.4 10.1 %attention1.1 = (bf16[2,256,256]{2,1,0:T(8,128)(2,1)}, bf16[4,2,256,256]{3,2,1,0:T(8,128)(2,1)}, bf16[4,2,256,256]{3,2,1,0:T(8,128)(2,1)}, bf16[4,2,256,256]{3,2,1,0:T(8,128)(2,1)}) custom-call(s32[1]{0:T(128)} %bitcast.z_ref, bf16[2,256,4096]{2,1,0:T(8,128)(2,1)} %refs_0_.11, bf16[2,256,4096]{2,1,0:T(8,128)(2,1)} %refs_1_.11, ...), custom_call_target="tpu_custom_call" | custom-call | flops 399999991808 | bytes 10485760 | tf_op jit(solution)/shard_map/attention1/pallas_call | solution.py:212
  252.6 3.0 slice.14
  255.6 10.4 %collective-permute-done.9.refs_1_.refs_3_.refs_4_.refs_5_ = bf16[4,2,256,256]{3,2,1,0:T(8,128)(2,1)} collective-permute-done((bf16[4,2,256,256]{3,2,1,0:T(8,128)(2,1)}, bf16[4,2,256,256]{3,2,1,0:T(8,128)(2,1)}, u32[]{:S(2)}, u32[]{:S(2)}) %collective-permute-start.9) | collective-permute-done | bytes 1048608 | tf_op jit(solution)/shard_map/ppermute | solution.py:493
  266.0 22.6 %collective-permute-done.11.refs_3_.refs_9_.refs_10_.refs_11_ = bf16[4,2,256,256]{3,2,1,0:T(8,128)(2,1)} collective-permute-done((bf16[4,2,256,256]{3,2,1,0:T(8,128)(2,1)}, bf16[4,2,256,256]{3,2,1,0:T(8,128)(2,1)}, u32[]{:S(2)}, u32[]{:S(2)}) %collective-permute-start.11) | collective-permute-done | bytes 1048608 | tf_op jit(solution)/shard_map/ppermute | solution.py:493
  288.6 9.1 %attention2.1 = (bf16[2,256,256]{2,1,0:T(8,128)(2,1)}, bf16[1,2,256,256]{3,2,1,0:T(8,128)(2,1)}, bf16[1,2,256,256]{3,2,1,0:T(8,128)(2,1)}, bf16[1,2,256,256]{3,2,1,0:T(8,128)(2,1)}) custom-call(s32[1]{0:T(128)} %bitcast.z_ref, bf16[2,256,4096]{2,1,0:T(8,128)(2,1)} %refs_0_.11, bf16[2,256,4096]{2,1,0:T(8,128)(2,1)} %refs_1_.11, ...), custom_call_target="tpu_custom_call" | custom-call | flops 399999991808 | bytes 10485760 | tf_op jit(solution)/shard_map/attention2/pallas_call | solution.py:212
  297.7 44.1 %collective-permute-start.4 = (bf16[4,2,256,256]{3,2,1,0:T(8,128)(2,1)}, bf16[4,2,256,256]{3,2,1,0:T(8,128)(2,1)S(1)}, u32[]{:S(2)}, u32[]{:S(2)}) collective-permute-start(bf16[4,2,256,256]{3,2,1,0:T(8,128)(2,1)} %get-tuple-element.40), channel_id=1, source_target_pairs={{0,4},{4,0},{8,12},{12,8},{1,5},{5,1},{9,13},{13,9},{2,6},{6,2},{1... | collective-permute-start | bytes 3145736 | tf_op jit(solution)/shard_map/ppermute | solution.py:493
  344.6 10.0 %collective-permute-done.5.refs_6_.refs_7_.refs_8_.refs_3_.refs_2_ = bf16[4,2,256,256]{3,2,1,0:T(8,128)(2,1)} collective-permute-done((bf16[4,2,256,256]{3,2,1,0:T(8,128)(2,1)}, bf16[4,2,256,256]{3,2,1,0:T(8,128)(2,1)}, u32[]{:S(2)}, u32[]{:S(2)}) %collective-permute-start.5) | collective-permute-done | bytes 1048608 | tf_op jit(solution)/shard_map/ppermute | solution.py:493
  354.7 3.3 collective-permute-start.16
  359.1 32.8 %all-gather.11.cloned.1.call-done = bf16[48,2,256,256]{3,2,1,0:T(8,128)(2,1)} async-done(((bf16[6,2,256,256]{3,2,1,0:T(8,128)(2,1)}), bf16[48,2,256,256]{3,2,1,0:T(8,128)(2,1)}) %all-gather.11.cloned.1.call-update) | async-done | bytes 12582928 | tf_op jit(solution)/shard_map/all_gather | solution.py:497
  391.8 13.0 %project0.1.refs_12_ = f32[2,256,6144]{2,1,0:T(8,128)} custom-call(s32[1]{0:T(128)} %bitcast.z_ref, bf16[2,256,256]{2,1,0:T(8,128)(2,1)} %get-tuple-element.45.refs_0_, bf16[4,2,256,256]{3,2,1,0:T(8,128)(2,1)} %collective-permute-done.9.refs_1_.refs_3_.refs_4_.refs_5_, bf16[4,2,256,256]{3,2,1,0:T(8,128)(2,1)} %collective-permute-done.10.refs_2_.refs_6_.refs_7_.refs_8_, ...), custom_call_target="tpu_custom_call" | custom-call | flops 15000000512 | bytes 31457280 | tf_op jit(solution)/shard_map/project0/pallas_call | solution.py:322
  406.8 9.0 %attention3.1 = (bf16[2,256,256]{2,1,0:T(8,128)(2,1)}, bf16[1,2,256,256]{3,2,1,0:T(8,128)(2,1)}, bf16[1,2,256,256]{3,2,1,0:T(8,128)(2,1)}, bf16[1,2,256,256]{3,2,1,0:T(8,128)(2,1)}) custom-call(s32[1]{0:T(128)} %bitcast.z_ref, bf16[2,256,4096]{2,1,0:T(8,128)(2,1)} %refs_0_.11, bf16[2,256,4096]{2,1,0:T(8,128)(2,1)} %refs_1_.11, ...), custom_call_target="tpu_custom_call" | custom-call | flops 399999991808 | bytes 10485760 | tf_op jit(solution)/shard_map/attention3/pallas_call | solution.py:212
  415.8 5.6 %collective-permute-start.13 = (bf16[1,2,256,256]{3,2,1,0:T(8,128)(2,1)}, bf16[1,2,256,256]{3,2,1,0:T(8,128)(2,1)S(1)}, u32[]{:S(2)}, u32[]{:S(2)}) collective-permute-start(bf16[1,2,256,256]{3,2,1,0:T(8,128)(2,1)} %get-tuple-element.58), channel_id=1, source_target_pairs={{0,4},{4,0},{8,12},{12,8},{1,5},{5,1},{9,13},{13,9},{2,6},{6,2},{1... | collective-permute-start | bytes 786440 | tf_op jit(solution)/shard_map/ppermute | solution.py:493
  424.1 19.1 %project12.1 = (f32[12,2,256,512]{3,2,1,0:T(8,128)S(1)}, bf16[12,4,2,256,256]{4,3,2,1,0:T(8,128)(2,1)S(1)}) custom-call(s32[1]{0:T(128)} %bitcast.z_ref, bf16[2,256,256]{2,1,0:T(8,128)(2,1)} %get-tuple-element.61.refs_0_, bf16[4,2,256,256]{3,2,1,0:T(8,128)(2,1)} %copy-done.2, ...), custom_call_target="tpu_custom_call" | custom-call | flops 15000000512 | bytes 31457280 | tf_op jit(solution)/shard_map/project12/pallas_call | solution.py:409
  443.3 7.7 %projectlast.1 = bf16[2,256,6144]{2,1,0:T(8,128)(2,1)} custom-call(s32[1]{0:T(128)} %bitcast.z_ref, bf16[2,256,256]{2,1,0:T(8,128)(2,1)S(1)} %copy-done, bf16[1,2,256,256]{3,2,1,0:T(8,128)(2,1)S(1)} %collective-permute-done.13.refs_1_, bf16[1,2,256,256]{3,2,1,0:T(8,128)(2,1)S(1)} %collective-permute-done.14.refs_2_, ...), custom_call_target="tpu_custom_call" | custom-call | flops 15000000512 | bytes 6291456 | tf_op jit(solution)/shard_map/projectlast/pallas_call | solution.py:464
  (50 shorter events, 21.4 us)
Async XLA Ops:
  6.5 352.5 %all-gather.5.cloned.1.call-start = ((), (), s32[]{:S(2)}) async-start(), calls=%async_computation | async-start | bytes 14155776 | tf_op jit(solution)/shard_map/all_gather | solution.py:497
  11.4 347.6 %all-gather.9.cloned.1.call-start = ((), (), s32[]{:S(2)}) async-start(), calls=%async_computation.2 | async-start | bytes 14155776 | tf_op jit(solution)/shard_map/all_gather | solution.py:497
  11.5 107.9 %collective-permute-start = (bf16[9,2,256,256]{3,2,1,0:T(8,128)(2,1)}, bf16[9,2,256,256]{3,2,1,0:T(8,128)(2,1)S(1)}, u32[]{:S(2)}, u32[]{:S(2)}) collective-permute-start(bf16[9,2,256,256]{3,2,1,0:T(8,128)(2,1)} %get-tuple-element.36), channel_id=1, source_target_pairs={{0,8},{4,12},{8,0},{12,4},{1,9},{5,13},{9,1},{13,5},{2,10},{6,14},... | collective-permute-start | bytes 7077896 | tf_op jit(solution)/shard_map/ppermute | solution.py:493
  15.6 121.2 %collective-permute-start.7 = (bf16[9,2,256,256]{3,2,1,0:T(8,128)(2,1)}, bf16[9,2,256,256]{3,2,1,0:T(8,128)(2,1)}, u32[]{:S(2)}, u32[]{:S(2)}) collective-permute-start(bf16[9,2,256,256]{3,2,1,0:T(8,128)(2,1)} %get-tuple-element.43), channel_id=1, source_target_pairs={{0,4},{4,0},{8,12},{12,8},{1,5},{5,1},{9,13},{13,9},{2,6},{6,2},{1... | collective-permute-start | bytes 7077896 | tf_op jit(solution)/shard_map/ppermute | solution.py:493
  17.2 119.6 %collective-permute-start.8 = (bf16[3,2,256,256]{3,2,1,0:T(8,128)(2,1)}, bf16[3,2,256,256]{3,2,1,0:T(8,128)(2,1)S(1)}, u32[]{:S(2)}, u32[]{:S(2)}) collective-permute-start(bf16[3,2,256,256]{3,2,1,0:T(8,128)(2,1)} %get-tuple-element.44), channel_id=1, source_target_pairs={{0,12},{4,8},{8,4},{12,0},{1,13},{5,9},{9,5},{13,1},{2,14},{6,10},... | collective-permute-start | bytes 2359304 | tf_op jit(solution)/shard_map/ppermute | solution.py:493
  125.0 77.9 %collective-permute-start.2 = (bf16[3,2,256,256]{3,2,1,0:T(8,128)(2,1)}, bf16[3,2,256,256]{3,2,1,0:T(8,128)(2,1)}, u32[]{:S(2)}, u32[]{:S(2)}) collective-permute-start(bf16[3,2,256,256]{3,2,1,0:T(8,128)(2,1)} %get-tuple-element.38), channel_id=1, source_target_pairs={{0,8},{4,12},{8,0},{12,4},{1,9},{5,13},{9,1},{13,5},{2,10},{6,14},... | collective-permute-start | bytes 2359304 | tf_op jit(solution)/shard_map/ppermute | solution.py:493
  125.1 80.6 %collective-permute-start.3 = (bf16[3,2,256,256]{3,2,1,0:T(8,128)(2,1)}, bf16[3,2,256,256]{3,2,1,0:T(8,128)(2,1)}, u32[]{:S(2)}, u32[]{:S(2)}) collective-permute-start(bf16[3,2,256,256]{3,2,1,0:T(8,128)(2,1)} %get-tuple-element.39), channel_id=1, source_target_pairs={{0,12},{4,8},{8,4},{12,0},{1,13},{5,9},{9,5},{13,1},{2,14},{6,10},... | collective-permute-start | bytes 2359304 | tf_op jit(solution)/shard_map/ppermute | solution.py:493
  128.2 114.2 %collective-permute-start.1 = (bf16[9,2,256,256]{3,2,1,0:T(8,128)(2,1)}, bf16[9,2,256,256]{3,2,1,0:T(8,128)(2,1)}, u32[]{:S(2)}, u32[]{:S(2)}) collective-permute-start(bf16[9,2,256,256]{3,2,1,0:T(8,128)(2,1)} %get-tuple-element.37), channel_id=1, source_target_pairs={{0,4},{4,0},{8,12},{12,8},{1,5},{5,1},{9,13},{13,9},{2,6},{6,2},{1... | collective-permute-start | bytes 7077896 | tf_op jit(solution)/shard_map/ppermute | solution.py:493
  131.4 227.7 %all-gather.7.cloned.1.call-start = ((), (), s32[]{:S(2)}) async-start(), calls=%async_computation.1 | async-start | bytes 14155776 | tf_op jit(solution)/shard_map/all_gather | solution.py:497
  147.8 118.2 %collective-permute-start.9 = (bf16[4,2,256,256]{3,2,1,0:T(8,128)(2,1)}, bf16[4,2,256,256]{3,2,1,0:T(8,128)(2,1)}, u32[]{:S(2)}, u32[]{:S(2)}) collective-permute-start(bf16[4,2,256,256]{3,2,1,0:T(8,128)(2,1)} %get-tuple-element.46), channel_id=1, source_target_pairs={{0,4},{4,0},{8,12},{12,8},{1,5},{5,1},{9,13},{13,9},{2,6},{6,2},{1... | collective-permute-start | bytes 3145736 | tf_op jit(solution)/shard_map/ppermute | solution.py:493
  197.5 68.5 %collective-permute-start.10 = (bf16[4,2,256,256]{3,2,1,0:T(8,128)(2,1)}, bf16[4,2,256,256]{3,2,1,0:T(8,128)(2,1)}, u32[]{:S(2)}, u32[]{:S(2)}) collective-permute-start(bf16[4,2,256,256]{3,2,1,0:T(8,128)(2,1)} %get-tuple-element.47), channel_id=1, source_target_pairs={{0,8},{4,12},{8,0},{12,4},{1,9},{5,13},{9,1},{13,5},{2,10},{6,14},... | collective-permute-start | bytes 3145736 | tf_op jit(solution)/shard_map/ppermute | solution.py:493
  201.6 190.3 %all-gather.11.cloned.1.call-start = ((), (), s32[]{:S(2)}) async-start(), calls=%async_computation.3 | async-start | bytes 14155776 | tf_op jit(solution)/shard_map/all_gather | solution.py:497
  202.9 85.7 %collective-permute-start.11 = (bf16[4,2,256,256]{3,2,1,0:T(8,128)(2,1)}, bf16[4,2,256,256]{3,2,1,0:T(8,128)(2,1)}, u32[]{:S(2)}, u32[]{:S(2)}) collective-permute-start(bf16[4,2,256,256]{3,2,1,0:T(8,128)(2,1)} %get-tuple-element.48), channel_id=1, source_target_pairs={{0,12},{4,8},{8,4},{12,0},{1,13},{5,9},{9,5},{13,1},{2,14},{6,10},... | collective-permute-start | bytes 3145736 | tf_op jit(solution)/shard_map/ppermute | solution.py:493
  252.5 102.2 %collective-permute-start.5 = (bf16[4,2,256,256]{3,2,1,0:T(8,128)(2,1)}, bf16[4,2,256,256]{3,2,1,0:T(8,128)(2,1)}, u32[]{:S(2)}, u32[]{:S(2)}) collective-permute-start(bf16[4,2,256,256]{3,2,1,0:T(8,128)(2,1)} %get-tuple-element.41), channel_id=1, source_target_pairs={{0,8},{4,12},{8,0},{12,4},{1,9},{5,13},{9,1},{13,5},{2,10},{6,14},... | collective-permute-start | bytes 3145736 | tf_op jit(solution)/shard_map/ppermute | solution.py:493
  288.6 53.2 %copy-start.4 = (bf16[4,2,256,256]{3,2,1,0:T(8,128)(2,1)S(1)}, bf16[4,2,256,256]{3,2,1,0:T(8,128)(2,1)}, u32[]{:S(2)}) copy-start(bf16[4,2,256,256]{3,2,1,0:T(8,128)(2,1)} %get-tuple-element.42) | copy-start | bytes 3145732
  297.7 107.1 %collective-permute-start.4 = (bf16[4,2,256,256]{3,2,1,0:T(8,128)(2,1)}, bf16[4,2,256,256]{3,2,1,0:T(8,128)(2,1)S(1)}, u32[]{:S(2)}, u32[]{:S(2)}) collective-permute-start(bf16[4,2,256,256]{3,2,1,0:T(8,128)(2,1)} %get-tuple-element.40), channel_id=1, source_target_pairs={{0,4},{4,0},{8,12},{12,8},{1,5},{5,1},{9,13},{13,9},{2,6},{6,2},{1... | collective-permute-start | bytes 3145736 | tf_op jit(solution)/shard_map/ppermute | solution.py:493
  341.9 63.0 %collective-permute-start.6 = (bf16[4,2,256,256]{3,2,1,0:T(8,128)(2,1)S(1)}, bf16[4,2,256,256]{3,2,1,0:T(8,128)(2,1)S(1)}, u32[]{:S(2)}, u32[]{:S(2)}) collective-permute-start(bf16[4,2,256,256]{3,2,1,0:T(8,128)(2,1)S(1)} %copy-done.4), channel_id=1, source_target_pairs={{0,12},{4,8},{8,4},{12,0},{1,13},{5,9},{9,5},{13,1},{2,14},{6,10},... | collective-permute-start | bytes 3145736 | tf_op jit(solution)/shard_map/ppermute | solution.py:493
  354.7 61.1 %collective-permute-start.12 = (bf16[1,2,256,256]{3,2,1,0:T(8,128)(2,1)}, bf16[1,2,256,256]{3,2,1,0:T(8,128)(2,1)}, u32[]{:S(2)}, u32[]{:S(2)}) collective-permute-start(bf16[1,2,256,256]{3,2,1,0:T(8,128)(2,1)} %get-tuple-element.57), channel_id=1, source_target_pairs={{0,4},{4,0},{8,12},{12,8},{1,5},{5,1},{9,13},{13,9},{2,6},{6,2},{1... | collective-permute-start | bytes 786440 | tf_op jit(solution)/shard_map/ppermute | solution.py:493
  354.7 69.5 %collective-permute-start.16 = (bf16[1,2,256,256]{3,2,1,0:T(8,128)(2,1)}, bf16[1,2,256,256]{3,2,1,0:T(8,128)(2,1)}, u32[]{:S(2)}, u32[]{:S(2)}) collective-permute-start(bf16[1,2,256,256]{3,2,1,0:T(8,128)(2,1)} %get-tuple-element.63), channel_id=1, source_target_pairs={{0,8},{4,12},{8,0},{12,4},{1,9},{5,13},{9,1},{13,5},{2,10},{6,14},... | collective-permute-start | bytes 786440 | tf_op jit(solution)/shard_map/ppermute | solution.py:493
  358.0 66.1 %collective-permute-start.17 = (bf16[1,2,256,256]{3,2,1,0:T(8,128)(2,1)}, bf16[1,2,256,256]{3,2,1,0:T(8,128)(2,1)}, u32[]{:S(2)}, u32[]{:S(2)}) collective-permute-start(bf16[1,2,256,256]{3,2,1,0:T(8,128)(2,1)} %get-tuple-element.64), channel_id=1, source_target_pairs={{0,12},{4,8},{8,4},{12,0},{1,13},{5,9},{9,5},{13,1},{2,14},{6,10},... | collective-permute-start | bytes 786440 | tf_op jit(solution)/shard_map/ppermute | solution.py:493
  415.8 27.5 %collective-permute-start.13 = (bf16[1,2,256,256]{3,2,1,0:T(8,128)(2,1)}, bf16[1,2,256,256]{3,2,1,0:T(8,128)(2,1)S(1)}, u32[]{:S(2)}, u32[]{:S(2)}) collective-permute-start(bf16[1,2,256,256]{3,2,1,0:T(8,128)(2,1)} %get-tuple-element.58), channel_id=1, source_target_pairs={{0,4},{4,0},{8,12},{12,8},{1,5},{5,1},{9,13},{13,9},{2,6},{6,2},{1... | collective-permute-start | bytes 786440 | tf_op jit(solution)/shard_map/ppermute | solution.py:493
  421.4 21.9 %collective-permute-start.14 = (bf16[1,2,256,256]{3,2,1,0:T(8,128)(2,1)}, bf16[1,2,256,256]{3,2,1,0:T(8,128)(2,1)S(1)}, u32[]{:S(2)}, u32[]{:S(2)}) collective-permute-start(bf16[1,2,256,256]{3,2,1,0:T(8,128)(2,1)} %get-tuple-element.59), channel_id=1, source_target_pairs={{0,8},{4,12},{8,0},{12,4},{1,9},{5,13},{9,1},{13,5},{2,10},{6,14},... | collective-permute-start | bytes 786440 | tf_op jit(solution)/shard_map/ppermute | solution.py:493
  422.7 20.6 %collective-permute-start.15 = (bf16[1,2,256,256]{3,2,1,0:T(8,128)(2,1)}, bf16[1,2,256,256]{3,2,1,0:T(8,128)(2,1)S(1)}, u32[]{:S(2)}, u32[]{:S(2)}) collective-permute-start(bf16[1,2,256,256]{3,2,1,0:T(8,128)(2,1)} %get-tuple-element.60), channel_id=1, source_target_pairs={{0,12},{4,8},{8,4},{12,0},{1,13},{5,9},{9,5},{13,1},{2,14},{6,10},... | collective-permute-start | bytes 786440 | tf_op jit(solution)/shard_map/ppermute | solution.py:493
  424.1 19.2 %copy-start = (bf16[2,256,256]{2,1,0:T(8,128)(2,1)S(1)}, bf16[2,256,256]{2,1,0:T(8,128)(2,1)}, u32[]{:S(2)}) copy-start(bf16[2,256,256]{2,1,0:T(8,128)(2,1)} %get-tuple-element.50.refs_0_) | copy-start | bytes 786436
  (4 other events, 4.4 us)
Sparse Core Ops, SparseCore 0:
  11.6 74.8 all-gather.4
  131.5 112.3 all-gather.8
  245.8 72.1 all-gather.6
  319.7 72.1 all-gather.10
